TPU v7x, 256 devices: a whole 4x4x8 slice. The times are simulated.
256 devices in a mesh: chi: 64 (over x, z, core), site: 4 (over y).
Axes of the slice: x: 4, y: 4, z: 8, core: 2. Of those that a mesh axis runs over, the one named last changes fastest.
Arguments:
- upper: bfloat16 [4, 256, 256, 2401], P('site', 'chi'), may hold values from -6 to 6
- corner_low: bfloat16 [4, 256, 256], P('site'), may hold values from -0.375 to 0.375
- edge_bottom: bfloat16 [4, 256, 256, 49], P('site', None, 'chi'), may hold values from -6 to 6
- corner_right: bfloat16 [4, 256, 256], P('site'), may hold values from -0.375 to 0.375
- edge_right: bfloat16 [4, 256, 256, 49], P('site', 'chi'), may hold values from -6 to 6
- right_side: float32 [4, 2, 2401], P('site'), may hold values from -6 to 6
Outputs:
- solution_field: float32 [4, 2, 2401], P('site')
- residual: float32 [4, 2, 2401], P('site')
All inputs are finite; a program needn't handle non-finite values.
Results may differ from a plain program's by a relative error of at most 0.033.
Values may be sent and summed in bfloat16 or wider, within the bound.
No kernel may reach another device: no remote copies, remote signals or barrier semaphores. Data moves between devices by JAX's collectives and lax.ppermute only.
A program may use at most 128 MiB of HBM per device.

v0:
```python
import math

import jax
import jax.numpy as jnp
from jax import lax
from jax.sharding import PartitionSpec as P

CHI = 256
D = 7
PHYS = 2
ITERS = 2
DD = 49


shift_value = 0.5


def body(upper, corner_low, edge_bottom, corner_right, edge_right, right_side):
    local_rows = upper.shape[1]
    upper_five = upper[0].reshape(local_rows, CHI, DD, DD)
    part_mixed = jnp.dot(
        corner_low[0], edge_bottom[0].reshape(CHI, -1), preferred_element_type=jnp.float32
    )
    part_mixed = part_mixed.astype(jnp.bfloat16).reshape(CHI, -1, DD)
    rows_lower = lax.all_to_all(part_mixed, "chi", split_axis=0, concat_axis=1, tiled=True)
    quad_lower = rows_lower.reshape(local_rows, CHI, D, D)
    part_columns = jnp.einsum(
        "gf,efr->ger", corner_right[0], edge_right[0], preferred_element_type=jnp.float32
    )
    part_columns = part_columns.astype(jnp.bfloat16)
    scale_low = 1.0 / math.sqrt(CHI)
    segment = lax.all_gather(part_columns, "chi", axis=1, tiled=True)
    width_here = segment.shape[1]
    quad_right = segment.reshape(CHI, width_here, D, D)
    value = (
        jnp.einsum("igab,gecd->ieacbd", quad_lower, quad_right, preferred_element_type=jnp.float32)
        * scale_low
    )
    lower = value.reshape(local_rows, width_here, DD, DD).astype(jnp.bfloat16)
    scale_metric = 1.0 / (CHI * DD)

    def norm_two(values):
        return lax.psum(jnp.sum(values * values), "site")

    residual = right_side[0].reshape(PHYS, DD, DD)
    solution = jnp.zeros_like(residual)
    direction = residual
    norm_now = norm_two(residual)
    for step in range(ITERS):
        forward_quant = direction.astype(jnp.bfloat16)
        forward_sectioned = jnp.einsum(
            "ieku,pkc->ieupc", upper_five, forward_quant, preferred_element_type=jnp.float32
        ).astype(jnp.bfloat16)
        partial_image = (
            jnp.einsum(
                "ieupc,iecd->pud", forward_sectioned, lower, preferred_element_type=jnp.float32
            )
            * scale_metric
        )
        metric_image = lax.psum(partial_image, "chi")
        quant = metric_image.astype(jnp.bfloat16)
        sectioned = jnp.einsum(
            "ieku,pud->iekpd", upper_five, quant, preferred_element_type=jnp.float32
        ).astype(jnp.bfloat16)
        partial_back = (
            jnp.einsum("iekpd,iecd->pkc", sectioned, lower, preferred_element_type=jnp.float32)
            * scale_metric
        )
        image = lax.psum(partial_back, "chi") + shift_value * direction
        alpha = norm_now / lax.psum(jnp.sum(direction * image), "site")
        solution = solution + alpha * direction
        residual = residual - alpha * image
        norm_next = norm_two(residual)
        direction = residual + norm_next / norm_now * direction
        norm_now = norm_next
    return (solution.reshape(1, PHYS, DD * DD), residual.reshape(1, PHYS, DD * DD))


def solution(mesh):
    placed = (
        P("site", "chi", None, None),
        P("site", None, None),
        P("site", None, "chi", None),
        P("site", None, None),
        P("site", "chi", None, None),
        P("site", None, None),
    )
    return jax.shard_map(
        body,
        mesh=mesh,
        in_specs=placed,
        out_specs=(P("site", None, None), P("site", None, None)),
        check_vma=False,
    )
```

profile of v0, /device:TPU:1, one launch (start us, length us, event | category | flops | bytes accessed | tf_op | source)
XLA Modules:
  0.0 1195.1 jit_solution(12800500595664805708)
XLA Ops:
  7.2 0.8 copy-done
  8.1 1.8 convolution_convert_fusion.1
  9.9 0.9 copy.29
  10.8 1.1 convolution_convert_fusion.2
  12.2 1.0 reshape.47
  13.2 13.0 %all-to-all-start = ((bf16[64,2,392]{2,1,0:T(2,128)(2,1)}), bf16[64,2,392]{2,1,0:T(2,128)(2,1)S(1)}, u32[]{:S(2)}, u32[]{:S(2)}) async-start(bf16[64,2,392]{2,1,0:T(2,128)(2,1)} %reshape.47), calls=%async_computation | async-start | bytes 262144 | tf_op jit(solution)/shard_map/all_to_all | solution.py:25
  26.1 1.4 multiply_reduce_fusion.3
  27.7 8.5 convolution_convert_fusion
  37.1 1.2 reshape.25
  38.3 58.8 %all-gather.2.cloned.1.call-done = bf16[256,256,49]{0,2,1:T(8,128)(2,1)} async-done(((bf16[256,4,49]{0,2,1:T(8,128)(2,1)}), bf16[256,256,49]{0,2,1:T(8,128)(2,1)}) %all-gather.2.cloned.1.call-update) | async-done | bytes 6422544 | tf_op jit(solution)/shard_map/all_gather | solution.py:32
  97.1 12.2 %copy.28 = bf16[256,256,49]{1,0,2:T(8,128)(2,1)} copy(bf16[256,256,49]{0,2,1:T(8,128)(2,1)} %all-gather.2.cloned.1.call-done) | data formatting | bytes 12845056 | tf_op jit(solution)/shard_map/all_gather | solution.py:32
  109.3 4.9 fusion.8
  114.2 2.0 copy.34
  116.2 2.2 copy-done.2
  118.4 9.5 fusion.80
  127.9 242.9 %psum.57 = bf16[2,49,49]{1,2,0:T(8,128)(2,1)S(1)} all-reduce(f32[2,49,49]{1,2,0:T(8,128)S(1)} %fusion.80), channel_id=1, replica_groups=mesh['chi'=64,'site'=4] {'chi'}, use_global_device_ids=true, to_apply=%region_2.0 | all-reduce | flops 4802 | bytes 28812 | tf_op jit(solution)/shard_map/psum | solution.py:60
  370.8 5.7 convert_bitcast_fusion.2
  376.5 8.4 fusion.70
  385.0 246.1 %psum.58 = f32[2,49,49]{1,2,0:T(8,128)S(1)} all-reduce(f32[2,49,49]{1,2,0:T(8,128)S(1)} %fusion.70), channel_id=1, replica_groups=mesh['chi'=64,'site'=4] {'chi'}, use_global_device_ids=true, to_apply=%region_3.0 | all-reduce | flops 4802 | bytes 38416 | tf_op jit(solution)/shard_map/psum | solution.py:69
  631.7 9.1 all-reduce
  642.1 0.6 multiply_reduce_fusion.1
  642.7 6.8 psum.60
  650.9 5.7 convert_bitcast_fusion.1
  656.6 8.4 fusion.60
  665.0 250.2 %psum.61 = bf16[2,49,49]{1,2,0:T(8,128)(2,1)S(1)} all-reduce(f32[2,49,49]{1,2,0:T(8,128)S(1)} %fusion.60), channel_id=1, replica_groups=mesh['chi'=64,'site'=4] {'chi'}, use_global_device_ids=true, to_apply=%region_8.0 | all-reduce | flops 4802 | bytes 28812 | tf_op jit(solution)/shard_map/psum | solution.py:60
  915.2 5.7 convert_bitcast_fusion
  920.9 9.1 fusion.50
  930.0 246.2 %psum.62 = f32[2,49,49]{1,2,0:T(8,128)S(1)} all-reduce(f32[2,49,49]{1,2,0:T(8,128)} %fusion.50), channel_id=1, replica_groups=mesh['chi'=64,'site'=4] {'chi'}, use_global_device_ids=true, to_apply=%region_9.0 | all-reduce | flops 4802 | bytes 38416 | tf_op jit(solution)/shard_map/psum | solution.py:69
  1176.2 0.6 multiply_reduce_fusion
  1176.8 8.3 psum.63
  1186.7 0.7 reshape.27
  1187.5 0.7 reshape.26
  (22 shorter events, 2.1 us)
Async XLA Ops:
  7.2 0.9 copy-start
  7.2 89.9 %all-gather.2.cloned.1.call-start = ((), (), s32[]{:S(2)}) async-start(), calls=%async_computation.1 | async-start | bytes 7454720 | tf_op jit(solution)/shard_map/all_gather | solution.py:32
  13.2 23.4 %all-to-all-start = ((bf16[64,2,392]{2,1,0:T(2,128)(2,1)}), bf16[64,2,392]{2,1,0:T(2,128)(2,1)S(1)}, u32[]{:S(2)}, u32[]{:S(2)}) async-start(bf16[64,2,392]{2,1,0:T(2,128)(2,1)} %reshape.47), calls=%async_computation | async-start | bytes 262144 | tf_op jit(solution)/shard_map/all_to_all | solution.py:25
  27.7 8.5 copy-start.3
  116.2 2.2 copy-start.2
  920.9 267.4 %copy-start.1 = (bf16[1,256,256]{2,1,0:T(8,128)(2,1)S(1)}, bf16[1,256,256]{2,1,0:T(8,128)(2,1)}, u32[]{:S(2)}) copy-start(bf16[1,256,256]{2,1,0:T(8,128)(2,1)} %param.9) | copy-start | bytes 393220
Sparse Core Ops, SparseCore 0:
  10.8 86.2 all-gather.1
where the time goes:
time: 1200 us
  blocking collectives  1010 us (84%)
  matrix products  68.9 us (6%)
  waiting for transfers between devices  58.8 us (5%)
  local copies, waits for them, and re-layouts  23.2 us (2%)
  between operations  18.2 us (2%)
  starting transfers between devices  13 us (1%)
    psum x2, blocking collectives, body(): metric_image = lax.psum(partial_image, 'chi')  493 us
    psum x2, blocking collectives, body(): image = lax.psum(partial_back, 'chi') + shift_value * direction  492 us
    all_gather x1, waiting for transfers between devices, body(): segment = lax.all_gather(part_columns, 'chi', axis=1, tiled=True)  58.8 us
  transfers between devices with their start and end apart: 2, of which 2 were waited for; matrix products, arithmetic and copies ran while one was open for 1% of the time, Pallas kernels for 0%

commit v1 on v0

v1 whole, which is shorter than its diff:
```python
import math

import jax
import jax.numpy as jnp
from jax import lax
from jax.sharding import Mesh, PartitionSpec as P

CHI = 256
D = 7
PHYS = 2
ITERS = 2
DD = 49
BF = jnp.bfloat16
F32 = jnp.float32

shift_value = 0.5
scale_metric = 1.0 / (CHI * DD)


def spread(value, axes, count):
    return lax.all_to_all(jnp.broadcast_to(value[None], (count,) + value.shape), axes, 0, 0, tiled=True)


def swap(value):
    return lax.ppermute(value, "core", [(0, 1), (1, 0)])


def sum_chi(partial):
    core = lax.axis_index("core")
    flat = partial.reshape(PHYS, DD * DD)
    keep = jnp.where(core == 0, flat[0], flat[1])
    send = jnp.where(core == 0, flat[1], flat[0])
    keep = (keep + swap(send)).astype(BF)
    keep = jnp.pad(keep, (0, 19 * 128 - DD * DD)).reshape(19, 128)
    half = jnp.sum(spread(keep, ("x", "z"), 32).astype(F32), axis=0)
    other = swap(half)
    both = jnp.where(core == 0, jnp.stack([half, other]), jnp.stack([other, half]))
    return both.reshape(PHYS, 19 * 128)[:, : DD * DD].reshape(PHYS, DD, DD)


def sum_site(value):
    rows = jnp.broadcast_to(value, (8, 128))
    for step in (1, 2):
        rows = rows + lax.ppermute(rows, "site", [(i, i ^ step) for i in range(4)])
    return rows[0, 0]


def body(upper, corner_low, edge_bottom, corner_right, edge_right, right_side):
    local_rows = upper.shape[1]
    upper_five = upper[0].reshape(local_rows, CHI, DD, DD)
    part_mixed = jnp.dot(
        corner_low[0], edge_bottom[0].reshape(CHI, -1), preferred_element_type=F32
    )
    part_mixed = part_mixed.astype(BF).reshape(CHI, -1, DD)
    rows_lower = lax.all_to_all(part_mixed, ("x", "z", "core"), split_axis=0, concat_axis=1, tiled=True)
    quad_lower = rows_lower.reshape(local_rows, CHI, D, D)
    part_columns = jnp.einsum("gf,efr->ger", corner_right[0], edge_right[0], preferred_element_type=F32)
    part_columns = part_columns.astype(BF)
    stage = spread(part_columns.reshape(CHI * 4 * DD // 128, 128), "x", 4)
    stage = lax.all_gather(stage, "z")
    stage = lax.all_gather(stage, "core")
    segment = stage.reshape(2, 8, 4, CHI, 4, DD).transpose(3, 2, 1, 0, 4, 5)
    quad_right = segment.reshape(CHI, CHI, D, D)
    value = jnp.einsum("igab,gecd->ieacbd", quad_lower, quad_right, preferred_element_type=F32)
    value = value * (1.0 / math.sqrt(CHI))
    lower = value.reshape(local_rows, CHI, DD, DD).astype(BF)

    residual = right_side[0].reshape(PHYS, DD, DD)
    solution = jnp.zeros_like(residual)
    direction = residual
    norm_now = sum_site(jnp.sum(residual * residual))
    for step in range(ITERS):
        sectioned = jnp.einsum("ieku,pkc->ieupc", upper_five, direction.astype(BF), preferred_element_type=F32)
        partial = jnp.einsum("ieupc,iecd->pud", sectioned.astype(BF), lower, preferred_element_type=F32)
        quant = sum_chi(partial * scale_metric).astype(BF)
        sectioned = jnp.einsum("ieku,pud->iekpd", upper_five, quant, preferred_element_type=F32)
        partial = jnp.einsum("iekpd,iecd->pkc", sectioned.astype(BF), lower, preferred_element_type=F32)
        image = sum_chi(partial * scale_metric) + shift_value * direction
        alpha = norm_now / sum_site(jnp.sum(direction * image))
        solution = solution + alpha * direction
        residual = residual - alpha * image
        norm_next = sum_site(jnp.sum(residual * residual))
        direction = residual + norm_next / norm_now * direction
        norm_now = norm_next
    return (solution.reshape(1, PHYS, DD * DD), residual.reshape(1, PHYS, DD * DD))


def solution(mesh):
    split = Mesh(mesh.devices.reshape(4, 8, 2, 4), ("x", "z", "core", "site"))
    chi = ("x", "z", "core")
    placed = (
        P("site", chi, None, None),
        P("site", None, None),
        P("site", None, chi, None),
        P("site", None, None),
        P("site", chi, None, None),
        P("site", None, None),
    )
    return jax.shard_map(
        body,
        mesh=split,
        in_specs=placed,
        out_specs=(P("site", None, None), P("site", None, None)),
        check_vma=False,
    )
```

time: 1200 us -> 378 us (0.32)
  blocking collectives: 1010 us -> 69 us
  local copies, waits for them, and re-layouts: 23.2 us -> 102 us
  starting transfers between devices: 13 us -> 35.6 us
    psum x7 -> x0, blocking collectives: 1010 us -> none  [the longest x2 493 us: body(): metric_image = lax.psum(partial_image, 'chi')]
    all_to_all x0 -> x5, blocking collectives: none -> 69 us  [spread(): lax.all_to_all(jnp.broadcast_to(value[None], (count,) + value.shape), axe...]
    reshape x4, local copies, waits for them, and re-layouts: 1.71 us -> 62.6 us  [the longest x1 51.3 us: body(): segment = stage.reshape(2, 8, 4, CHI, 4, DD).transpose(3, 2, 1, 0, 4, 5)]
    ppermute x0 -> x16, starting transfers between devices: none -> 27.2 us  [the longest x8 18.7 us: swap(): return lax.ppermute(value, 'core', [(0, 1), (1, 0)])]
    transpose x0 -> x1, local copies, waits for them, and re-layouts: none -> 26.4 us  [body(): segment = stage.reshape(2, 8, 4, CHI, 4, DD).transpose(3, 2, 1, 0, 4, 5)]
    ppermute x0 -> x16, waiting for transfers between devices: none -> 18.2 us  [the longest x8 12.3 us: sum_site(): rows = rows + lax.ppermute(rows, 'site', [(i, i ^ step) for i in range(4)])]
    all_gather x1 -> x0, local copies, waits for them, and re-layouts: 12.2 us -> none  [body(): segment = lax.all_gather(part_columns, 'chi', axis=1, tiled=True)]
    all_gather x1 -> x2, waiting for transfers between devices: 58.8 us -> 50.5 us  [the longest x1 48.9 us: body(): stage = lax.all_gather(stage, 'z')]
  transfers between devices with their start and end apart: 2 -> 19, of which waited for: 2 -> 16; matrix products, arithmetic and copies ran while one was open for 1% -> 5% of each run, Pallas kernels for 0% -> 0%
where the time goes in v1:
time: 378 us; the launch traced here: 373 us
  local copies, waits for them, and re-layouts  102 us (27%)
  matrix products  70.7 us (19%)
  blocking collectives  69 us (18%)
  waiting for transfers between devices  68.7 us (18%)
  starting transfers between devices  35.6 us (9%)
  between operations  18.8 us (5%)
  other arithmetic  8.09 us (2%)
    all_to_all x5, blocking collectives, spread(): lax.all_to_all(jnp.broadcast_to(value[None], (count,) + value.shape), axe...  69 us
    reshape x1, local copies, waits for them, and re-layouts, body(): segment = stage.reshape(2, 8, 4, CHI, 4, DD).transpose(3, 2, 1, 0, 4, 5)  51.3 us
    all_gather x1, waiting for transfers between devices, body(): stage = lax.all_gather(stage, 'z')  48.9 us
    transpose x1, local copies, waits for them, and re-layouts, body(): segment = stage.reshape(2, 8, 4, CHI, 4, DD).transpose(3, 2, 1, 0, 4, 5)  26.4 us
    dot_general x2, matrix products, body(): jnp.einsum('ieupc,iecd->pud', sectioned.astype(BF), lower, preferred_elem...  19.7 us
    ppermute x8, starting transfers between devices, swap(): return lax.ppermute(value, 'core', [(0, 1), (1, 0)])  18.7 us
    dot_general x2, matrix products, body(): jnp.einsum('iekpd,iecd->pkc', sectioned.astype(BF), lower, preferred_elem...  16.9 us
    dot_general x2, matrix products, body(): jnp.einsum('ieku,pkc->ieupc', upper_five, direction.astype(BF), preferred...  15.9 us
  transfers between devices with their start and end apart: 19, of which 16 were waited for; matrix products, arithmetic and copies ran while one was open for 5% of the time, Pallas kernels for 0%

profile of v1, /device:TPU:1, one launch (start us, length us, event | category | flops | bytes accessed | tf_op | source)
XLA Modules:
  0.0 373.3 jit_solution(12260544228493042622)
XLA Ops:
  9.9 11.1 %all_to_all.40 = bf16[4,392,128]{2,1,0:T(8,128)(2,1)} all-to-all(bf16[4,392,128]{2,1,0:T(8,128)(2,1)S(1)} %broadcast_in_dim.49), channel_id=1, replica_groups=mesh['x'=4,'z'=8,'core'=2,'site'=4] {'x'}, dimensions={0} | all-to-all | bytes 802816 | tf_op jit(solution)/shard_map/all_to_all | solution.py:21
  21.0 48.9 %all-gather.5.cloned.1.call-done = bf16[32,392,128]{2,1,0:T(8,128)(2,1)} async-done(((bf16[4,392,128]{2,1,0:T(8,128)(2,1)}), bf16[32,392,128]{2,1,0:T(8,128)(2,1)}) %all-gather.5.cloned.1.call-update) | async-done | bytes 3211280 | tf_op jit(solution)/shard_map/all_gather | solution.py:60
  71.5 8.3 %all-to-all-start.1 = ((bf16[64,2,392]{2,1,0:T(2,128)(2,1)}), bf16[64,2,392]{2,1,0:T(2,128)(2,1)S(1)}, u32[]{:S(2)}, u32[]{:S(2)}) async-start(bf16[64,2,392]{2,1,0:T(2,128)(2,1)} %reshape.149), calls=%async_computation.1 | async-start | bytes 262144 | tf_op jit(solution)/shard_map/all_to_all | solution.py:55
  80.0 10.1 %convolution_convert_fusion = bf16[4,256,49,2,49]{1,4,3,2,0:T(8,128)(2,1)} fusion(bf16[4,256,49,49,1]{1,0,3,2,4:T(4,128)(2,1)} %bitcast.206, bf16[2,49,49]{2,1,0:T(8,128)(2,1)S(1)} %convert_element_type.91), kind=kOutput, calls=%fused_computation.12 | convolution fusion | flops 486807552 | bytes 14761348 | tf_op jit(solution)/shard_map/ieku,pkc->ieupc/dot_general | solution.py:73
  91.8 1.6 all-gather.7.cloned.1.call-done
  93.4 51.3 %reshape.121 = bf16[2,8,4,256,4,49]{5,4,3,2,1,0:T(4,128)(2,1)} reshape(bf16[16,4,392,128]{3,2,1,0:T(8,128)(2,1)} %all-gather.7.cloned.1.call-done) | data formatting | bytes 12845056 | tf_op jit(solution)/shard_map/reshape | solution.py:62
  144.7 26.4 %copy.141 = bf16[256,4,8,2,4,49]{0,4,3,2,1,5:T(4,128)(2,1)} copy(bf16[256,4,8,2,4,49]{5,4,0,1,2,3:T(4,128)(2,1)} %bitcast.210) | data formatting | bytes 12845056 | tf_op jit(solution)/shard_map/transpose | solution.py:62
  171.1 11.1 %reshape.122 = bf16[256,256,7,7]{0,1,3,2:T(8,128)(2,1)} reshape(bf16[256,4,8,2,4,49]{0,4,3,2,1,5:T(4,128)(2,1)} %copy.141) | data formatting | bytes 12845056 | tf_op jit(solution)/shard_map/reshape | solution.py:63
  182.2 5.4 %fusion.10 = bf16[4,256,7,7,7,7]{1,4,2,0,5,3:T(8,128)(2,1)S(1)} fusion(bf16[256,256,7,7]{0,1,3,2:T(8,128)(2,1)} %reshape.122, bf16[4,256,7,7,1,1]{3,2,1,0,5,4:T(8,128)(2,1)S(1)} %bitcast.211), kind=kOutput, calls=%fused_computation.15 | convolution fusion | flops 1263732736 | bytes 11440128 | tf_op jit(solution)/shard_map/igab,gecd->ieacbd/dot_general | solution.py:64
  187.6 2.0 copy.148
  189.6 11.2 %fusion.84 = f32[2,49,49]{1,2,0:T(8,128)S(1)} fusion(bf16[4,256,49,2,49]{1,4,3,2,0:T(8,128)(2,1)} %convolution_convert_fusion, bf16[4,256,49,49]{1,0,3,2:T(4,128)(2,1)S(1)} %bitcast.212), kind=kOutput, calls=%fused_computation.45 | convolution fusion | flops 481895104 | bytes 14770952 | tf_op jit(solution)/shard_map/ieupc,iecd->pud/dot_general | solution.py:74
  202.4 18.5 %all_to_all.41 = bf16[32,19,128]{2,1,0:T(8,128)(2,1)S(1)} all-to-all(bf16[32,19,128]{2,1,0:T(8,128)(2,1)S(1)} %broadcast_in_dim.51), channel_id=1, replica_groups=mesh['x'=4,'z'=8,'core'=2,'site'=4] {'x','z'}, dimensions={0} | all-to-all | bytes 311296 | tf_op jit(solution)/shard_map/all_to_all | solution.py:21
  220.9 3.1 collective-permute-start.3
  225.1 5.8 %convert_bitcast_fusion.2 = bf16[4,256,49,2,49]{1,4,2,0,3:T(8,128)(2,1)S(1)} fusion(bf16[4,256,49,49]{1,0,3,2:T(4,128)(2,1)} %bitcast.207, bf16[2,49,49]{2,1,0:T(8,128)(2,1)S(1)} %convert_element_type.95), kind=kOutput, calls=%fused_computation.10 | convolution fusion | flops 486807552 | bytes 14761348 | tf_op jit(solution)/shard_map/ieku,pud->iekpd/dot_general | solution.py:76
  230.9 8.4 %fusion.74 = f32[2,49,49]{1,2,0:T(8,128)S(1)} fusion(bf16[4,256,49,2,49]{1,4,2,0,3:T(8,128)(2,1)S(1)} %convert_bitcast_fusion.2, bf16[4,256,49,49]{1,0,3,2:T(4,128)(2,1)} %bitcast.213), kind=kOutput, calls=%fused_computation.43 | convolution fusion | flops 481895104 | bytes 14770952 | tf_op jit(solution)/shard_map/iekpd,iecd->pkc/dot_general | solution.py:77
  241.0 12.9 %all_to_all.42 = bf16[32,19,128]{2,1,0:T(8,128)(2,1)S(1)} all-to-all(bf16[32,19,128]{2,1,0:T(8,128)(2,1)S(1)} %broadcast_in_dim.53), channel_id=1, replica_groups=mesh['x'=4,'z'=8,'core'=2,'site'=4] {'x','z'}, dimensions={0} | all-to-all | bytes 311296 | tf_op jit(solution)/shard_map/all_to_all | solution.py:21
  254.0 3.0 collective-permute-start.5
  262.3 2.8 collective-permute-start.7
  268.0 1.9 collective-permute-done.1
  274.0 2.2 collective-permute-done.8
  277.8 3.1 collective-permute-done.9
  283.6 5.8 %convert_bitcast_fusion.1 = bf16[4,256,49,2,49]{1,4,2,0,3:T(8,128)(2,1)S(1)} fusion(bf16[4,256,49,49]{1,0,3,2:T(4,128)(2,1)} %bitcast.208, bf16[2,49,49]{2,1,0:T(8,128)(2,1)S(1)} %convert_element_type.101), kind=kOutput, calls=%fused_computation.9 | convolution fusion | flops 486807552 | bytes 14761348 | tf_op jit(solution)/shard_map/ieku,pkc->ieupc/dot_general | solution.py:73
  289.3 8.4 %fusion.64 = f32[2,49,49]{1,2,0:T(8,128)S(1)} fusion(bf16[4,256,49,2,49]{1,4,2,0,3:T(8,128)(2,1)S(1)} %convert_bitcast_fusion.1, bf16[4,256,49,49]{1,0,3,2:T(4,128)(2,1)} %bitcast.214), kind=kOutput, calls=%fused_computation.41 | convolution fusion | flops 481895104 | bytes 14770952 | tf_op jit(solution)/shard_map/ieupc,iecd->pud/dot_general | solution.py:74
  298.0 5.3 %collective-permute-start.10 = (f32[2401]{0:T(1024)S(1)}, f32[2401]{0:T(1024)S(1)}, u32[]{:S(2)}, u32[]{:S(2)}) collective-permute-start(f32[2401]{0:T(1024)S(1)} %select_n.99), channel_id=1, source_target_pairs={{0,4},{4,0},{1,5},{5,1},{2,6},{6,2},{3,7},{7,3},{8,12},{12,8},{9,1... | collective-permute-start | bytes 28820 | tf_op jit(solution)/shard_map/ppermute | solution.py:25
  304.2 13.3 %all_to_all.43 = bf16[32,19,128]{2,1,0:T(8,128)(2,1)S(1)} all-to-all(bf16[32,19,128]{2,1,0:T(8,128)(2,1)S(1)} %broadcast_in_dim.57), channel_id=1, replica_groups=mesh['x'=4,'z'=8,'core'=2,'site'=4] {'x','z'}, dimensions={0} | all-to-all | bytes 311296 | tf_op jit(solution)/shard_map/all_to_all | solution.py:21
  317.6 3.0 collective-permute-start.11
  321.6 5.8 %convert_bitcast_fusion = bf16[4,256,49,2,49]{1,4,2,0,3:T(8,128)(2,1)S(1)} fusion(bf16[4,256,49,49]{1,0,3,2:T(4,128)(2,1)} %bitcast.209, bf16[2,49,49]{2,1,0:T(8,128)(2,1)S(1)} %convert_element_type.106), kind=kOutput, calls=%fused_computation.8 | convolution fusion | flops 486807552 | bytes 14761348 | tf_op jit(solution)/shard_map/ieku,pud->iekpd/dot_general | solution.py:76
  327.4 8.5 %fusion.54 = f32[2,49,49]{1,2,0:T(8,128)S(1)} fusion(bf16[4,256,49,2,49]{1,4,2,0,3:T(8,128)(2,1)S(1)} %convert_bitcast_fusion, bf16[4,256,49,49]{1,0,3,2:T(4,128)(2,1)} %bitcast.215), kind=kOutput, calls=%fused_computation.39 | convolution fusion | flops 481895104 | bytes 14770952 | tf_op jit(solution)/shard_map/iekpd,iecd->pkc/dot_general | solution.py:77
  337.5 13.2 %all_to_all.44 = bf16[32,19,128]{2,1,0:T(8,128)(2,1)S(1)} all-to-all(bf16[32,19,128]{2,1,0:T(8,128)(2,1)S(1)} %broadcast_in_dim.59), channel_id=1, replica_groups=mesh['x'=4,'z'=8,'core'=2,'site'=4] {'x','z'}, dimensions={0} | all-to-all | bytes 311296 | tf_op jit(solution)/shard_map/all_to_all | solution.py:21
  350.6 3.0 collective-permute-start.13
  356.3 2.1 collective-permute-done.14
  360.1 2.9 collective-permute-done.15
  (124 shorter events, 34.2 us)
Async XLA Ops:
  7.2 0.9 copy-start
  7.2 62.8 %copy-start.5 = (bf16[1,256,4,49]{1,2,3,0:T(4,128)(2,1)S(1)}, bf16[1,256,4,49]{1,2,3,0:T(4,128)(2,1)}, u32[]{:S(2)}) copy-start(bf16[1,256,4,49]{1,2,3,0:T(4,128)(2,1)} %param.8) | copy-start | bytes 301060
  7.2 62.8 %copy-start.4 = (bf16[1,256,256]{2,1,0:T(8,128)(2,1)S(1)}, bf16[1,256,256]{2,1,0:T(8,128)(2,1)}, u32[]{:S(2)}) copy-start(bf16[1,256,256]{2,1,0:T(8,128)(2,1)} %param.7) | copy-start | bytes 393220
  7.2 72.6 %copy-start.3 = (f32[1,2,2401]{2,1,0:T(2,128)S(1)}, f32[1,2,2401]{2,1,0:T(2,128)}, u32[]{:S(2)}) copy-start(f32[1,2,2401]{2,1,0:T(2,128)} %param.11) | copy-start | bytes 57628
  7.2 62.7 %all-gather.5.cloned.1.call-start = ((), (), s32[]{:S(2)}) async-start(), calls=%async_computation.6 | async-start | bytes 3612672 | tf_op jit(solution)/shard_map/all_gather | solution.py:60
  20.9 72.5 %all-gather.7.cloned.1.call-start = ((), (), s32[]{:S(2)}) async-start(), calls=%async_computation.7 | async-start | bytes 9633792 | tf_op jit(solution)/shard_map/all_gather | solution.py:61
  71.5 18.6 %all-to-all-start.1 = ((bf16[64,2,392]{2,1,0:T(2,128)(2,1)}), bf16[64,2,392]{2,1,0:T(2,128)(2,1)S(1)}, u32[]{:S(2)}, u32[]{:S(2)}) async-start(bf16[64,2,392]{2,1,0:T(2,128)(2,1)} %reshape.149), calls=%async_computation.1 | async-start | bytes 262144 | tf_op jit(solution)/shard_map/all_to_all | solution.py:55
  189.6 11.3 %copy-start.2 = (bf16[4,256,7,7,7,7]{1,0,5,4,3,2:T(4,128)(2,1)}, bf16[4,256,7,7,7,7]{1,0,5,4,3,2:T(4,128)(2,1)S(1)}, u32[]{:S(2)}) copy-start(bf16[4,256,7,7,7,7]{1,0,5,4,3,2:T(4,128)(2,1)S(1)} %copy.148) | copy-start | bytes 14751748
  201.1 1.3 collective-permute-start.2
  220.9 3.9 %collective-permute-start.3 = (bf16[19,128]{1,0:T(8,128)(2,1)S(1)}, bf16[19,128]{1,0:T(8,128)(2,1)S(1)}, u32[]{:S(2)}, u32[]{:S(2)}) collective-permute-start(bf16[19,128]{1,0:T(8,128)(2,1)S(1)} %convert_reduce_fusion.3), channel_id=1, source_target_pairs={{0,4},{4,0},{1,5},{5,1},{2,6},{6,2},{3,7},{7,3},{8,12},{12,8},{9,1... | collective-permute-start | bytes 14600 | tf_op jit(solution)/shard_map/ppermute | solution.py:25
  239.5 1.4 collective-permute-start.4
  254.0 3.8 %collective-permute-start.5 = (f32[19,128]{1,0:T(8,128)S(1)}, f32[19,128]{1,0:T(8,128)S(1)}, u32[]{:S(2)}, u32[]{:S(2)}) collective-permute-start(f32[19,128]{1,0:T(8,128)S(1)} %convert_reduce_fusion.2), channel_id=1, source_target_pairs={{0,4},{4,0},{1,5},{5,1},{2,6},{6,2},{3,7},{7,3},{8,12},{12,8},{9,1... | collective-permute-start | bytes 29192 | tf_op jit(solution)/shard_map/ppermute | solution.py:25
  259.1 2.5 collective-permute-start.6
  261.1 4.1 %collective-permute-start = (f32[8,128]{1,0:T(8,128)S(1)}, f32[8,128]{1,0:T(8,128)S(1)}, u32[]{:S(2)}, u32[]{:S(2)}) collective-permute-start(f32[8,128]{1,0:T(8,128)S(1)} %broadcast_in_dim.47), channel_id=1, source_target_pairs={{0,1},{1,0},{2,3},{3,2},{4,5},{5,4},{6,7},{7,6},{8,9},{9,8},{10,11... | collective-permute-start | bytes 12296 | tf_op jit(solution)/shard_map/ppermute | solution.py:44
  262.3 4.5 %collective-permute-start.7 = (f32[8,128]{1,0:T(8,128)S(1)}, f32[8,128]{1,0:T(8,128)S(1)}, u32[]{:S(2)}, u32[]{:S(2)}) collective-permute-start(f32[8,128]{1,0:T(8,128)S(1)} %broadcast_add_fusion.2), channel_id=1, source_target_pairs={{0,2},{1,3},{2,0},{3,1},{4,6},{5,7},{6,4},{7,5},{8,10},{9,11},{10,... | collective-permute-start | bytes 12296 | tf_op jit(solution)/shard_map/ppermute | solution.py:44
  265.8 4.0 %collective-permute-start.1 = (f32[8,128]{1,0:T(8,128)S(1)}, f32[8,128]{1,0:T(8,128)S(1)}, u32[]{:S(2)}, u32[]{:S(2)}) collective-permute-start(f32[8,128]{1,0:T(8,128)S(1)} %broadcast_add_fusion.3), channel_id=1, source_target_pairs={{0,2},{1,3},{2,0},{3,1},{4,6},{5,7},{6,4},{7,5},{8,10},{9,11},{10,... | collective-permute-start | bytes 12296 | tf_op jit(solution)/shard_map/ppermute | solution.py:44
  273.6 2.5 collective-permute-start.8
  276.8 4.0 %collective-permute-start.9 = (f32[8,128]{1,0:T(8,128)S(1)}, f32[8,128]{1,0:T(8,128)S(1)}, u32[]{:S(2)}, u32[]{:S(2)}) collective-permute-start(f32[8,128]{1,0:T(8,128)S(1)} %broadcast_add_fusion.1), channel_id=1, source_target_pairs={{0,2},{1,3},{2,0},{3,1},{4,6},{5,7},{6,4},{7,5},{8,10},{9,11},{10,... | collective-permute-start | bytes 12296 | tf_op jit(solution)/shard_map/ppermute | solution.py:44
  298.0 6.1 %collective-permute-start.10 = (f32[2401]{0:T(1024)S(1)}, f32[2401]{0:T(1024)S(1)}, u32[]{:S(2)}, u32[]{:S(2)}) collective-permute-start(f32[2401]{0:T(1024)S(1)} %select_n.99), channel_id=1, source_target_pairs={{0,4},{4,0},{1,5},{5,1},{2,6},{6,2},{3,7},{7,3},{8,12},{12,8},{9,1... | collective-permute-start | bytes 28820 | tf_op jit(solution)/shard_map/ppermute | solution.py:25
  317.6 3.8 %collective-permute-start.11 = (bf16[19,128]{1,0:T(8,128)(2,1)S(1)}, bf16[19,128]{1,0:T(8,128)(2,1)S(1)}, u32[]{:S(2)}, u32[]{:S(2)}) collective-permute-start(bf16[19,128]{1,0:T(8,128)(2,1)S(1)} %convert_reduce_fusion.1), channel_id=1, source_target_pairs={{0,4},{4,0},{1,5},{5,1},{2,6},{6,2},{3,7},{7,3},{8,12},{12,8},{9,1... | collective-permute-start | bytes 14600 | tf_op jit(solution)/shard_map/ppermute | solution.py:25
  327.4 38.8 %copy-start.1 = (bf16[1,256,256]{2,1,0:T(8,128)(2,1)S(1)}, bf16[1,256,256]{2,1,0:T(8,128)(2,1)}, u32[]{:S(2)}) copy-start(bf16[1,256,256]{2,1,0:T(8,128)(2,1)} %param.9) | copy-start | bytes 393220
  336.1 1.3 collective-permute-start.12
  350.6 3.8 %collective-permute-start.13 = (f32[19,128]{1,0:T(8,128)S(1)}, f32[19,128]{1,0:T(8,128)S(1)}, u32[]{:S(2)}, u32[]{:S(2)}) collective-permute-start(f32[19,128]{1,0:T(8,128)S(1)} %convert_reduce_fusion), channel_id=1, source_target_pairs={{0,4},{4,0},{1,5},{5,1},{2,6},{6,2},{3,7},{7,3},{8,12},{12,8},{9,1... | collective-permute-start | bytes 29192 | tf_op jit(solution)/shard_map/ppermute | solution.py:25
  355.8 2.5 collective-permute-start.14
  359.0 4.0 %collective-permute-start.15 = (f32[8,128]{1,0:T(8,128)S(1)}, f32[8,128]{1,0:T(8,128)S(1)}, u32[]{:S(2)}, u32[]{:S(2)}) collective-permute-start(f32[8,128]{1,0:T(8,128)S(1)} %broadcast_add_fusion), channel_id=1, source_target_pairs={{0,2},{1,3},{2,0},{3,1},{4,6},{5,7},{6,4},{7,5},{8,10},{9,11},{10,... | collective-permute-start | bytes 12296 | tf_op jit(solution)/shard_map/ppermute | solution.py:44
Sparse Core Ops, SparseCore 0:
  21.1 48.8 all-gather.4
  71.7 21.6 all-gather.6

commit v2 on v1

v2 whole, which is shorter than its diff:
```python
import functools
import math

import jax
import jax.numpy as jnp
import numpy as np
from jax import lax
from jax.experimental import pallas as pl
from jax.experimental.pallas import tpu as pltpu
from jax.sharding import Mesh, PartitionSpec as P

CHI = 256
D = 7
PHYS = 2
DD = 49
BF = jnp.bfloat16
F32 = jnp.float32

NX, NZ, NCORE, NSITE = 4, 8, 2, 4
CHIPS = NX * NZ
ROWS_I = 8
COLS_E = 128
GROUP = 8
PAIR = D * GROUP
SLAB = 400
WIDE = 2432
BLOCKS = WIDE // 128
CHUNK = 80
STRIPE = 256
VEC = PHYS * PAIR

shift_value = 0.5
scale_metric = 1.0 / (CHI * DD)


def tables():
    lane = np.arange(WIDE)
    valid = lane < DD * DD
    first = np.zeros((128, WIDE), np.float32)
    first[(lane // DD)[valid], lane[valid]] = 1
    second = np.zeros((128, WIDE), np.float32)
    second[(lane % DD)[valid], lane[valid]] = 1
    fold = np.zeros((VEC, D * VEC), np.float32)
    for r in range(D):
        for p in range(PHYS):
            for q in range(D):
                for s in range(GROUP):
                    fold[p * PAIR + r * GROUP + q, r * VEC + p * PAIR + q * GROUP + s] = 1
    return first, second, fold


def parity_table():
    table = np.zeros((NCORE, COLS_E, CHI), np.float32)
    for c in range(NCORE):
        for z in range(NZ):
            for x in range(NX):
                for q in range(4):
                    table[c, (z * NX + x) * 4 + q, ((x * NZ + z) * NCORE + c) * 4 + q] = 1
    return table


def unpack(parts):
    low = lax.broadcasted_iota(jnp.int32, (32, 128), 1) < 64
    rows = []
    for half in parts:
        rows.append(jnp.where(low, half, 0.0))
        rows.append(jnp.where(low, pltpu.roll(half, 64, 1), 0.0)[:24])
    return jnp.concatenate(rows, axis=0)


def pack(rows):
    out = []
    for p in range(PHYS):
        upper_rows = jnp.concatenate([rows[p * PAIR + 32 : p * PAIR + 56], jnp.zeros((8, 128), F32)], axis=0)
        out.append(rows[p * PAIR : p * PAIR + 32] + pltpu.roll(upper_rows, 64, 1))
    return out


def two_terms(value):
    high = value.astype(BF)
    return high, (value - high.astype(F32)).astype(BF)


def dot(a, b):
    return jnp.dot(a, b, preferred_element_type=F32)


def dot_lanes(a, b):
    return lax.dot_general(a, b, (((1,), (1,)), ((), ())), preferred_element_type=F32)


def metric_kernel(mixed_ref, cols_ref, own_ref, other_ref, out_ref, low_ref):
    step = pl.program_id(0)

    @pl.when(step == 0)
    def _():
        for rk in range(D):
            cols = [cols_ref[:, rk * D + rb].reshape(COLS_E, CHI) for rb in range(D)]
            low = dot_lanes(mixed_ref[...], jnp.concatenate(cols, axis=0)) * (1.0 / math.sqrt(CHI))
            for i in range(ROWS_I):
                strip = [low[i * PAIR : (i + 1) * PAIR, rb * COLS_E : (rb + 1) * COLS_E] for rb in range(D)]
                strip.append(jnp.zeros((SLAB - D * PAIR, COLS_E), F32))
                strip = jnp.concatenate(strip, axis=0).astype(BF)
                low_ref[rk, :, i * COLS_E : (i + 1) * COLS_E] = strip

    half = range(ROWS_I // 2)
    upper = jnp.concatenate([own_ref[i] for i in half] + [other_ref[i] for i in half], axis=1)
    inside = lax.broadcasted_iota(jnp.int32, (1, STRIPE), 1) + step * STRIPE < DD * DD
    for rk in range(D):
        out_ref[rk] = jnp.where(inside, dot_lanes(low_ref[rk], upper), 0.0).astype(BF)


def build_metric(mixed, cols, own, other):
    stripe = pl.BlockSpec((ROWS_I // 2, STRIPE, COLS_E), lambda n: (0, n, 0))
    return pl.pallas_call(
        metric_kernel,
        grid=(pl.cdiv(WIDE, STRIPE),),
        in_specs=[
            pl.BlockSpec((ROWS_I * PAIR, CHI), lambda n: (0, 0)),
            pl.BlockSpec((NZ, DD, 16, CHI), lambda n: (0, 0, 0, 0)),
            stripe,
            stripe,
        ],
        out_specs=pl.BlockSpec((D, SLAB, STRIPE), lambda n: (0, 0, n)),
        out_shape=pltpu.HBM((D, SLAB, WIDE), BF),
        scratch_shapes=[pltpu.VMEM((D, SLAB, ROWS_I * COLS_E), BF)],
        compiler_params=pltpu.CompilerParams(vmem_limit_bytes=30 * 1024 * 1024),
        cost_estimate=pl.CostEstimate(flops=15_000_000_000, bytes_accessed=22_000_000, transcendentals=0),
        name="build_metric",
    )(mixed, *(pltpu.with_memory_space_constraint(a, pltpu.HBM) for a in (cols, own, other)))


def forward_step(step, metric_ref, e_ref, acc_ref):
    for block in range(BLOCKS):
        lanes = slice(block * 128, (block + 1) * 128)
        tile = metric_ref[step, :, lanes].astype(F32)
        for p in range(PHYS):
            eight = e_ref[pl.ds(pl.multiple_of(p * PAIR + step * GROUP, GROUP), GROUP), lanes]
            factors = [jnp.broadcast_to(eight[q : q + 1], (GROUP, 128)) for q in range(D)]
            for rb in range(D):
                total = acc_ref[p * PAIR + rb * GROUP : p * PAIR + (rb + 1) * GROUP, lanes]
                for q in range(D):
                    row = (rb * D + q) * GROUP
                    total = total + tile[row : row + GROUP] * factors[q]
                acc_ref[p * PAIR + rb * GROUP : p * PAIR + (rb + 1) * GROUP, lanes] = total


def backward_step(step, metric_ref, f_ref, z_ref):
    for block in range(BLOCKS):
        lanes = slice(block * 128, (block + 1) * 128)
        tile = metric_ref[step, :, lanes].astype(F32)
        for p in range(PHYS):
            factors = [f_ref[p * PAIR + rb * GROUP : p * PAIR + (rb + 1) * GROUP, lanes] for rb in range(D)]
            for q in range(D):
                total = tile[q * GROUP : (q + 1) * GROUP] * factors[0]
                for rb in range(1, D):
                    row = (rb * D + q) * GROUP
                    total = total + tile[row : row + GROUP] * factors[rb]
                z_ref[step, p * PAIR + q * GROUP : p * PAIR + (q + 1) * GROUP, lanes] = total


def halves(core_ref, own_ref, other_ref):
    first = core_ref[0] == 0
    own, other = own_ref[...], other_ref[...]
    return [jnp.where(first, own, other), jnp.where(first, other, own)]


def lane_sums(parts):
    total = parts[0]
    for part in parts[1:]:
        total = total + part
    return jnp.sum(total, axis=0, keepdims=True)


def whole(row_ref):
    return jnp.sum(row_ref[...], axis=1, keepdims=True)


def apply_kernel(forward, prologue, n_in, n_out, core_ref, *refs):
    metric_ref, expand_ref, reduce_ref, fold_ref = refs[:4]
    ins, outs = refs[4 : 4 + n_in], refs[4 + n_in : 4 + n_in + n_out]
    keep_ref, send_ref, wide_ref, sum_ref, slab_ref, sems = refs[4 + n_in + n_out :]
    step = pl.program_id(0)

    def fetch(r, c):
        rows = pl.ds(c * CHUNK, CHUNK)
        return pltpu.make_async_copy(metric_ref.at[r, rows], slab_ref.at[r, rows], sems.at[r, c])

    @pl.when(step == 0)
    def _():
        for r in range(D):
            for c in range(SLAB // CHUNK):
                fetch(r, c).start()
        vec = prologue(core_ref, ins, outs)
        wide_ref[...] = dot(unpack(vec).astype(BF), expand_ref[...])
        if forward:
            sum_ref[...] = jnp.zeros_like(sum_ref)

    for c in range(SLAB // CHUNK):
        fetch(step, c).wait()
    (forward_step if forward else backward_step)(step, slab_ref, wide_ref, sum_ref)

    @pl.when(step == D - 1)
    def _():
        if forward:
            high, low = two_terms(sum_ref[...])
            rows = dot(high, reduce_ref[...]) + dot(low, reduce_ref[...])
        else:
            sums = [dot(sum_ref[r].astype(BF), reduce_ref[...]) for r in range(D)]
            high, low = two_terms(jnp.concatenate(sums, axis=0))
            rows = dot(fold_ref[...], high) + dot(fold_ref[...], low)
        parts = pack(rows * scale_metric)
        first = core_ref[0] == 0
        keep_ref[...] = jnp.where(first, parts[0], parts[1])
        send_ref[...] = jnp.where(first, parts[1], parts[0])


def full(shape):
    return pl.BlockSpec(shape, lambda *r: (0,) * len(shape))


VECTOR = jax.ShapeDtypeStruct((PHYS, 32, 128), F32)
HALF = jax.ShapeDtypeStruct((32, 128), F32)
LANES = jax.ShapeDtypeStruct((1, 128), F32)


def apply_metric(forward, prologue, core, metric, constants, ins, outs):
    wide = pltpu.VMEM((VEC, WIDE), F32)
    out_shape = list(outs) + [HALF, HALF]
    return pl.pallas_call(
        functools.partial(apply_kernel, forward, prologue, len(ins), len(outs)),
        grid=(D,),
        in_specs=[pl.BlockSpec(memory_space=pltpu.SMEM), pl.BlockSpec(memory_space=pl.ANY)]
        + [full(c.shape) for c in constants]
        + [full(i.shape) for i in ins],
        out_specs=[full(o.shape) for o in out_shape],
        out_shape=out_shape,
        scratch_shapes=[
            wide,
            wide if forward else pltpu.VMEM((D, VEC, WIDE), F32),
            pltpu.VMEM((D, SLAB, WIDE), BF),
            pltpu.SemaphoreType.DMA((D, SLAB // CHUNK)),
        ],
        compiler_params=pltpu.CompilerParams(vmem_limit_bytes=34 * 1024 * 1024),
        cost_estimate=pl.CostEstimate(flops=50_000_000, bytes_accessed=14_000_000, transcendentals=0),
        name="forward" if forward else "backward",
    )(core, pltpu.with_memory_space_constraint(metric, pltpu.HBM), *constants, *ins)


def first_vector(core_ref, ins, outs):
    return [ins[0][p] for p in range(PHYS)]


def first_image(core_ref, ins, outs):
    own_ref, other_ref, start_ref = ins
    image_ref, curve_ref = outs
    image = halves(core_ref, own_ref, other_ref)
    parts = []
    for p in range(PHYS):
        image_ref[p] = image[p]
        parts.append(image[p] * image[p] + shift_value * (start_ref[p] * start_ref[p]))
    curve_ref[...] = lane_sums(parts)
    return image


def next_residual(core_ref, ins, outs):
    own_ref, other_ref, start_ref, norm_ref, curve_ref = ins
    residual_ref, next_ref = outs
    back = halves(core_ref, own_ref, other_ref)
    alpha = whole(norm_ref) / whole(curve_ref)
    residual = [start_ref[p] - alpha * (back[p] + shift_value * start_ref[p]) for p in range(PHYS)]
    for p in range(PHYS):
        residual_ref[p] = residual[p]
    next_ref[...] = lane_sums([r * r for r in residual])
    return residual


def next_image(core_ref, ins, outs):
    own_ref, other_ref, start_ref, image_ref, residual_ref, norm_ref, next_ref = ins
    direction_ref, curve_ref = outs
    image = halves(core_ref, own_ref, other_ref)
    beta = whole(next_ref) / whole(norm_ref)
    image = [image[p] + beta * image_ref[p] for p in range(PHYS)]
    parts = []
    for p in range(PHYS):
        direction = residual_ref[p] + beta * start_ref[p]
        direction_ref[p] = direction
        parts.append(image[p] * image[p] + shift_value * (direction * direction))
    curve_ref[...] = lane_sums(parts)
    return image


def finish_kernel(core_ref, own_ref, other_ref, start_ref, residual_ref, direction_ref, norm_ref, curve_ref, next_ref,
                  last_ref, solution_ref, out_ref):
    back = halves(core_ref, own_ref, other_ref)
    alpha_0 = whole(norm_ref) / whole(curve_ref)
    alpha_1 = whole(next_ref) / whole(last_ref)
    for p in range(PHYS):
        direction = direction_ref[p]
        solution_ref[p] = alpha_0 * start_ref[p] + alpha_1 * direction
        out_ref[p] = residual_ref[p] - alpha_1 * (back[p] + shift_value * direction)


def finish(core, *ins):
    return pl.pallas_call(
        finish_kernel,
        in_specs=[pl.BlockSpec(memory_space=pltpu.SMEM)] + [full(i.shape) for i in ins],
        out_specs=[full(VECTOR.shape)] * 2,
        out_shape=[VECTOR, VECTOR],
        name="finish",
    )(core, *ins)


def spread(value, axes, count):
    return lax.all_to_all(jnp.broadcast_to(value[None], (count,) + value.shape), axes, 0, 0, tiled=True)


def swap(value):
    return lax.ppermute(value, "core", [(0, 1), (1, 0)])


def sum_chi(keep, send, lanes=None):
    keep = (keep + swap(send)).astype(BF)
    parts = spread(keep, ("x", "z"), CHIPS)
    if lanes is not None:
        for step in (1, 2):
            lanes = lanes + lax.ppermute(lanes, "site", [(i, i ^ step) for i in range(NSITE)])
        parts, lanes = lax.optimization_barrier((parts, lanes))
    half = jnp.sum(parts.astype(F32), axis=0)
    pair = (half, swap(half))
    return pair if lanes is None else (pair, lanes)


def to_packed(field):
    move = np.zeros((2, 32, DD), np.float32)
    for dk in range(D):
        for rk in range(D):
            move[rk // 4, rk % 4 * GROUP + dk, dk * D + rk] = 1
    grid = jnp.einsum("hrc,pkc->prhk", move, field.reshape(PHYS, DD, DD), precision=lax.Precision.HIGHEST)
    return jnp.pad(grid, ((0, 0), (0, 0), (0, 0), (0, 64 - DD))).reshape(PHYS, 32, 128)


def from_packed(packed):
    grid = packed.reshape(PHYS, 4, 8, 2, 64).transpose(0, 4, 3, 1, 2).reshape(PHYS, 64, 8, 8)
    return grid[:, :DD, :D, :D].transpose(0, 1, 3, 2).reshape(1, PHYS, DD * DD)


def body(upper, corner_low, edge_bottom, corner_right, edge_right, right_side):
    core = lax.axis_index("core")

    cols = jnp.einsum("efr,gf->reg", edge_right[0], corner_right[0], preferred_element_type=F32).astype(BF)
    cols = spread(cols.reshape(DD * 4 * CHI // 128, 128), "x", NX)
    cols = cols.reshape(NX, DD, 4, CHI).transpose(1, 0, 2, 3).reshape(DD, 4 * NX, CHI)
    cols_all = lax.all_gather(cols, "z")

    mixed = jnp.einsum("ih,hgq->giq", corner_low[0], edge_bottom[0], preferred_element_type=F32).astype(BF)
    mixed = mixed.reshape(4, 64, 4, DD).transpose(1, 0, 2, 3)
    mixed = lax.all_to_all(mixed, ("x", "z", "core"), 0, 0, tiled=True).reshape(CHI, 4, DD)
    rows = np.zeros((PAIR, DD), np.float32)
    rows[np.arange(DD) // D * GROUP + np.arange(DD) % D, np.arange(DD)] = 1
    mixed = jnp.einsum("rq,giq->irg", jnp.asarray(rows, BF), mixed, preferred_element_type=F32).astype(BF)
    mixed = mixed.reshape(4 * PAIR, CHI)
    mixed = jnp.concatenate([mixed, swap(mixed)], axis=0)

    pick = jnp.asarray(parity_table(), BF)
    choose = lambda c: jnp.einsum(
        "je,iek->ikj", lax.dynamic_index_in_dim(pick, c, 0, keepdims=False), upper[0], preferred_element_type=F32
    ).astype(BF)
    other = swap(choose(1 - core))
    own = choose(core)

    metric = build_metric(mixed, cols_all, own, other)

    first, second, fold = (jnp.asarray(t, BF) for t in tables())
    flag = core.astype(jnp.int32).reshape(1)
    forward = functools.partial(apply_metric, True)
    backward = functools.partial(apply_metric, False)
    ahead, behind = (first, second.T, fold), (second, first.T, fold)

    start = to_packed(right_side[0])
    keep, send = forward(first_vector, flag, metric, ahead, [start], [])
    pair, norm_0 = sum_chi(keep, send, jnp.sum(start * start, axis=(0, 1))[None])
    image, curve_0, keep, send = backward(first_image, flag, metric, behind, [*pair, start], [VECTOR, LANES])
    pair, curve_0 = sum_chi(keep, send, curve_0)
    residual, norm_1, keep, send = forward(
        next_residual, flag, metric, ahead, [*pair, start, norm_0, curve_0], [VECTOR, LANES]
    )
    pair, norm_1 = sum_chi(keep, send, norm_1)
    direction, curve_1, keep, send = backward(
        next_image, flag, metric, behind, [*pair, start, image, residual, norm_0, norm_1], [VECTOR, LANES]
    )
    pair, curve_1 = sum_chi(keep, send, curve_1)
    answer, residual = finish(flag, *pair, start, residual, direction, norm_0, curve_0, norm_1, curve_1)
    return from_packed(answer), from_packed(residual)


def solution(mesh):
    split = Mesh(mesh.devices.reshape(NX, NZ, NCORE, NSITE), ("x", "z", "core", "site"))
    chi = ("x", "z", "core")
    placed = (
        P("site", chi, None, None),
        P("site", None, None),
        P("site", None, chi, None),
        P("site", None, None),
        P("site", chi, None, None),
        P("site", None, None),
    )
    return jax.shard_map(
        body,
        mesh=split,
        in_specs=placed,
        out_specs=(P("site", None, None), P("site", None, None)),
        check_vma=False,
    )
```

time: 378 us -> 230 us (0.61)
  local copies, waits for them, and re-layouts: 102 us -> 25.3 us
  matrix products: 70.7 us -> 11.1 us
  blocking collectives: 69 us -> 11.8 us
  Pallas kernels: 0 us -> 54.1 us
  starting transfers between devices: 35.6 us -> 69.5 us
  waiting for transfers between devices: 68.7 us -> 41.7 us
  other arithmetic: 8.09 us -> 0.86 us
  between operations: 18.8 us -> 14.5 us
    reshape x5 -> x8, local copies, waits for them, and re-layouts: 63.9 us -> 3.76 us  [the longest x4 1.72 us: from_packed(): packed.reshape(PHYS, 4, 8, 2, 64).transpose(0, 4, 3, 1, 2)]
    dot_general x11 -> x6, matrix products: 70.7 us -> 11.1 us  [the longest x2 9.24 us: body(): jnp.einsum('je,iek->ikj', lax.dynamic_index_in_dim(pick, c, 0, keepdims=F...]
    all_to_all x5 -> x1, blocking collectives: 69 us -> 11.8 us  [spread(): lax.all_to_all(jnp.broadcast_to(value[None], (count,) + value.shape), axe...]
    pallas_call x0 -> x6, Pallas kernels: none -> 54.1 us  [the longest x4 30.1 us: apply_metric(): pl.pallas_call(functools.partial(apply_kernel, forward, prologue, len(ins...]
    all_gather x2 -> x1, waiting for transfers between devices: 50.5 us -> 7.27 us  [body(): cols_all = lax.all_gather(cols, 'z')]
    transpose x1 -> x6, local copies, waits for them, and re-layouts: 26.4 us -> 0.79 us  [the longest x4 0.55 us: from_packed(): return grid[:, :DD, :D, :D].transpose(0, 1, 3, 2).reshape(1, PHYS, DD * DD)]
    all_to_all x1 -> x5, starting transfers between devices: 8.33 us -> 33.2 us  [the longest x4 23.5 us: spread(): lax.all_to_all(jnp.broadcast_to(value[None], (count,) + value.shape), axe...]
    all_to_all x1 -> x5, waiting for transfers between devices: 0.01 us -> 17.8 us  [the longest x4 12.3 us: spread(): lax.all_to_all(jnp.broadcast_to(value[None], (count,) + value.shape), axe...]
  transfers between devices with their start and end apart: 19 -> 24, of which waited for: 16 -> 23; matrix products, arithmetic and copies ran while one was open for 5% -> 11% of each run, Pallas kernels for 0% -> 0%
where the time goes in v2:
time: 230 us; the launch traced here: 229 us
  starting transfers between devices  69.5 us (30%)
  Pallas kernels  54.1 us (24%)
  waiting for transfers between devices  41.7 us (18%)
  local copies, waits for them, and re-layouts  25.3 us (11%)
  between operations  14.5 us (6%)
  blocking collectives  11.8 us (5%)
  matrix products  11.1 us (5%)
    pallas_call x4, Pallas kernels, apply_metric(): pl.pallas_call(functools.partial(apply_kernel, forward, prologue, len(ins...  30.1 us
    all_to_all x4, starting transfers between devices, spread(): lax.all_to_all(jnp.broadcast_to(value[None], (count,) + value.shape), axe...  23.5 us
    pallas_call x1, Pallas kernels, build_metric(): pl.pallas_call(metric_kernel, grid=(pl.cdiv(WIDE, STRIPE),), in_specs=[pl...  22.4 us
    ppermute x10, starting transfers between devices, swap(): return lax.ppermute(value, 'core', [(0, 1), (1, 0)])  20 us
    ppermute x8, starting transfers between devices, sum_chi(): lax.ppermute(lanes, 'site', [(i, i ^ step) for i in range(NSITE)])  16.2 us
    all_to_all x4, waiting for transfers between devices, spread(): lax.all_to_all(jnp.broadcast_to(value[None], (count,) + value.shape), axe...  12.3 us
    all_to_all x1, blocking collectives, spread(): lax.all_to_all(jnp.broadcast_to(value[None], (count,) + value.shape), axe...  11.8 us
    all_to_all x1, starting transfers between devices, body(): lax.all_to_all(mixed, ('x', 'z', 'core'), 0, 0, tiled=True)  9.74 us
  transfers between devices with their start and end apart: 24, of which 23 were waited for; matrix products, arithmetic and copies ran while one was open for 11% of the time, Pallas kernels for 0%

profile of v2, /device:TPU:1, one launch (start us, length us, event | category | flops | bytes accessed | tf_op | source)
XLA Modules:
  0.0 228.8 jit_solution(8943527124706314794)
XLA Ops:
  9.3 11.8 %all_to_all.30 = bf16[4,392,128]{2,1,0:T(8,128)(2,1)S(1)} all-to-all(bf16[4,392,128]{2,1,0:T(8,128)(2,1)S(1)} %broadcast_in_dim.15), channel_id=1, replica_groups=mesh['x'=4,'z'=8,'core'=2,'site'=4] {'x'}, dimensions={0} | all-to-all | bytes 802816 | tf_op jit(solution)/shard_map/all_to_all | solution.py:315
  22.5 3.9 %fusion.5 = bf16[4,2401,128]{2,1,0:T(8,128)(2,1)S(1)} fusion(bf16[4,256,2401]{1,0,2:T(4,128)(2,1)} %bitcast.55, bf16[2,128,256]{2,1,0:T(8,128)(2,1)S(1)} %copy-done.12, s32[]{:T(128)S(6)} %select_n.8), kind=kOutput, calls=%fused_computation.5 | convolution fusion | flops 630637056 | bytes 7441412 | tf_op jit(solution)/shard_map/je,iek->ikj/dot_general | solution.py:366
  26.4 9.5 %copy.77 = bf16[4,2401,128]{2,0,1:T(4,128)(2,1)S(1)} copy(bf16[4,2401,128]{2,1,0:T(8,128)(2,1)S(1)} %fusion.5) | data formatting | bytes 4917248 | tf_op jit(solution)/shard_map/convert_element_type | solution.py:368
  35.9 2.0 collective-permute-start.1
  39.4 9.7 %all-to-all-start = ((bf16[64,2,392]{2,1,0:T(2,128)(2,1)}), bf16[64,2,392]{2,1,0:T(2,128)(2,1)S(1)}, u32[]{:S(2)}, u32[]{:S(2)}) async-start(bf16[64,2,392]{2,1,0:T(2,128)(2,1)} %reshape.67), calls=%async_computation | async-start | bytes 262144 | tf_op jit(solution)/shard_map/all_to_all | solution.py:358
  49.1 5.3 %fusion.2.own_ref = bf16[4,2401,128]{2,1,0:T(8,128)(2,1)} fusion(bf16[4,256,2401]{1,0,2:T(4,128)(2,1)} %bitcast.56, bf16[2,128,256]{2,1,0:T(8,128)(2,1)S(1)} %copy-done.12, s32[]{:T(128)S(6)} %select_n.7), kind=kOutput, calls=%fused_computation.4 | convolution fusion | flops 630637056 | bytes 7441412 | tf_op jit(solution)/shard_map/je,iek->ikj/dot_general | solution.py:366
  54.6 5.5 %all-to-all-done = bf16[64,2,392]{2,1,0:T(2,128)(2,1)S(1)} async-done(((bf16[64,2,392]{2,1,0:T(2,128)(2,1)}), bf16[64,2,392]{2,1,0:T(2,128)(2,1)S(1)}, u32[]{:S(2)}, u32[]{:S(2)}) %all-to-all-start) | async-done | bytes 100384 | tf_op jit(solution)/shard_map/all_to_all | solution.py:358
  62.5 3.6 %copy.78.other_ref = bf16[4,2401,128]{2,1,0:T(8,128)(2,1)} copy(bf16[4,2401,128]{2,0,1:T(4,128)(2,1)} %collective-permute-done.1) | data formatting | bytes 4917248 | tf_op jit(solution)/shard_map/ppermute | solution.py:319
  66.1 7.3 %all-gather.2.cloned.1.call-done.cols_ref = bf16[8,49,16,256]{3,2,1,0:T(8,128)(2,1)} async-done(((bf16[1,49,16,256]{3,2,1,0:T(8,128)(2,1)}), bf16[8,49,16,256]{3,2,1,0:T(8,128)(2,1)}) %all-gather.2.cloned.1.call-update) | async-done | bytes 3211280 | tf_op jit(solution)/shard_map/all_gather | solution.py:354
  73.3 22.4 %build_metric.1.refs_0_ = bf16[7,400,2432]{2,1,0:T(8,128)(2,1)} custom-call(bf16[448,256]{1,0:T(8,128)(2,1)S(1)} %pad_maximum_fusion.mixed_ref, bf16[8,49,16,256]{3,2,1,0:T(8,128)(2,1)} %all-gather.2.cloned.1.call-done.cols_ref, bf16[4,2401,128]{2,1,0:T(8,128)(2,1)} %fusion.2.own_ref, bf16[4,2401,128]{2,1,0:T(8,128)(2,1)} %copy.78.other_ref), custom_call_target="tpu_custom_call" | custom-call | flops 15000000512 | bytes 22000000 | tf_op jit(solution)/shard_map/build_metric/pallas_call | solution.py:115
  95.8 7.0 %forward.2 = (f32[32,128]{1,0:T(8,128)S(1)}, f32[32,128]{1,0:T(8,128)S(1)}) custom-call(s32[1]{0:T(128)} %bitcast.core_ref, bf16[7,400,2432]{2,1,0:T(8,128)(2,1)} %build_metric.1.refs_0_, bf16[128,2432]{1,0:T(8,128)(2,1)S(1)} %copy-done.4, bf16[2432,128]{1,0:T(8,128)(2,1)S(1)} %copy-done.5, bf16[112,784]{1,0:T(8,128)(2,1)S(1)} %copy-done.1, ...), custom_call_target="tpu_custom_call" | custom-call | flops 50000000 | bytes 14000000 | tf_op jit(solution)/shard_map/forward/pallas_call | solution.py:230
  105.2 6.9 %all-to-all-start.2 = ((bf16[32,32,128]{2,1,0:T(8,128)(2,1)}), bf16[32,32,128]{2,1,0:T(8,128)(2,1)S(1)}, u32[]{:S(2)}, u32[]{:S(2)}) async-start(bf16[32,32,128]{2,1,0:T(8,128)(2,1)} %broadcast_in_dim.16), calls=%async_computation.2 | async-start | bytes 524288 | tf_op jit(solution)/shard_map/all_to_all | solution.py:315
  114.6 2.7 %collective-permute-start.4 = (f32[1,128]{1,0:T(1,128)S(1)}, f32[1,128]{1,0:T(1,128)S(1)}, u32[]{:S(2)}, u32[]{:S(2)}) collective-permute-start(f32[1,128]{1,0:T(1,128)S(1)} %add.49), channel_id=1, source_target_pairs={{0,2},{1,3},{2,0},{3,1},{4,6},{5,7},{6,4},{7,5},{8,10},{9,11},{10,... | collective-permute-start | bytes 1544 | tf_op jit(solution)/shard_map/ppermute | solution.py:327
  118.5 3.3 %all-to-all-done.2 = bf16[32,32,128]{2,1,0:T(8,128)(2,1)S(1)} async-done(((bf16[32,32,128]{2,1,0:T(8,128)(2,1)}), bf16[32,32,128]{2,1,0:T(8,128)(2,1)S(1)}, u32[]{:S(2)}, u32[]{:S(2)}) %all-to-all-start.2) | async-done | bytes 262176 | tf_op jit(solution)/shard_map/all_to_all | solution.py:315
  121.8 3.8 %collective-permute-start.5 = (f32[32,128]{1,0:T(8,128)S(1)}, f32[32,128]{1,0:T(8,128)S(1)}, u32[]{:S(2)}, u32[]{:S(2)}) collective-permute-start(f32[32,128]{1,0:T(8,128)S(1)} %convert_reduce_fusion.3.refs_4_), channel_id=1, source_target_pairs={{0,4},{4,0},{1,5},{5,1},{2,6},{6,2},{3,7},{7,3},{8,12},{12,8},{9,1... | collective-permute-start | bytes 49160 | tf_op jit(solution)/shard_map/ppermute | solution.py:319
  126.4 8.1 %backward.2 = (f32[2,32,128]{2,1,0:T(8,128)S(1)}, f32[1,128]{1,0:T(1,128)S(1)}, f32[32,128]{1,0:T(8,128)S(1)}, f32[32,128]{1,0:T(8,128)S(1)}) custom-call(s32[1]{0:T(128)} %bitcast.core_ref, bf16[7,400,2432]{2,1,0:T(8,128)(2,1)} %build_metric.1.refs_0_, bf16[128,2432]{1,0:T(8,128)(2,1)S(1)} %copy-done.2, bf16[2432,128]{1,0:T(8,128)(2,1)S(1)} %copy-done.3, ...), custom_call_target="tpu_custom_call" | custom-call | flops 50000000 | bytes 14000000 | tf_op jit(solution)/shard_map/backward/pallas_call | solution.py:230
  136.5 5.5 %all-to-all-start.3 = ((bf16[32,32,128]{2,1,0:T(8,128)(2,1)}), bf16[32,32,128]{2,1,0:T(8,128)(2,1)S(1)}, u32[]{:S(2)}, u32[]{:S(2)}) async-start(bf16[32,32,128]{2,1,0:T(8,128)(2,1)} %broadcast_in_dim.18), calls=%async_computation.3 | async-start | bytes 524288 | tf_op jit(solution)/shard_map/all_to_all | solution.py:315
  142.0 1.5 collective-permute-start.7
  144.7 2.7 %collective-permute-start.8 = (f32[1,128]{1,0:T(1,128)S(1)}, f32[1,128]{1,0:T(1,128)S(1)}, u32[]{:S(2)}, u32[]{:S(2)}) collective-permute-start(f32[1,128]{1,0:T(1,128)S(1)} %add.52), channel_id=1, source_target_pairs={{0,2},{1,3},{2,0},{3,1},{4,6},{5,7},{6,4},{7,5},{8,10},{9,11},{10,... | collective-permute-start | bytes 1544 | tf_op jit(solution)/shard_map/ppermute | solution.py:327
  148.6 3.1 %all-to-all-done.3 = bf16[32,32,128]{2,1,0:T(8,128)(2,1)S(1)} async-done(((bf16[32,32,128]{2,1,0:T(8,128)(2,1)}), bf16[32,32,128]{2,1,0:T(8,128)(2,1)S(1)}, u32[]{:S(2)}, u32[]{:S(2)}) %all-to-all-start.3) | async-done | bytes 262176 | tf_op jit(solution)/shard_map/all_to_all | solution.py:315
  151.8 3.8 %collective-permute-start.9 = (f32[32,128]{1,0:T(8,128)S(1)}, f32[32,128]{1,0:T(8,128)S(1)}, u32[]{:S(2)}, u32[]{:S(2)}) collective-permute-start(f32[32,128]{1,0:T(8,128)S(1)} %convert_reduce_fusion.2.refs_4_), channel_id=1, source_target_pairs={{0,4},{4,0},{1,5},{5,1},{2,6},{6,2},{3,7},{7,3},{8,12},{12,8},{9,1... | collective-permute-start | bytes 49160 | tf_op jit(solution)/shard_map/ppermute | solution.py:319
  156.4 6.9 %forward.3 = (f32[2,32,128]{2,1,0:T(8,128)S(1)}, f32[1,128]{1,0:T(1,128)S(1)}, f32[32,128]{1,0:T(8,128)S(1)}, f32[32,128]{1,0:T(8,128)S(1)}) custom-call(s32[1]{0:T(128)} %bitcast.core_ref, bf16[7,400,2432]{2,1,0:T(8,128)(2,1)} %build_metric.1.refs_0_, bf16[128,2432]{1,0:T(8,128)(2,1)S(1)} %copy-done.4, bf16[2432,128]{1,0:T(8,128)(2,1)S(1)} %copy-done.5, ...), custom_call_target="tpu_custom_call" | custom-call | flops 50000000 | bytes 14000000 | tf_op jit(solution)/shard_map/forward/pallas_call | solution.py:230
  165.3 5.7 %all-to-all-start.4 = ((bf16[32,32,128]{2,1,0:T(8,128)(2,1)}), bf16[32,32,128]{2,1,0:T(8,128)(2,1)S(1)}, u32[]{:S(2)}, u32[]{:S(2)}) async-start(bf16[32,32,128]{2,1,0:T(8,128)(2,1)} %broadcast_in_dim.19), calls=%async_computation.4 | async-start | bytes 524288 | tf_op jit(solution)/shard_map/all_to_all | solution.py:315
  173.5 2.7 %collective-permute-start.12 = (f32[1,128]{1,0:T(1,128)S(1)}, f32[1,128]{1,0:T(1,128)S(1)}, u32[]{:S(2)}, u32[]{:S(2)}) collective-permute-start(f32[1,128]{1,0:T(1,128)S(1)} %add.55), channel_id=1, source_target_pairs={{0,2},{1,3},{2,0},{3,1},{4,6},{5,7},{6,4},{7,5},{8,10},{9,11},{10,... | collective-permute-start | bytes 1544 | tf_op jit(solution)/shard_map/ppermute | solution.py:327
  177.4 3.3 %all-to-all-done.4 = bf16[32,32,128]{2,1,0:T(8,128)(2,1)S(1)} async-done(((bf16[32,32,128]{2,1,0:T(8,128)(2,1)}), bf16[32,32,128]{2,1,0:T(8,128)(2,1)S(1)}, u32[]{:S(2)}, u32[]{:S(2)}) %all-to-all-start.4) | async-done | bytes 262176 | tf_op jit(solution)/shard_map/all_to_all | solution.py:315
  180.8 3.8 %collective-permute-start.13 = (f32[32,128]{1,0:T(8,128)S(1)}, f32[32,128]{1,0:T(8,128)S(1)}, u32[]{:S(2)}, u32[]{:S(2)}) collective-permute-start(f32[32,128]{1,0:T(8,128)S(1)} %convert_reduce_fusion.1.refs_4_), channel_id=1, source_target_pairs={{0,4},{4,0},{1,5},{5,1},{2,6},{6,2},{3,7},{7,3},{8,12},{12,8},{9,1... | collective-permute-start | bytes 49160 | tf_op jit(solution)/shard_map/ppermute | solution.py:319
  185.4 8.1 %backward.3 = (f32[2,32,128]{2,1,0:T(8,128)S(1)}, f32[1,128]{1,0:T(1,128)S(1)}, f32[32,128]{1,0:T(8,128)S(1)}, f32[32,128]{1,0:T(8,128)S(1)}) custom-call(s32[1]{0:T(128)} %bitcast.core_ref, bf16[7,400,2432]{2,1,0:T(8,128)(2,1)} %build_metric.1.refs_0_, bf16[128,2432]{1,0:T(8,128)(2,1)S(1)} %copy-done.2, bf16[2432,128]{1,0:T(8,128)(2,1)S(1)} %copy-done.3, ...), custom_call_target="tpu_custom_call" | custom-call | flops 50000000 | bytes 14000000 | tf_op jit(solution)/shard_map/backward/pallas_call | solution.py:230
  196.0 5.5 %all-to-all-start.5 = ((bf16[32,32,128]{2,1,0:T(8,128)(2,1)}), bf16[32,32,128]{2,1,0:T(8,128)(2,1)S(1)}, u32[]{:S(2)}, u32[]{:S(2)}) async-start(bf16[32,32,128]{2,1,0:T(8,128)(2,1)} %broadcast_in_dim.40), calls=%async_computation.5 | async-start | bytes 524288 | tf_op jit(solution)/shard_map/all_to_all | solution.py:315
  204.0 2.7 %collective-permute-start.16 = (f32[1,128]{1,0:T(1,128)S(1)}, f32[1,128]{1,0:T(1,128)S(1)}, u32[]{:S(2)}, u32[]{:S(2)}) collective-permute-start(f32[1,128]{1,0:T(1,128)S(1)} %add.58), channel_id=1, source_target_pairs={{0,2},{1,3},{2,0},{3,1},{4,6},{5,7},{6,4},{7,5},{8,10},{9,11},{10,... | collective-permute-start | bytes 1544 | tf_op jit(solution)/shard_map/ppermute | solution.py:327
  208.4 2.7 %all-to-all-done.5 = bf16[32,32,128]{2,1,0:T(8,128)(2,1)S(1)} async-done(((bf16[32,32,128]{2,1,0:T(8,128)(2,1)}), bf16[32,32,128]{2,1,0:T(8,128)(2,1)S(1)}, u32[]{:S(2)}, u32[]{:S(2)}) %all-to-all-start.5) | async-done | bytes 262176 | tf_op jit(solution)/shard_map/all_to_all | solution.py:315
  211.2 3.8 %collective-permute-start.17 = (f32[32,128]{1,0:T(8,128)S(1)}, f32[32,128]{1,0:T(8,128)S(1)}, u32[]{:S(2)}, u32[]{:S(2)}) collective-permute-start(f32[32,128]{1,0:T(8,128)S(1)} %convert_reduce_fusion.own_ref), channel_id=1, source_target_pairs={{0,4},{4,0},{1,5},{5,1},{2,6},{6,2},{3,7},{7,3},{8,12},{12,8},{9,1... | collective-permute-start | bytes 49160 | tf_op jit(solution)/shard_map/ppermute | solution.py:319
  216.4 1.5 finish.1
  (119 shorter events, 38.4 us)
Async XLA Ops:
  7.2 66.2 %all-gather.2.cloned.1.call-start = ((), (), s32[]{:S(2)}) async-start(), calls=%async_computation.6 | async-start | bytes 3612672 | tf_op jit(solution)/shard_map/all_gather | solution.py:354
  35.9 26.6 %collective-permute-start.1 = (bf16[4,2401,128]{2,0,1:T(4,128)(2,1)S(1)}, bf16[4,2401,128]{2,0,1:T(4,128)(2,1)}, u32[]{:S(2)}, u32[]{:S(2)}) collective-permute-start(bf16[4,2401,128]{2,0,1:T(4,128)(2,1)S(1)} %copy.77), channel_id=1, source_target_pairs={{0,4},{4,0},{1,5},{5,1},{2,6},{6,2},{3,7},{7,3},{8,12},{12,8},{9,1... | collective-permute-start | bytes 7375880 | tf_op jit(solution)/shard_map/ppermute | solution.py:319
  39.4 20.7 %all-to-all-start = ((bf16[64,2,392]{2,1,0:T(2,128)(2,1)}), bf16[64,2,392]{2,1,0:T(2,128)(2,1)S(1)}, u32[]{:S(2)}, u32[]{:S(2)}) async-start(bf16[64,2,392]{2,1,0:T(2,128)(2,1)} %reshape.67), calls=%async_computation | async-start | bytes 262144 | tf_op jit(solution)/shard_map/all_to_all | solution.py:358
  60.6 1.9 collective-permute-start
  62.0 123.3 %copy-start.6 = (f32[2,32,128]{2,1,0:T(8,128)}, f32[2,32,128]{2,1,0:T(8,128)S(1)}, u32[]{:S(2)}) copy-start(f32[2,32,128]{2,1,0:T(8,128)S(1)} %reshape.52.refs_4_.refs_6_.start_ref) | copy-start | bytes 98308
  66.1 29.7 %copy-start.1 = (bf16[112,784]{1,0:T(8,128)(2,1)S(1)}, bf16[112,784]{1,0:T(8,128)(2,1)}, u32[]{:S(2)}) copy-start(bf16[112,784]{1,0:T(8,128)(2,1)} %constant.38.clone.refs_3_) | copy-start | bytes 526852
  66.1 29.7 %copy-start.4 = (bf16[128,2432]{1,0:T(8,128)(2,1)S(1)}, bf16[128,2432]{1,0:T(8,128)(2,1)}, u32[]{:S(2)}) copy-start(bf16[128,2432]{1,0:T(8,128)(2,1)} %constant.36.clone.refs_1_) | copy-start | bytes 1867780
  66.1 29.7 %copy-start.5 = (bf16[2432,128]{1,0:T(8,128)(2,1)S(1)}, bf16[2432,128]{1,0:T(8,128)(2,1)}, u32[]{:S(2)}) copy-start(bf16[2432,128]{1,0:T(8,128)(2,1)} %constant.49.refs_2_) | copy-start | bytes 1867780
  95.7 30.7 %copy-start.2 = (bf16[128,2432]{1,0:T(8,128)(2,1)S(1)}, bf16[128,2432]{1,0:T(8,128)(2,1)}, u32[]{:S(2)}) copy-start(bf16[128,2432]{1,0:T(8,128)(2,1)} %constant.37.clone.refs_1_) | copy-start | bytes 1867780
  95.7 30.7 %copy-start.3 = (bf16[2432,128]{1,0:T(8,128)(2,1)S(1)}, bf16[2432,128]{1,0:T(8,128)(2,1)}, u32[]{:S(2)}) copy-start(bf16[2432,128]{1,0:T(8,128)(2,1)} %constant.48.refs_2_) | copy-start | bytes 1867780
  102.8 1.7 collective-permute-start.2
  105.2 16.5 %all-to-all-start.2 = ((bf16[32,32,128]{2,1,0:T(8,128)(2,1)}), bf16[32,32,128]{2,1,0:T(8,128)(2,1)S(1)}, u32[]{:S(2)}, u32[]{:S(2)}) async-start(bf16[32,32,128]{2,1,0:T(8,128)(2,1)} %broadcast_in_dim.16), calls=%async_computation.2 | async-start | bytes 524288 | tf_op jit(solution)/shard_map/all_to_all | solution.py:315
  112.2 2.4 %collective-permute-start.3 = (f32[1,128]{1,0:T(1,128)S(1)}, f32[1,128]{1,0:T(1,128)S(1)}, u32[]{:S(2)}, u32[]{:S(2)}) collective-permute-start(f32[1,128]{1,0:T(1,128)S(1)} %broadcast_in_dim.17), channel_id=1, source_target_pairs={{0,1},{1,0},{2,3},{3,2},{4,5},{5,4},{6,7},{7,6},{8,9},{9,8},{10,11... | collective-permute-start | bytes 1544 | tf_op jit(solution)/shard_map/ppermute | solution.py:327
  114.6 3.9 %collective-permute-start.4 = (f32[1,128]{1,0:T(1,128)S(1)}, f32[1,128]{1,0:T(1,128)S(1)}, u32[]{:S(2)}, u32[]{:S(2)}) collective-permute-start(f32[1,128]{1,0:T(1,128)S(1)} %add.49), channel_id=1, source_target_pairs={{0,2},{1,3},{2,0},{3,1},{4,6},{5,7},{6,4},{7,5},{8,10},{9,11},{10,... | collective-permute-start | bytes 1544 | tf_op jit(solution)/shard_map/ppermute | solution.py:327
  118.5 66.9 %copy-start.9 = (f32[1,128]{1,0:T(1,128)}, f32[1,128]{1,0:T(1,128)S(1)}, u32[]{:S(2)}) copy-start(f32[1,128]{1,0:T(1,128)S(1)} %add.50.refs_7_.refs_9_.norm_ref) | copy-start | bytes 1540
  121.8 4.6 %collective-permute-start.5 = (f32[32,128]{1,0:T(8,128)S(1)}, f32[32,128]{1,0:T(8,128)S(1)}, u32[]{:S(2)}, u32[]{:S(2)}) collective-permute-start(f32[32,128]{1,0:T(8,128)S(1)} %convert_reduce_fusion.3.refs_4_), channel_id=1, source_target_pairs={{0,4},{4,0},{1,5},{5,1},{2,6},{6,2},{3,7},{7,3},{8,12},{12,8},{9,1... | collective-permute-start | bytes 49160 | tf_op jit(solution)/shard_map/ppermute | solution.py:319
  134.5 1.3 collective-permute-start.6
  136.5 15.2 %all-to-all-start.3 = ((bf16[32,32,128]{2,1,0:T(8,128)(2,1)}), bf16[32,32,128]{2,1,0:T(8,128)(2,1)S(1)}, u32[]{:S(2)}, u32[]{:S(2)}) async-start(bf16[32,32,128]{2,1,0:T(8,128)(2,1)} %broadcast_in_dim.18), calls=%async_computation.3 | async-start | bytes 524288 | tf_op jit(solution)/shard_map/all_to_all | solution.py:315
  142.0 2.7 %collective-permute-start.7 = (f32[1,128]{1,0:T(1,128)S(1)}, f32[1,128]{1,0:T(1,128)S(1)}, u32[]{:S(2)}, u32[]{:S(2)}) collective-permute-start(f32[1,128]{1,0:T(1,128)S(1)} %get-tuple-element.31), channel_id=1, source_target_pairs={{0,1},{1,0},{2,3},{3,2},{4,5},{5,4},{6,7},{7,6},{8,9},{9,8},{10,11... | collective-permute-start | bytes 1544 | tf_op jit(solution)/shard_map/ppermute | solution.py:327
  144.7 3.9 %collective-permute-start.8 = (f32[1,128]{1,0:T(1,128)S(1)}, f32[1,128]{1,0:T(1,128)S(1)}, u32[]{:S(2)}, u32[]{:S(2)}) collective-permute-start(f32[1,128]{1,0:T(1,128)S(1)} %add.52), channel_id=1, source_target_pairs={{0,2},{1,3},{2,0},{3,1},{4,6},{5,7},{6,4},{7,5},{8,10},{9,11},{10,... | collective-permute-start | bytes 1544 | tf_op jit(solution)/shard_map/ppermute | solution.py:327
  151.8 4.6 %collective-permute-start.9 = (f32[32,128]{1,0:T(8,128)S(1)}, f32[32,128]{1,0:T(8,128)S(1)}, u32[]{:S(2)}, u32[]{:S(2)}) collective-permute-start(f32[32,128]{1,0:T(8,128)S(1)} %convert_reduce_fusion.2.refs_4_), channel_id=1, source_target_pairs={{0,4},{4,0},{1,5},{5,1},{2,6},{6,2},{3,7},{7,3},{8,12},{12,8},{9,1... | collective-permute-start | bytes 49160 | tf_op jit(solution)/shard_map/ppermute | solution.py:319
  163.3 30.1 %copy-start.7 = (f32[2,32,128]{2,1,0:T(8,128)}, f32[2,32,128]{2,1,0:T(8,128)S(1)}, u32[]{:S(2)}) copy-start(f32[2,32,128]{2,1,0:T(8,128)S(1)} %get-tuple-element.40.refs_8_.residual_ref) | copy-start | bytes 98308
  163.3 1.3 collective-permute-start.10
  165.3 15.4 %all-to-all-start.4 = ((bf16[32,32,128]{2,1,0:T(8,128)(2,1)}), bf16[32,32,128]{2,1,0:T(8,128)(2,1)S(1)}, u32[]{:S(2)}, u32[]{:S(2)}) async-start(bf16[32,32,128]{2,1,0:T(8,128)(2,1)} %broadcast_in_dim.19), calls=%async_computation.4 | async-start | bytes 524288 | tf_op jit(solution)/shard_map/all_to_all | solution.py:315
  171.0 2.5 %collective-permute-start.11 = (f32[1,128]{1,0:T(1,128)S(1)}, f32[1,128]{1,0:T(1,128)S(1)}, u32[]{:S(2)}, u32[]{:S(2)}) collective-permute-start(f32[1,128]{1,0:T(1,128)S(1)} %get-tuple-element.37), channel_id=1, source_target_pairs={{0,1},{1,0},{2,3},{3,2},{4,5},{5,4},{6,7},{7,6},{8,9},{9,8},{10,11... | collective-permute-start | bytes 1544 | tf_op jit(solution)/shard_map/ppermute | solution.py:327
  173.5 3.9 %collective-permute-start.12 = (f32[1,128]{1,0:T(1,128)S(1)}, f32[1,128]{1,0:T(1,128)S(1)}, u32[]{:S(2)}, u32[]{:S(2)}) collective-permute-start(f32[1,128]{1,0:T(1,128)S(1)} %add.55), channel_id=1, source_target_pairs={{0,2},{1,3},{2,0},{3,1},{4,6},{5,7},{6,4},{7,5},{8,10},{9,11},{10,... | collective-permute-start | bytes 1544 | tf_op jit(solution)/shard_map/ppermute | solution.py:327
  180.8 4.6 %collective-permute-start.13 = (f32[32,128]{1,0:T(8,128)S(1)}, f32[32,128]{1,0:T(8,128)S(1)}, u32[]{:S(2)}, u32[]{:S(2)}) collective-permute-start(f32[32,128]{1,0:T(8,128)S(1)} %convert_reduce_fusion.1.refs_4_), channel_id=1, source_target_pairs={{0,4},{4,0},{1,5},{5,1},{2,6},{6,2},{3,7},{7,3},{8,12},{12,8},{9,1... | collective-permute-start | bytes 49160 | tf_op jit(solution)/shard_map/ppermute | solution.py:319
  194.1 1.2 collective-permute-start.14
  196.0 15.1 %all-to-all-start.5 = ((bf16[32,32,128]{2,1,0:T(8,128)(2,1)}), bf16[32,32,128]{2,1,0:T(8,128)(2,1)S(1)}, u32[]{:S(2)}, u32[]{:S(2)}) async-start(bf16[32,32,128]{2,1,0:T(8,128)(2,1)} %broadcast_in_dim.40), calls=%async_computation.5 | async-start | bytes 524288 | tf_op jit(solution)/shard_map/all_to_all | solution.py:315
  201.5 2.5 %collective-permute-start.15 = (f32[1,128]{1,0:T(1,128)S(1)}, f32[1,128]{1,0:T(1,128)S(1)}, u32[]{:S(2)}, u32[]{:S(2)}) collective-permute-start(f32[1,128]{1,0:T(1,128)S(1)} %get-tuple-element.44), channel_id=1, source_target_pairs={{0,1},{1,0},{2,3},{3,2},{4,5},{5,4},{6,7},{7,6},{8,9},{9,8},{10,11... | collective-permute-start | bytes 1544 | tf_op jit(solution)/shard_map/ppermute | solution.py:327
  204.0 3.9 %collective-permute-start.16 = (f32[1,128]{1,0:T(1,128)S(1)}, f32[1,128]{1,0:T(1,128)S(1)}, u32[]{:S(2)}, u32[]{:S(2)}) collective-permute-start(f32[1,128]{1,0:T(1,128)S(1)} %add.58), channel_id=1, source_target_pairs={{0,2},{1,3},{2,0},{3,1},{4,6},{5,7},{6,4},{7,5},{8,10},{9,11},{10,... | collective-permute-start | bytes 1544 | tf_op jit(solution)/shard_map/ppermute | solution.py:327
  211.2 4.6 %collective-permute-start.17 = (f32[32,128]{1,0:T(8,128)S(1)}, f32[32,128]{1,0:T(8,128)S(1)}, u32[]{:S(2)}, u32[]{:S(2)}) collective-permute-start(f32[32,128]{1,0:T(8,128)S(1)} %convert_reduce_fusion.own_ref), channel_id=1, source_target_pairs={{0,4},{4,0},{1,5},{5,1},{2,6},{6,2},{3,7},{7,3},{8,12},{12,8},{9,1... | collective-permute-start | bytes 49160 | tf_op jit(solution)/shard_map/ppermute | solution.py:319
  (12 other events, 148.0 us)
Sparse Core Ops, SparseCore 0:
  22.6 50.6 all-gather.1

commit v3 on v2

v3 whole, which is shorter than its diff:
```python
import functools
import math

import jax
import jax.numpy as jnp
import numpy as np
from jax import lax
from jax.experimental import pallas as pl
from jax.experimental.pallas import tpu as pltpu
from jax.sharding import Mesh, PartitionSpec as P

CHI = 256
D = 7
PHYS = 2
DD = 49
BF = jnp.bfloat16
F32 = jnp.float32

NX, NZ, NCORE, NSITE = 4, 8, 2, 4
CHIPS = NX * NZ
ROWS_I = 8
GROUP = 8
PAIR = D * GROUP
RB = 4
SLAB = RB * PAIR
WIDE = 2432
BLOCKS = WIDE // 128
CHUNK = 112
STRIPE = 512
PART = 128
OFFSETS = (0, -1, 1, -2, 2, -3, 3, 4)
VEC = PHYS * PAIR
IMG = PHYS * RB * GROUP

shift_value = 0.5
scale_metric = 1.0 / (CHI * DD)


def tables():
    lane = np.arange(WIDE)
    valid = lane < DD * DD
    first = np.zeros((128, WIDE), np.float32)
    first[(lane // DD)[valid], lane[valid]] = 1
    second = np.zeros((128, WIDE), np.float32)
    second[(lane % DD)[valid], lane[valid]] = 1
    fold = np.zeros((VEC, D * VEC), np.float32)
    for r in range(D):
        for p in range(PHYS):
            for q in range(D):
                for s in range(GROUP):
                    fold[p * PAIR + r * GROUP + q, r * VEC + p * PAIR + q * GROUP + s] = 1
    own = np.zeros((PAIR, WIDE), np.float32)
    for r in range(D):
        for q in range(D):
            own[r * GROUP + q] = second[q * D + r]
    return first, second, fold, own


def low_lanes():
    return lax.broadcasted_iota(jnp.int32, (32, 128), 1) < 64


def unpack(parts):
    rows = []
    for half in parts:
        rows.append(jnp.where(low_lanes(), half, 0.0))
        rows.append(jnp.where(low_lanes(), pltpu.roll(half, 64, 1), 0.0)[:24])
    return jnp.concatenate(rows, axis=0)


def pack(rows):
    out = []
    for p in range(PHYS):
        upper_rows = jnp.concatenate([rows[p * PAIR + 32 : p * PAIR + 56], jnp.zeros((8, 128), F32)], axis=0)
        out.append(rows[p * PAIR : p * PAIR + 32] + pltpu.roll(upper_rows, 64, 1))
    return out


def unpack_image(both):
    return jnp.concatenate(
        [jnp.where(low_lanes(), both, 0.0), jnp.where(low_lanes(), pltpu.roll(both, 64, 1), 0.0)], axis=0
    )


def pack_image(rows):
    return rows[:32] + pltpu.roll(rows[32:], 64, 1)


def two_terms(value):
    high = value.astype(BF)
    return high, (value - high.astype(F32)).astype(BF)


def dot(a, b):
    return jnp.dot(a, b, preferred_element_type=F32)


def dot_lanes(a, b):
    return lax.dot_general(a, b, (((1,), (1,)), ((), ())), preferred_element_type=F32)


def metric_kernel(n_blocks, more, mixed_ref, *refs):
    blocks, refs = refs[:n_blocks], refs[n_blocks:]
    own_ref, other_ref = refs[:2]
    out_ref, low_ref = refs[-2:]

    def block(b, pair):
        if b < 3 or n_blocks == 4:
            return blocks[b][pair]
        here = pair // (D * RB // 2)
        return blocks[3 + here][pair - here * (D * RB // 2)]

    @pl.when(pl.program_id(0) == 0)
    def _():
        for rk in range(D):
            cols = [block(b, rk * RB + rb) for rb in range(RB) for b in range(4)]
            low = dot_lanes(mixed_ref[...], jnp.concatenate(cols, axis=0)) * (1.0 / math.sqrt(CHI))
            for i in range(ROWS_I):
                strip = [low[i * PAIR : (i + 1) * PAIR, rb * PART : (rb + 1) * PART] for rb in range(RB)]
                low_ref[rk * SLAB : (rk + 1) * SLAB, i * PART : (i + 1) * PART] = jnp.concatenate(strip, axis=0).astype(BF)

    half = range(ROWS_I // 2)
    upper = jnp.concatenate([own_ref[i] for i in half] + [other_ref[i] for i in half], axis=1)
    value = dot_lanes(low_ref[...], upper)
    for rk in range(D):
        slab = value[rk * SLAB : (rk + 1) * SLAB]
        if more:
            slab = slab + refs[2][rk].astype(F32)
        out_ref[rk] = slab.astype(BF)


def build_metric(mixed, blocks, own, other, before=None):
    part = 0 if before is None else 1
    stripe = pl.BlockSpec((ROWS_I // 2, STRIPE, PART), lambda n: (0, n, part))
    result = pl.BlockSpec((D, SLAB, STRIPE), lambda n: (0, 0, n))
    arrays = [*blocks, own, other] + ([] if before is None else [before])
    return pl.pallas_call(
        functools.partial(metric_kernel, len(blocks), before is not None),
        grid=(pl.cdiv(WIDE, STRIPE),),
        in_specs=[full(mixed.shape)] + [full(b.shape) for b in blocks] + [stripe, stripe]
        + ([] if before is None else [result]),
        out_specs=result,
        out_shape=pltpu.HBM((D, SLAB, WIDE), BF),
        scratch_shapes=[pltpu.VMEM((D * SLAB, ROWS_I * PART), BF)],
        compiler_params=pltpu.CompilerParams(vmem_limit_bytes=34 * 1024 * 1024),
        cost_estimate=pl.CostEstimate(flops=8_000_000_000, bytes_accessed=22_000_000, transcendentals=0),
        name="build_first" if before is None else "build_second",
    )(mixed, *(pltpu.with_memory_space_constraint(a, pltpu.HBM) for a in arrays))


def full(shape):
    return pl.BlockSpec(shape, lambda *r: (0,) * len(shape))


def forward_step(step, metric_ref, e_ref, acc_ref):
    for block in range(BLOCKS):
        lanes = slice(block * 128, (block + 1) * 128)
        tile = metric_ref[step, :, lanes].astype(F32)
        for p in range(PHYS):
            eight = e_ref[pl.ds(pl.multiple_of(p * PAIR + step * GROUP, GROUP), GROUP), lanes]
            factors = [jnp.broadcast_to(eight[q : q + 1], (GROUP, 128)) for q in range(D)]
            for rb in range(RB):
                place = slice((p * RB + rb) * GROUP, (p * RB + rb + 1) * GROUP)
                total = acc_ref[place, lanes]
                for q in range(D):
                    row = (rb * D + q) * GROUP
                    total = total + tile[row : row + GROUP] * factors[q]
                acc_ref[place, lanes] = total


def backward_step(step, metric_ref, f_ref, z_ref):
    for block in range(BLOCKS):
        lanes = slice(block * 128, (block + 1) * 128)
        tile = metric_ref[step, :, lanes].astype(F32)
        for p in range(PHYS):
            factors = [f_ref[(p * RB + rb) * GROUP : (p * RB + rb + 1) * GROUP, lanes] for rb in range(RB)]
            for q in range(D):
                total = tile[q * GROUP : (q + 1) * GROUP] * factors[0]
                for rb in range(1, RB):
                    row = (rb * D + q) * GROUP
                    total = total + tile[row : row + GROUP] * factors[rb]
                z_ref[step, p * PAIR + q * GROUP : p * PAIR + (q + 1) * GROUP, lanes] = total


def halves(core_ref, own_ref, other_ref):
    first = core_ref[0] == 0
    own, other = own_ref[...], other_ref[...]
    return [jnp.where(first, own, other), jnp.where(first, other, own)]


def lane_sums(parts):
    total = parts[0]
    for part in parts[1:]:
        total = total + part
    return jnp.sum(total, axis=0, keepdims=True)


def apply_kernel(forward, prologue, n_in, n_out, core_ref, *refs):
    metric_ref, expand_ref, reduce_ref, fold_ref = refs[:4]
    ins, outs = refs[4 : 4 + n_in], refs[4 + n_in : 4 + n_in + n_out]
    wide_ref, sum_ref, slab_ref, sems = refs[-4:]
    step = pl.program_id(0)

    def fetch(r, c):
        rows = pl.ds(c * CHUNK, CHUNK)
        return pltpu.make_async_copy(metric_ref.at[r, rows], slab_ref.at[r, rows], sems.at[r, c])

    @pl.when(step == 0)
    def _():
        for r in range(D):
            for c in range(SLAB // CHUNK):
                fetch(r, c).start()
        vec = prologue(core_ref, ins, outs)
        rows = unpack(vec) if forward else unpack_image(vec)
        wide_ref[...] = dot(rows.astype(BF), expand_ref[...])
        if forward:
            sum_ref[...] = jnp.zeros_like(sum_ref)

    for c in range(SLAB // CHUNK):
        fetch(step, c).wait()
    (forward_step if forward else backward_step)(step, slab_ref, wide_ref, sum_ref)

    @pl.when(step == D - 1)
    def _():
        if forward:
            high, low = two_terms(sum_ref[...])
            rows = dot(high, reduce_ref[...]) + dot(low, reduce_ref[...])
            refs[-5][...] = pack_image(rows * scale_metric)
        else:
            sums = [dot(sum_ref[r].astype(BF), reduce_ref[...]) for r in range(D)]
            high, low = two_terms(jnp.concatenate(sums, axis=0))
            rows = dot(fold_ref[...], high) + dot(fold_ref[...], low)
            parts = pack(rows * scale_metric)
            first = core_ref[0] == 0
            refs[-6][...] = jnp.where(first, parts[0], parts[1])
            refs[-5][...] = jnp.where(first, parts[1], parts[0])


VECTOR = jax.ShapeDtypeStruct((PHYS, 32, 128), F32)
HALF = jax.ShapeDtypeStruct((32, 128), F32)


def sum_rows(count):
    return jax.ShapeDtypeStruct((count, 128), F32)


def apply_metric(forward, prologue, core, metric, constants, ins, outs):
    out_shape = list(outs) + ([HALF] if forward else [HALF, HALF])
    return pl.pallas_call(
        functools.partial(apply_kernel, forward, prologue, len(ins), len(outs)),
        grid=(D,),
        in_specs=[pl.BlockSpec(memory_space=pltpu.SMEM), pl.BlockSpec(memory_space=pl.ANY)]
        + [full(c.shape) for c in constants]
        + [full(i.shape) for i in ins],
        out_specs=[full(o.shape) for o in out_shape],
        out_shape=out_shape,
        scratch_shapes=[
            pltpu.VMEM((VEC if forward else IMG, WIDE), F32),
            pltpu.VMEM((IMG, WIDE) if forward else (D, VEC, WIDE), F32),
            pltpu.VMEM((D, SLAB, WIDE), BF),
            pltpu.SemaphoreType.DMA((D, SLAB // CHUNK)),
        ],
        compiler_params=pltpu.CompilerParams(vmem_limit_bytes=30 * 1024 * 1024),
        cost_estimate=pl.CostEstimate(flops=50_000_000, bytes_accessed=8_000_000, transcendentals=0),
        name="forward" if forward else "backward",
    )(core, pltpu.with_memory_space_constraint(metric, pltpu.HBM), *constants, *ins)


def first_vector(core_ref, ins, outs):
    return [ins[0][p] for p in range(PHYS)]


def share(a, b):
    return (shift_value / NCORE) * (a * b)


def sums_of(*groups):
    return jnp.concatenate([lane_sums(group) for group in groups], axis=0)


def first_image(core_ref, ins, outs):
    image = ins[0][...]
    start = [ins[1][p] for p in range(PHYS)]
    outs[0][...] = sums_of([image * image] + [share(v, v) for v in start], [v * v / NCORE for v in start])
    return image


def row(sums_ref, n):
    return jnp.sum(sums_ref[n : n + 1], axis=1, keepdims=True)


def next_residual(core_ref, ins, outs):
    own_ref, other_ref, start_ref, sums_ref = ins
    back = halves(core_ref, own_ref, other_ref)
    alpha = row(sums_ref, 1) / row(sums_ref, 0)
    residual = [start_ref[p] - alpha * (back[p] + shift_value * start_ref[p]) for p in range(PHYS)]
    for p in range(PHYS):
        outs[0][p] = residual[p]
    return residual


def next_image(core_ref, ins, outs):
    image, first = ins[0][...], ins[1][...]
    residual = [ins[2][p] for p in range(PHYS)]
    start = [ins[3][p] for p in range(PHYS)]
    outs[0][...] = sums_of(
        [image * image] + [share(r, r) for r in residual],
        [image * first] + [share(r, d) for r, d in zip(residual, start)],
        [r * r / NCORE for r in residual],
    )
    return image


def flatten(parts, expand_ref, own_ref):
    rest = unpack(parts)
    wide = None
    for _ in range(3):
        term = rest.astype(BF)
        rest = rest - term.astype(F32)
        piece = dot(term, expand_ref[...])
        wide = piece if wide is None else wide + piece
    own = own_ref[...].astype(F32)
    rows = [jnp.sum(wide[p * PAIR : (p + 1) * PAIR] * own, axis=0, keepdims=True) for p in range(PHYS)]
    return jnp.concatenate(rows, axis=0)[:, : DD * DD]


def finish_kernel(core_ref, expand_ref, own_lane_ref, half_0_ref, other_0_ref, half_1_ref, other_1_ref,
                  start_ref, residual_ref, sums_0_ref, sums_1_ref, solution_ref, out_ref):
    back_0 = halves(core_ref, half_0_ref, other_0_ref)
    back_r = halves(core_ref, half_1_ref, other_1_ref)
    curve_0, norm_0 = row(sums_0_ref, 0), row(sums_0_ref, 1)
    norm_1 = row(sums_1_ref, 2)
    alpha_0 = norm_0 / curve_0
    beta = norm_1 / norm_0
    curve_1 = row(sums_1_ref, 0) + beta * (2.0 * row(sums_1_ref, 1) + beta * curve_0)
    alpha_1 = norm_1 / curve_1
    answer, residual = [], []
    for p in range(PHYS):
        direction = residual_ref[p] + beta * start_ref[p]
        back = back_r[p] + beta * back_0[p] + shift_value * direction
        answer.append(alpha_0 * start_ref[p] + alpha_1 * direction)
        residual.append(residual_ref[p] - alpha_1 * back)
    solution_ref[0] = flatten(answer, expand_ref, own_lane_ref)
    out_ref[0] = flatten(residual, expand_ref, own_lane_ref)


def finish(core, *ins):
    field = jax.ShapeDtypeStruct((1, PHYS, DD * DD), F32)
    return pl.pallas_call(
        finish_kernel,
        in_specs=[pl.BlockSpec(memory_space=pltpu.SMEM)] + [full(i.shape) for i in ins],
        out_specs=[full(field.shape)] * 2,
        out_shape=[field, field],
        compiler_params=pltpu.CompilerParams(vmem_limit_bytes=16 * 1024 * 1024),
        name="finish",
    )(core, *ins)


def spread(value, axes, count):
    return lax.all_to_all(jnp.broadcast_to(value[None], (count,) + value.shape), axes, 0, 0, tiled=True)


def swap(value):
    return lax.ppermute(value, "core", [(0, 1), (1, 0)])


def sum_sites(lanes):
    for step in (1, 2):
        lanes = lanes + lax.ppermute(lanes, "site", [(i, i ^ step) for i in range(NSITE)])
    return lanes


def sum_chips(value, lanes=None, cores=False):
    parts = spread(value.astype(BF), ("x", "z"), CHIPS)
    if lanes is not None:
        lanes = sum_sites(lanes)
        if cores:
            lanes = lanes + swap(lanes)
        parts, lanes = lax.optimization_barrier((parts, lanes))
    return jnp.sum(parts.astype(F32), axis=0), lanes


def sum_halves(keep, send, lanes):
    half, lanes = sum_chips(keep + swap(send), lanes, True)
    return half, swap(half), lanes


def to_packed(field):
    move = np.zeros((2, 32, DD), np.float32)
    for dk in range(D):
        for rk in range(D):
            move[rk // 4, rk % 4 * GROUP + dk, dk * D + rk] = 1
    grid = jnp.einsum("hrc,pkc->prhk", move, field.reshape(PHYS, DD, DD), precision=lax.Precision.HIGHEST)
    return jnp.pad(grid, ((0, 0), (0, 0), (0, 0), (0, 64 - DD))).reshape(PHYS, 32, 128)


def ring(value, step):
    return lax.ppermute(value, "z", [(i, (i + step) % NZ) for i in range(NZ)])


def body(upper, corner_low, edge_bottom, corner_right, edge_right, right_side):
    core = lax.axis_index("core")

    mixed = jnp.einsum("ih,hgq->giq", corner_low[0], edge_bottom[0], preferred_element_type=F32).astype(BF)
    mixed = mixed.reshape(4, 64, 4, DD).transpose(1, 0, 2, 3)

    cols = jnp.einsum("efr,gf->reg", edge_right[0], corner_right[0], preferred_element_type=F32).astype(BF)
    cols = jnp.pad(cols.reshape(D, D, 4, CHI), ((0, 0), (0, 1), (0, 0), (0, 0))).reshape(D, NCORE, RB, 4, CHI)
    mine = lax.dynamic_index_in_dim(cols, core, 1, keepdims=False)
    other = swap(lax.dynamic_index_in_dim(cols, 1 - core, 1, keepdims=False))
    cols = jnp.stack([jnp.where(core == 0, mine, other), jnp.where(core == 0, other, mine)], axis=2)
    cols = spread(cols.reshape(D * RB * 8 * CHI // 128, 128), "x", NX)
    cols = cols.reshape(NX, D * RB, 8, CHI).transpose(1, 0, 2, 3).reshape(D * RB, 8 * NX, CHI)

    row = jnp.arange(CHI)
    z = (lax.axis_index("z") + jnp.asarray(OFFSETS)[row // 32] + NZ) % NZ
    place = (row // 8 % NX * NZ + z) * 8 + row % 8
    pick = (place[:, None] == jnp.arange(CHI)[None, :]).astype(BF)
    own = jnp.einsum("je,iek->ikj", pick, upper[0], preferred_element_type=F32).astype(BF)
    own = jnp.pad(own, ((0, 0), (0, WIDE - DD * DD), (0, 0)))

    cols, mixed, own = lax.optimization_barrier((cols, mixed, own))
    other = swap(own)
    up, down = [cols], [cols]
    for _ in range(2):
        up.append(ring(up[-1], 1))
        down.append(ring(down[-1], -1))

    rows = np.zeros((PAIR, DD), np.float32)
    rows[np.arange(DD) // D * GROUP + np.arange(DD) % D, np.arange(DD)] = 1
    mixed = lax.all_to_all(mixed, ("x", "z", "core"), 0, 0, tiled=True).reshape(CHI, 4, DD)
    mixed = jnp.einsum("rq,giq->irg", jnp.asarray(rows, BF), mixed, preferred_element_type=F32).astype(BF)
    mixed = mixed.reshape(4 * PAIR, CHI)
    mixed = jnp.concatenate([mixed, swap(mixed)], axis=0)
    start = to_packed(right_side[0])

    up.append(ring(up[-1], 1))
    down.append(ring(down[-1], -1))
    metric = build_metric(mixed, [cols, up[1], down[1], up[2]], own, other)
    far_up, far_down, metric = lax.optimization_barrier((up[3], down[3], metric))
    last = [ring(far_up[: D * RB // 2], 1), ring(far_down[D * RB // 2 :], -1)]
    metric = build_metric(mixed, [down[2], far_up, far_down, *last], own, other, metric)

    first, second, fold, own_lane = (jnp.asarray(t, BF) for t in tables())
    flag = core.astype(jnp.int32).reshape(1)
    forward = functools.partial(apply_metric, True)
    backward = functools.partial(apply_metric, False)
    ahead, behind = (first, second.T, fold), (second, first.T, fold)

    (part,) = forward(first_vector, flag, metric, ahead, [start], [])
    image, _ = sum_chips(part)
    sums_0, keep, send = backward(first_image, flag, metric, behind, [image, start], [sum_rows(2)])
    half_0, other_0, sums_0 = sum_halves(keep, send, sums_0)
    residual, part = forward(next_residual, flag, metric, ahead, [half_0, other_0, start, sums_0], [VECTOR])
    image_r, _ = sum_chips(part)
    sums_1, keep, send = backward(next_image, flag, metric, behind, [image_r, image, residual, start], [sum_rows(3)])
    half_1, other_1, sums_1 = sum_halves(keep, send, sums_1)
    return finish(flag, first, own_lane, half_0, other_0, half_1, other_1, start, residual, sums_0, sums_1)


def solution(mesh):
    split = Mesh(mesh.devices.reshape(NX, NZ, NCORE, NSITE), ("x", "z", "core", "site"))
    chi = ("x", "z", "core")
    placed = (
        P("site", chi, None, None),
        P("site", None, None),
        P("site", None, chi, None),
        P("site", None, None),
        P("site", chi, None, None),
        P("site", None, None),
    )
    return jax.shard_map(
        body,
        mesh=split,
        in_specs=placed,
        out_specs=(P("site", None, None), P("site", None, None)),
        check_vma=False,
    )
```

time: 230 us -> 196 us (0.85)
  blocking collectives: 11.8 us -> 47.2 us
  local copies, waits for them, and re-layouts: 25.3 us -> 7.41 us
  waiting for transfers between devices: 41.7 us -> 25.1 us
  between operations: 14.5 us -> 1.09 us
  starting transfers between devices: 69.5 us -> 58.7 us
  matrix products: 11.1 us -> 5.85 us
  Pallas kernels: 54.1 us -> 50 us
    all_to_all x0 -> x1, blocking collectives: none -> 17.7 us  [body(): lax.all_to_all(mixed, ('x', 'z', 'core'), 0, 0, tiled=True)]
    all_to_all x1 -> x2, blocking collectives: 11.8 us -> 29.4 us  [spread(): lax.all_to_all(jnp.broadcast_to(value[None], (count,) + value.shape), axe...]
    all_to_all x4 -> x3, starting transfers between devices: 23.5 us -> 11.9 us  [spread(): lax.all_to_all(jnp.broadcast_to(value[None], (count,) + value.shape), axe...]
    all_to_all x4 -> x3, waiting for transfers between devices: 12.3 us -> 1.61 us  [spread(): lax.all_to_all(jnp.broadcast_to(value[None], (count,) + value.shape), axe...]
    pallas_call x4, Pallas kernels: 30.1 us -> 19.8 us  [apply_metric(): pl.pallas_call(functools.partial(apply_kernel, forward, prologue, len(ins...]
    all_to_all x1 -> x0, starting transfers between devices: 9.74 us -> none  [body(): lax.all_to_all(mixed, ('x', 'z', 'core'), 0, 0, tiled=True)]
    convert_element_type x1 -> x0, local copies, waits for them, and re-layouts: 9.46 us -> none  [body(): choose = lambda c: jnp.einsum('je,iek->ikj', lax.dynamic_index_in_dim(pic...]
    ppermute x8 -> x12, waiting for transfers between devices: 9.43 us -> 16.8 us  [the longest x8 12.4 us: ring(): return lax.ppermute(value, 'z', [(i, (i + step) % NZ) for i in range(NZ)])]
  transfers between devices with their start and end apart: 24 -> 24, of which waited for: 23 -> 16; matrix products, arithmetic and copies ran while one was open for 11% -> 4% of each run, Pallas kernels for 0% -> 7%
where the time goes in v3:
time: 196 us
  starting transfers between devices  58.7 us (30%)
  Pallas kernels  50 us (26%)
  blocking collectives  47.2 us (24%)
  waiting for transfers between devices  25.1 us (13%)
  local copies, waits for them, and re-layouts  7.41 us (4%)
  matrix products  5.85 us (3%)
    all_to_all x2, blocking collectives, spread(): lax.all_to_all(jnp.broadcast_to(value[None], (count,) + value.shape), axe...  29.4 us
    pallas_call x2, Pallas kernels, build_metric(): pl.pallas_call(functools.partial(metric_kernel, len(blocks), before is no...  28.4 us
    ppermute x9, starting transfers between devices, swap(): return lax.ppermute(value, 'core', [(0, 1), (1, 0)])  26.3 us
    pallas_call x4, Pallas kernels, apply_metric(): pl.pallas_call(functools.partial(apply_kernel, forward, prologue, len(ins...  19.8 us
    all_to_all x1, blocking collectives, body(): lax.all_to_all(mixed, ('x', 'z', 'core'), 0, 0, tiled=True)  17.7 us
    ppermute x8, waiting for transfers between devices, ring(): return lax.ppermute(value, 'z', [(i, (i + step) % NZ) for i in range(NZ)])  12.4 us
    all_to_all x3, starting transfers between devices, spread(): lax.all_to_all(jnp.broadcast_to(value[None], (count,) + value.shape), axe...  11.9 us
    ppermute x8, starting transfers between devices, ring(): return lax.ppermute(value, 'z', [(i, (i + step) % NZ) for i in range(NZ)])  11.7 us
  transfers between devices with their start and end apart: 24, of which 16 were waited for; matrix products, arithmetic and copies ran while one was open for 4% of the time, Pallas kernels for 7%

profile of v3, /device:TPU:1, one launch (start us, length us, event | category | flops | bytes accessed | tf_op | source)
XLA Modules:
  0.0 195.8 jit_solution(12786181956716530890)
XLA Ops:
  2.8 3.3 %collective-permute-start = (bf16[7,4,4,256]{3,2,1,0:T(4,128)(2,1)S(1)}, bf16[7,4,4,256]{3,2,1,0:T(4,128)(2,1)S(1)}, u32[]{:S(2)}, u32[]{:S(2)}) collective-permute-start(bf16[7,4,4,256]{3,2,1,0:T(4,128)(2,1)S(1)} %dynamic-slice_bitcast_fusion), channel_id=1, source_target_pairs={{0,4},{4,0},{1,5},{5,1},{2,6},{6,2},{3,7},{7,3},{8,12},{12,8},{9,1... | collective-permute-start | bytes 172040 | tf_op jit(solution)/shard_map/ppermute | solution.py:364
  8.1 3.5 %all-to-all-start = ((bf16[4,448,128]{2,1,0:T(8,128)(2,1)}), bf16[4,448,128]{2,1,0:T(8,128)(2,1)S(1)}, u32[]{:S(2)}, u32[]{:S(2)}) async-start(bf16[4,448,128]{2,1,0:T(8,128)(2,1)} %broadcast_in_dim.13), calls=%async_computation | async-start | bytes 917504 | tf_op jit(solution)/shard_map/all_to_all | solution.py:360
  11.5 4.0 %fusion.1 = bf16[4,2401,256]{2,1,0:T(8,128)(2,1)S(1)} fusion(bf16[4,256,2401]{1,0,2:T(4,128)(2,1)} %bitcast.60, s32[256]{0:T(256)S(1)} %fusion.18), kind=kOutput, calls=%fused_computation.2 | convolution fusion | flops 1261339648 | bytes 9835520 | tf_op jit(solution)/shard_map/je,iek->ikj/dot_general | solution.py:419
  15.5 2.5 %pad.13.refs_4_.refs_5_ = bf16[4,2432,256]{2,1,0:T(8,128)(2,1)} pad(bf16[4,2401,256]{2,1,0:T(8,128)(2,1)S(1)} %fusion.1, bf16[]{:T(256)} %constant.88.clone.1), padding=0_0x0_31x0_0 | pad | bytes 9897986 | tf_op jit(solution)/shard_map/jit(_pad)/pad | solution.py:420
  18.4 1.6 all-to-all-done
  22.0 3.9 %collective-permute-start.2 = (bf16[28,32,256]{2,1,0:T(8,128)(2,1)S(1)}, bf16[28,32,256]{2,1,0:T(8,128)(2,1)}, u32[]{:S(2)}, u32[]{:S(2)}) collective-permute-start(bf16[28,32,256]{2,1,0:T(8,128)(2,1)S(1)} %copy_bitcast_fusion.refs_0_), channel_id=1, source_target_pairs={{0,56},{8,0},{16,8},{24,16},{32,24},{40,32},{48,40},{56,48},{1,57}... | collective-permute-start | bytes 1376264 | tf_op jit(solution)/shard_map/ppermute | solution.py:398
  26.4 17.7 %all_to_all.30 = bf16[64,2,392]{2,1,0:T(2,128)(2,1)S(1)} all-to-all(bf16[64,2,392]{2,1,0:T(2,128)(2,1)S(1)} %reshape.187), channel_id=1, replica_groups=mesh['x'=4,'z'=8,'core'=2,'site'=4] {'x','z','core'}, dimensions={0} | all-to-all | bytes 200704 | tf_op jit(solution)/shard_map/all_to_all | solution.py:431
  45.4 1.8 collective-permute-start.3
  49.5 7.9 %collective-permute-done.5.refs_3_ = bf16[28,32,256]{2,1,0:T(8,128)(2,1)S(1)} collective-permute-done((bf16[28,32,256]{2,1,0:T(8,128)(2,1)S(1)}, bf16[28,32,256]{2,1,0:T(8,128)(2,1)S(1)}, u32[]{:S(2)}, u32[]{:S(2)}) %collective-permute-start.5) | collective-permute-done | bytes 458784 | tf_op jit(solution)/shard_map/ppermute | solution.py:398
  57.4 2.9 %collective-permute-start.7 = (bf16[28,32,256]{2,1,0:T(8,128)(2,1)S(1)}, bf16[28,32,256]{2,1,0:T(8,128)(2,1)S(1)}, u32[]{:S(2)}, u32[]{:S(2)}) collective-permute-start(bf16[28,32,256]{2,1,0:T(8,128)(2,1)S(1)} %collective-permute-done.3.refs_0_), channel_id=1, source_target_pairs={{0,56},{8,0},{16,8},{24,16},{32,24},{40,32},{48,40},{56,48},{1,57}... | collective-permute-start | bytes 1376264 | tf_op jit(solution)/shard_map/ppermute | solution.py:398
  60.3 13.7 %build_first.1.refs_7_ = bf16[7,224,2432]{2,1,0:T(8,128)(2,1)} custom-call(bf16[448,256]{1,0:T(8,128)(2,1)S(1)} %pad_maximum_fusion.mixed_ref, bf16[28,32,256]{2,1,0:T(8,128)(2,1)} %copy-done.7, bf16[28,32,256]{2,1,0:T(8,128)(2,1)} %copy-done.16, bf16[28,32,256]{2,1,0:T(8,128)(2,1)} %collective-permute-done.2.refs_2_, bf16[28,32,256]{2,1,0:T(8,128)(2,1)} %copy-done.17, ...), custom_call_target="tpu_custom_call" | custom-call | flops 8000000000 | bytes 22000000 | tf_op jit(solution)/shard_map/build_first/pallas_call | solution.py:137
  74.2 1.5 collective-permute-start.9
  76.3 3.2 %collective-permute-done.10.refs_4_ = bf16[14,32,256]{2,1,0:T(8,128)(2,1)} collective-permute-done((bf16[14,32,256]{2,1,0:T(8,128)(2,1)S(1)}, bf16[14,32,256]{2,1,0:T(8,128)(2,1)}, u32[]{:S(2)}, u32[]{:S(2)}) %collective-permute-start.10) | collective-permute-done | bytes 229408 | tf_op jit(solution)/shard_map/ppermute | solution.py:398
  80.9 14.7 %build_second.1.refs_0_ = bf16[7,224,2432]{2,1,0:T(8,128)(2,1)} custom-call(bf16[448,256]{1,0:T(8,128)(2,1)S(1)} %pad_maximum_fusion.mixed_ref, bf16[28,32,256]{2,1,0:T(8,128)(2,1)} %copy-done.15, bf16[28,32,256]{2,1,0:T(8,128)(2,1)} %copy-done.10, bf16[28,32,256]{2,1,0:T(8,128)(2,1)} %copy-done.11, bf16[14,32,256]{2,1,0:T(8,128)(2,1)} %collective-permute-done.9.refs_3_, ...), custom_call_target="tpu_custom_call" | custom-call | flops 8000000000 | bytes 22000000 | tf_op jit(solution)/shard_map/build_second/pallas_call | solution.py:137
  95.6 4.6 %forward.2 = f32[32,128]{1,0:T(8,128)S(1)} custom-call(s32[1]{0:T(128)} %bitcast.core_ref, bf16[7,224,2432]{2,1,0:T(8,128)(2,1)} %build_second.1.refs_0_, bf16[128,2432]{1,0:T(8,128)(2,1)S(1)} %copy-done.1, bf16[2432,128]{1,0:T(8,128)(2,1)S(1)} %copy-done.5, bf16[112,784]{1,0:T(8,128)(2,1)S(1)} %copy-done.2, ...), custom_call_target="tpu_custom_call" | custom-call | flops 50000000 | bytes 8000000 | tf_op jit(solution)/shard_map/forward/pallas_call | solution.py:249
  100.3 13.1 %all_to_all.31 = bf16[32,32,128]{2,1,0:T(8,128)(2,1)S(1)} all-to-all(bf16[32,32,128]{2,1,0:T(8,128)(2,1)S(1)} %broadcast_in_dim.14), channel_id=1, replica_groups=mesh['x'=4,'z'=8,'core'=2,'site'=4] {'x','z'}, dimensions={0} | all-to-all | bytes 524288 | tf_op jit(solution)/shard_map/all_to_all | solution.py:360
  113.4 5.3 %backward.2 = (f32[2,128]{1,0:T(2,128)S(1)}, f32[32,128]{1,0:T(8,128)S(1)}, f32[32,128]{1,0:T(8,128)S(1)}) custom-call(s32[1]{0:T(128)} %bitcast.core_ref, bf16[7,224,2432]{2,1,0:T(8,128)(2,1)} %build_second.1.refs_0_, bf16[128,2432]{1,0:T(8,128)(2,1)S(1)} %copy-done.3, bf16[2432,128]{1,0:T(8,128)(2,1)S(1)} %copy-done.4, bf16[112,784]{1,0:T(8,128)(2,1)S(1)} %copy-done.2, ...), custom_call_target="tpu_custom_call" | custom-call | flops 50000000 | bytes 8000000 | tf_op jit(solution)/shard_map/backward/pallas_call | solution.py:249
  118.8 4.8 %collective-permute-start.11 = (f32[32,128]{1,0:T(8,128)S(1)}, f32[32,128]{1,0:T(8,128)S(1)}, u32[]{:S(2)}, u32[]{:S(2)}) collective-permute-start(f32[32,128]{1,0:T(8,128)S(1)} %get-tuple-element.27), channel_id=1, source_target_pairs={{0,4},{4,0},{1,5},{5,1},{2,6},{6,2},{3,7},{7,3},{8,12},{12,8},{9,1... | collective-permute-start | bytes 49160 | tf_op jit(solution)/shard_map/ppermute | solution.py:364
  125.1 4.3 %all-to-all-start.3 = ((bf16[32,32,128]{2,1,0:T(8,128)(2,1)}), bf16[32,32,128]{2,1,0:T(8,128)(2,1)S(1)}, u32[]{:S(2)}, u32[]{:S(2)}) async-start(bf16[32,32,128]{2,1,0:T(8,128)(2,1)} %broadcast_in_dim.15), calls=%async_computation.3 | async-start | bytes 524288 | tf_op jit(solution)/shard_map/all_to_all | solution.py:360
  129.4 1.6 collective-permute-start.12
  132.2 2.9 %collective-permute-start.13 = (f32[2,128]{1,0:T(2,128)S(1)}, f32[2,128]{1,0:T(2,128)S(1)}, u32[]{:S(2)}, u32[]{:S(2)}) collective-permute-start(f32[2,128]{1,0:T(2,128)S(1)} %add.130), channel_id=1, source_target_pairs={{0,2},{1,3},{2,0},{3,1},{4,6},{5,7},{6,4},{7,5},{8,10},{9,11},{10,... | collective-permute-start | bytes 3080 | tf_op jit(solution)/shard_map/ppermute | solution.py:369
  136.1 2.9 %collective-permute-start.14 = (f32[2,128]{1,0:T(2,128)S(1)}, f32[2,128]{1,0:T(2,128)S(1)}, u32[]{:S(2)}, u32[]{:S(2)}) collective-permute-start(f32[2,128]{1,0:T(2,128)S(1)} %add.131), channel_id=1, source_target_pairs={{0,4},{4,0},{1,5},{5,1},{2,6},{6,2},{3,7},{7,3},{8,12},{12,8},{9,1... | collective-permute-start | bytes 3080 | tf_op jit(solution)/shard_map/ppermute | solution.py:364
  139.9 3.0 %collective-permute-start.15 = (f32[32,128]{1,0:T(8,128)S(1)}, f32[32,128]{1,0:T(8,128)S(1)}, u32[]{:S(2)}, u32[]{:S(2)}) collective-permute-start(f32[32,128]{1,0:T(8,128)S(1)} %convert_reduce_fusion.2.refs_4_.half_0_ref), channel_id=1, source_target_pairs={{0,4},{4,0},{1,5},{5,1},{2,6},{6,2},{3,7},{7,3},{8,12},{12,8},{9,1... | collective-permute-start | bytes 49160 | tf_op jit(solution)/shard_map/ppermute | solution.py:364
  143.8 4.5 %forward.3 = (f32[2,32,128]{2,1,0:T(8,128)S(1)}, f32[32,128]{1,0:T(8,128)S(1)}) custom-call(s32[1]{0:T(128)} %bitcast.core_ref, bf16[7,224,2432]{2,1,0:T(8,128)(2,1)} %build_second.1.refs_0_, bf16[128,2432]{1,0:T(8,128)(2,1)S(1)} %copy-done.1, bf16[2432,128]{1,0:T(8,128)(2,1)S(1)} %copy-done.5, bf16[112,784]{1,0:T(8,128)(2,1)S(1)} %copy-done.2, ...), custom_call_target="tpu_custom_call" | custom-call | flops 50000000 | bytes 8000000 | tf_op jit(solution)/shard_map/forward/pallas_call | solution.py:249
  148.4 16.4 %all_to_all.32 = bf16[32,32,128]{2,1,0:T(8,128)(2,1)S(1)} all-to-all(bf16[32,32,128]{2,1,0:T(8,128)(2,1)S(1)} %broadcast_in_dim.16), channel_id=1, replica_groups=mesh['x'=4,'z'=8,'core'=2,'site'=4] {'x','z'}, dimensions={0} | all-to-all | bytes 524288 | tf_op jit(solution)/shard_map/all_to_all | solution.py:360
  164.8 5.4 %backward.3 = (f32[3,128]{1,0:T(4,128)S(1)}, f32[32,128]{1,0:T(8,128)S(1)}, f32[32,128]{1,0:T(8,128)S(1)}) custom-call(s32[1]{0:T(128)} %bitcast.core_ref, bf16[7,224,2432]{2,1,0:T(8,128)(2,1)} %build_second.1.refs_0_, bf16[128,2432]{1,0:T(8,128)(2,1)S(1)} %copy-done.3, bf16[2432,128]{1,0:T(8,128)(2,1)S(1)} %copy-done.4, bf16[112,784]{1,0:T(8,128)(2,1)S(1)} %copy-done.2, ...), custom_call_target="tpu_custom_call" | custom-call | flops 50000000 | bytes 8000000 | tf_op jit(solution)/shard_map/backward/pallas_call | solution.py:249
  170.1 3.8 %collective-permute-start.16 = (f32[32,128]{1,0:T(8,128)S(1)}, f32[32,128]{1,0:T(8,128)S(1)}, u32[]{:S(2)}, u32[]{:S(2)}) collective-permute-start(f32[32,128]{1,0:T(8,128)S(1)} %get-tuple-element.34), channel_id=1, source_target_pairs={{0,4},{4,0},{1,5},{5,1},{2,6},{6,2},{3,7},{7,3},{8,12},{12,8},{9,1... | collective-permute-start | bytes 49160 | tf_op jit(solution)/shard_map/ppermute | solution.py:364
  175.5 4.2 %all-to-all-start.5 = ((bf16[32,32,128]{2,1,0:T(8,128)(2,1)}), bf16[32,32,128]{2,1,0:T(8,128)(2,1)S(1)}, u32[]{:S(2)}, u32[]{:S(2)}) async-start(bf16[32,32,128]{2,1,0:T(8,128)(2,1)} %broadcast_in_dim.17), calls=%async_computation.5 | async-start | bytes 524288 | tf_op jit(solution)/shard_map/all_to_all | solution.py:360
  182.2 2.9 %collective-permute-start.18 = (f32[3,128]{1,0:T(4,128)S(1)}, f32[3,128]{1,0:T(4,128)S(1)}, u32[]{:S(2)}, u32[]{:S(2)}) collective-permute-start(f32[3,128]{1,0:T(4,128)S(1)} %add.134), channel_id=1, source_target_pairs={{0,2},{1,3},{2,0},{3,1},{4,6},{5,7},{6,4},{7,5},{8,10},{9,11},{10,... | collective-permute-start | bytes 4616 | tf_op jit(solution)/shard_map/ppermute | solution.py:369
  186.1 2.9 %collective-permute-start.19 = (f32[3,128]{1,0:T(4,128)S(1)}, f32[3,128]{1,0:T(4,128)S(1)}, u32[]{:S(2)}, u32[]{:S(2)}) collective-permute-start(f32[3,128]{1,0:T(4,128)S(1)} %add.135), channel_id=1, source_target_pairs={{0,4},{4,0},{1,5},{5,1},{2,6},{6,2},{3,7},{7,3},{8,12},{12,8},{9,1... | collective-permute-start | bytes 4616 | tf_op jit(solution)/shard_map/ppermute | solution.py:364
  189.9 3.2 %collective-permute-start.20 = (f32[32,128]{1,0:T(8,128)S(1)}, f32[32,128]{1,0:T(8,128)S(1)}, u32[]{:S(2)}, u32[]{:S(2)}) collective-permute-start(f32[32,128]{1,0:T(8,128)S(1)} %convert_reduce_fusion.half_1_ref), channel_id=1, source_target_pairs={{0,4},{4,0},{1,5},{5,1},{2,6},{6,2},{3,7},{7,3},{8,12},{12,8},{9,1... | collective-permute-start | bytes 49160 | tf_op jit(solution)/shard_map/ppermute | solution.py:364
  194.0 1.8 finish.1
  (109 shorter events, 25.0 us)
Async XLA Ops:
  2.8 4.2 %collective-permute-start = (bf16[7,4,4,256]{3,2,1,0:T(4,128)(2,1)S(1)}, bf16[7,4,4,256]{3,2,1,0:T(4,128)(2,1)S(1)}, u32[]{:S(2)}, u32[]{:S(2)}) collective-permute-start(bf16[7,4,4,256]{3,2,1,0:T(4,128)(2,1)S(1)} %dynamic-slice_bitcast_fusion), channel_id=1, source_target_pairs={{0,4},{4,0},{1,5},{5,1},{2,6},{6,2},{3,7},{7,3},{8,12},{12,8},{9,1... | collective-permute-start | bytes 172040 | tf_op jit(solution)/shard_map/ppermute | solution.py:364
  8.1 12.0 %all-to-all-start = ((bf16[4,448,128]{2,1,0:T(8,128)(2,1)}), bf16[4,448,128]{2,1,0:T(8,128)(2,1)S(1)}, u32[]{:S(2)}, u32[]{:S(2)}) async-start(bf16[4,448,128]{2,1,0:T(8,128)(2,1)} %broadcast_in_dim.13), calls=%async_computation | async-start | bytes 917504 | tf_op jit(solution)/shard_map/all_to_all | solution.py:360
  15.5 31.6 %copy-start.14 = (bf16[56,49,1]{1,0,2:T(8,128)(2,1)S(1)}, bf16[56,49,1]{1,0,2:T(8,128)(2,1)}, u32[]{:S(2)}) copy-start(bf16[56,49,1]{1,0,2:T(8,128)(2,1)} %constant.148) | copy-start | bytes 16468
  20.3 40.1 %copy-start.7 = (bf16[28,32,256]{2,1,0:T(8,128)(2,1)}, bf16[28,32,256]{2,1,0:T(8,128)(2,1)S(1)}, u32[]{:S(2)}) copy-start(bf16[28,32,256]{2,1,0:T(8,128)(2,1)S(1)} %copy_bitcast_fusion.refs_0_) | copy-start | bytes 1376260
  20.3 40.1 %collective-permute-start.8 = (bf16[4,2432,256]{2,1,0:T(8,128)(2,1)}, bf16[4,2432,256]{2,1,0:T(8,128)(2,1)}, u32[]{:S(2)}, u32[]{:S(2)}) collective-permute-start(bf16[4,2432,256]{2,1,0:T(8,128)(2,1)} %pad.13.refs_4_.refs_5_), channel_id=1, source_target_pairs={{0,4},{4,0},{1,5},{5,1},{2,6},{6,2},{3,7},{7,3},{8,12},{12,8},{9,1... | collective-permute-start | bytes 14942216 | tf_op jit(solution)/shard_map/ppermute | solution.py:364
  21.5 22.8 %collective-permute-start.4 = (bf16[28,32,256]{2,1,0:T(8,128)(2,1)S(1)}, bf16[28,32,256]{2,1,0:T(8,128)(2,1)S(1)}, u32[]{:S(2)}, u32[]{:S(2)}) collective-permute-start(bf16[28,32,256]{2,1,0:T(8,128)(2,1)S(1)} %copy_bitcast_fusion.refs_0_), channel_id=1, source_target_pairs={{0,8},{8,16},{16,24},{24,32},{32,40},{40,48},{48,56},{56,0},{1,9},... | collective-permute-start | bytes 1376264 | tf_op jit(solution)/shard_map/ppermute | solution.py:398
  22.0 23.4 %collective-permute-start.2 = (bf16[28,32,256]{2,1,0:T(8,128)(2,1)S(1)}, bf16[28,32,256]{2,1,0:T(8,128)(2,1)}, u32[]{:S(2)}, u32[]{:S(2)}) collective-permute-start(bf16[28,32,256]{2,1,0:T(8,128)(2,1)S(1)} %copy_bitcast_fusion.refs_0_), channel_id=1, source_target_pairs={{0,56},{8,0},{16,8},{24,16},{32,24},{40,32},{48,40},{56,48},{1,57}... | collective-permute-start | bytes 1376264 | tf_op jit(solution)/shard_map/ppermute | solution.py:398
  44.4 13.0 %collective-permute-start.5 = (bf16[28,32,256]{2,1,0:T(8,128)(2,1)S(1)}, bf16[28,32,256]{2,1,0:T(8,128)(2,1)S(1)}, u32[]{:S(2)}, u32[]{:S(2)}) collective-permute-start(bf16[28,32,256]{2,1,0:T(8,128)(2,1)S(1)} %collective-permute-done.4.refs_1_), channel_id=1, source_target_pairs={{0,8},{8,16},{16,24},{24,32},{32,40},{40,48},{48,56},{56,0},{1,9},... | collective-permute-start | bytes 1376264 | tf_op jit(solution)/shard_map/ppermute | solution.py:398
  45.4 12.0 %collective-permute-start.3 = (bf16[28,32,256]{2,1,0:T(8,128)(2,1)}, bf16[28,32,256]{2,1,0:T(8,128)(2,1)S(1)}, u32[]{:S(2)}, u32[]{:S(2)}) collective-permute-start(bf16[28,32,256]{2,1,0:T(8,128)(2,1)} %collective-permute-done.2.refs_2_), channel_id=1, source_target_pairs={{0,56},{8,0},{16,8},{24,16},{32,24},{40,32},{48,40},{56,48},{1,57}... | collective-permute-start | bytes 1376264 | tf_op jit(solution)/shard_map/ppermute | solution.py:398
  47.4 2.0 %collective-permute-start.1 = (bf16[224,256]{1,0:T(8,128)(2,1)S(1)}, bf16[224,256]{1,0:T(8,128)(2,1)S(1)}, u32[]{:S(2)}, u32[]{:S(2)}) collective-permute-start(bf16[224,256]{1,0:T(8,128)(2,1)S(1)} %bitcast.65), channel_id=1, source_target_pairs={{0,4},{4,0},{1,5},{5,1},{2,6},{6,2},{3,7},{7,3},{8,12},{12,8},{9,1... | collective-permute-start | bytes 344072 | tf_op jit(solution)/shard_map/ppermute | solution.py:364
  49.4 26.2 %copy-start.13 = (f32[1,2,2401]{2,1,0:T(2,128)S(1)}, f32[1,2,2401]{2,1,0:T(2,128)}, u32[]{:S(2)}) copy-start(f32[1,2,2401]{2,1,0:T(2,128)} %param.18) | copy-start | bytes 57628
  49.5 26.4 %copy-start.12 = (f32[2,32,49,1]{2,1,3,0:T(8,128)S(1)}, f32[2,32,49,1]{2,1,3,0:T(8,128)}, u32[]{:S(2)}) copy-start(f32[2,32,49,1]{2,1,3,0:T(8,128)} %constant.149) | copy-start | bytes 37636
  57.4 16.6 %collective-permute-start.6 = (bf16[28,32,256]{2,1,0:T(8,128)(2,1)S(1)}, bf16[28,32,256]{2,1,0:T(8,128)(2,1)S(1)}, u32[]{:S(2)}, u32[]{:S(2)}) collective-permute-start(bf16[28,32,256]{2,1,0:T(8,128)(2,1)S(1)} %collective-permute-done.5.refs_3_), channel_id=1, source_target_pairs={{0,8},{8,16},{16,24},{24,32},{32,40},{40,48},{48,56},{56,0},{1,9},... | collective-permute-start | bytes 1376264 | tf_op jit(solution)/shard_map/ppermute | solution.py:398
  57.4 16.6 %collective-permute-start.7 = (bf16[28,32,256]{2,1,0:T(8,128)(2,1)S(1)}, bf16[28,32,256]{2,1,0:T(8,128)(2,1)S(1)}, u32[]{:S(2)}, u32[]{:S(2)}) collective-permute-start(bf16[28,32,256]{2,1,0:T(8,128)(2,1)S(1)} %collective-permute-done.3.refs_0_), channel_id=1, source_target_pairs={{0,56},{8,0},{16,8},{24,16},{32,24},{40,32},{48,40},{56,48},{1,57}... | collective-permute-start | bytes 1376264 | tf_op jit(solution)/shard_map/ppermute | solution.py:398
  74.0 5.5 %collective-permute-start.10 = (bf16[14,32,256]{2,1,0:T(8,128)(2,1)S(1)}, bf16[14,32,256]{2,1,0:T(8,128)(2,1)}, u32[]{:S(2)}, u32[]{:S(2)}) collective-permute-start(bf16[14,32,256]{2,1,0:T(8,128)(2,1)S(1)} %slice.7), channel_id=1, source_target_pairs={{0,56},{8,0},{16,8},{24,16},{32,24},{40,32},{48,40},{56,48},{1,57}... | collective-permute-start | bytes 688136 | tf_op jit(solution)/shard_map/ppermute | solution.py:398
  74.2 6.7 %collective-permute-start.9 = (bf16[14,32,256]{2,1,0:T(8,128)(2,1)S(1)}, bf16[14,32,256]{2,1,0:T(8,128)(2,1)}, u32[]{:S(2)}, u32[]{:S(2)}) collective-permute-start(bf16[14,32,256]{2,1,0:T(8,128)(2,1)S(1)} %slice.6), channel_id=1, source_target_pairs={{0,8},{8,16},{16,24},{24,32},{32,40},{40,48},{48,56},{56,0},{1,9},... | collective-permute-start | bytes 688136 | tf_op jit(solution)/shard_map/ppermute | solution.py:398
  76.3 19.3 %copy-start.1 = (bf16[128,2432]{1,0:T(8,128)(2,1)S(1)}, bf16[128,2432]{1,0:T(8,128)(2,1)}, u32[]{:S(2)}) copy-start(bf16[128,2432]{1,0:T(8,128)(2,1)} %constant.104.clone.refs_1_.expand_ref) | copy-start | bytes 1867780
  76.3 19.3 %copy-start.2 = (bf16[112,784]{1,0:T(8,128)(2,1)S(1)}, bf16[112,784]{1,0:T(8,128)(2,1)}, u32[]{:S(2)}) copy-start(bf16[112,784]{1,0:T(8,128)(2,1)} %constant.106.clone.refs_3_) | copy-start | bytes 526852
  76.3 19.3 %copy-start.5 = (bf16[2432,128]{1,0:T(8,128)(2,1)S(1)}, bf16[2432,128]{1,0:T(8,128)(2,1)}, u32[]{:S(2)}) copy-start(bf16[2432,128]{1,0:T(8,128)(2,1)} %constant.121.refs_2_) | copy-start | bytes 1867780
  118.8 5.6 %collective-permute-start.11 = (f32[32,128]{1,0:T(8,128)S(1)}, f32[32,128]{1,0:T(8,128)S(1)}, u32[]{:S(2)}, u32[]{:S(2)}) collective-permute-start(f32[32,128]{1,0:T(8,128)S(1)} %get-tuple-element.27), channel_id=1, source_target_pairs={{0,4},{4,0},{1,5},{5,1},{2,6},{6,2},{3,7},{7,3},{8,12},{12,8},{9,1... | collective-permute-start | bytes 49160 | tf_op jit(solution)/shard_map/ppermute | solution.py:364
  125.1 14.7 %all-to-all-start.3 = ((bf16[32,32,128]{2,1,0:T(8,128)(2,1)}), bf16[32,32,128]{2,1,0:T(8,128)(2,1)S(1)}, u32[]{:S(2)}, u32[]{:S(2)}) async-start(bf16[32,32,128]{2,1,0:T(8,128)(2,1)} %broadcast_in_dim.15), calls=%async_computation.3 | async-start | bytes 524288 | tf_op jit(solution)/shard_map/all_to_all | solution.py:360
  129.4 2.7 %collective-permute-start.12 = (f32[2,128]{1,0:T(2,128)S(1)}, f32[2,128]{1,0:T(2,128)S(1)}, u32[]{:S(2)}, u32[]{:S(2)}) collective-permute-start(f32[2,128]{1,0:T(2,128)S(1)} %get-tuple-element.28), channel_id=1, source_target_pairs={{0,1},{1,0},{2,3},{3,2},{4,5},{5,4},{6,7},{7,6},{8,9},{9,8},{10,11... | collective-permute-start | bytes 3080 | tf_op jit(solution)/shard_map/ppermute | solution.py:369
  132.2 3.9 %collective-permute-start.13 = (f32[2,128]{1,0:T(2,128)S(1)}, f32[2,128]{1,0:T(2,128)S(1)}, u32[]{:S(2)}, u32[]{:S(2)}) collective-permute-start(f32[2,128]{1,0:T(2,128)S(1)} %add.130), channel_id=1, source_target_pairs={{0,2},{1,3},{2,0},{3,1},{4,6},{5,7},{6,4},{7,5},{8,10},{9,11},{10,... | collective-permute-start | bytes 3080 | tf_op jit(solution)/shard_map/ppermute | solution.py:369
  136.1 3.7 %collective-permute-start.14 = (f32[2,128]{1,0:T(2,128)S(1)}, f32[2,128]{1,0:T(2,128)S(1)}, u32[]{:S(2)}, u32[]{:S(2)}) collective-permute-start(f32[2,128]{1,0:T(2,128)S(1)} %add.131), channel_id=1, source_target_pairs={{0,4},{4,0},{1,5},{5,1},{2,6},{6,2},{3,7},{7,3},{8,12},{12,8},{9,1... | collective-permute-start | bytes 3080 | tf_op jit(solution)/shard_map/ppermute | solution.py:364
  139.9 3.9 %collective-permute-start.15 = (f32[32,128]{1,0:T(8,128)S(1)}, f32[32,128]{1,0:T(8,128)S(1)}, u32[]{:S(2)}, u32[]{:S(2)}) collective-permute-start(f32[32,128]{1,0:T(8,128)S(1)} %convert_reduce_fusion.2.refs_4_.half_0_ref), channel_id=1, source_target_pairs={{0,4},{4,0},{1,5},{5,1},{2,6},{6,2},{3,7},{7,3},{8,12},{12,8},{9,1... | collective-permute-start | bytes 49160 | tf_op jit(solution)/shard_map/ppermute | solution.py:364
  164.8 29.2 %copy-start.6 = (bf16[56,2432]{1,0:T(8,128)(2,1)S(1)}, bf16[56,2432]{1,0:T(8,128)(2,1)}, u32[]{:S(2)}) copy-start(bf16[56,2432]{1,0:T(8,128)(2,1)} %constant.107.clone.own_lane_ref) | copy-start | bytes 817156
  170.1 4.6 %collective-permute-start.16 = (f32[32,128]{1,0:T(8,128)S(1)}, f32[32,128]{1,0:T(8,128)S(1)}, u32[]{:S(2)}, u32[]{:S(2)}) collective-permute-start(f32[32,128]{1,0:T(8,128)S(1)} %get-tuple-element.34), channel_id=1, source_target_pairs={{0,4},{4,0},{1,5},{5,1},{2,6},{6,2},{3,7},{7,3},{8,12},{12,8},{9,1... | collective-permute-start | bytes 49160 | tf_op jit(solution)/shard_map/ppermute | solution.py:364
  175.5 14.4 %all-to-all-start.5 = ((bf16[32,32,128]{2,1,0:T(8,128)(2,1)}), bf16[32,32,128]{2,1,0:T(8,128)(2,1)S(1)}, u32[]{:S(2)}, u32[]{:S(2)}) async-start(bf16[32,32,128]{2,1,0:T(8,128)(2,1)} %broadcast_in_dim.17), calls=%async_computation.5 | async-start | bytes 524288 | tf_op jit(solution)/shard_map/all_to_all | solution.py:360
  179.7 2.5 %collective-permute-start.17 = (f32[3,128]{1,0:T(4,128)S(1)}, f32[3,128]{1,0:T(4,128)S(1)}, u32[]{:S(2)}, u32[]{:S(2)}) collective-permute-start(f32[3,128]{1,0:T(4,128)S(1)} %get-tuple-element.35), channel_id=1, source_target_pairs={{0,1},{1,0},{2,3},{3,2},{4,5},{5,4},{6,7},{7,6},{8,9},{9,8},{10,11... | collective-permute-start | bytes 4616 | tf_op jit(solution)/shard_map/ppermute | solution.py:369
  182.2 3.9 %collective-permute-start.18 = (f32[3,128]{1,0:T(4,128)S(1)}, f32[3,128]{1,0:T(4,128)S(1)}, u32[]{:S(2)}, u32[]{:S(2)}) collective-permute-start(f32[3,128]{1,0:T(4,128)S(1)} %add.134), channel_id=1, source_target_pairs={{0,2},{1,3},{2,0},{3,1},{4,6},{5,7},{6,4},{7,5},{8,10},{9,11},{10,... | collective-permute-start | bytes 4616 | tf_op jit(solution)/shard_map/ppermute | solution.py:369
  186.1 3.7 %collective-permute-start.19 = (f32[3,128]{1,0:T(4,128)S(1)}, f32[3,128]{1,0:T(4,128)S(1)}, u32[]{:S(2)}, u32[]{:S(2)}) collective-permute-start(f32[3,128]{1,0:T(4,128)S(1)} %add.135), channel_id=1, source_target_pairs={{0,4},{4,0},{1,5},{5,1},{2,6},{6,2},{3,7},{7,3},{8,12},{12,8},{9,1... | collective-permute-start | bytes 4616 | tf_op jit(solution)/shard_map/ppermute | solution.py:364
  189.9 4.1 %collective-permute-start.20 = (f32[32,128]{1,0:T(8,128)S(1)}, f32[32,128]{1,0:T(8,128)S(1)}, u32[]{:S(2)}, u32[]{:S(2)}) collective-permute-start(f32[32,128]{1,0:T(8,128)S(1)} %convert_reduce_fusion.half_1_ref), channel_id=1, source_target_pairs={{0,4},{4,0},{1,5},{5,1},{2,6},{6,2},{3,7},{7,3},{8,12},{12,8},{9,1... | collective-permute-start | bytes 49160 | tf_op jit(solution)/shard_map/ppermute | solution.py:364
  (10 other events, 87.9 us)

commit v4 on v3

--- a/solution.py
+++ b/solution.py
@@ -365,17 +365,16 @@
 
 
 def sum_sites(lanes):
-    for step in (1, 2):
-        lanes = lanes + lax.ppermute(lanes, "site", [(i, i ^ step) for i in range(NSITE)])
-    return lanes
+    others = [lax.ppermute(lanes, "site", [(i, i ^ step) for i in range(NSITE)]) for step in (1, 2, 3)]
+    return lanes + others[0] + others[1] + others[2]
 
 
 def sum_chips(value, lanes=None, cores=False):
     parts = spread(value.astype(BF), ("x", "z"), CHIPS)
     if lanes is not None:
-        lanes = sum_sites(lanes)
         if cores:
             lanes = lanes + swap(lanes)
+        lanes = sum_sites(lanes)
         parts, lanes = lax.optimization_barrier((parts, lanes))
     return jnp.sum(parts.astype(F32), axis=0), lanes
 

time: 196 us -> 197 us (level)
  waiting for transfers between devices: 25.1 us -> 29.1 us
  starting transfers between devices: 58.7 us -> 54.8 us
    all_to_all x3, waiting for transfers between devices: 1.61 us -> 4.69 us  [spread(): lax.all_to_all(jnp.broadcast_to(value[None], (count,) + value.shape), axe...]
    ppermute x9, starting transfers between devices: 26.3 us -> 23.4 us  [swap(): return lax.ppermute(value, 'core', [(0, 1), (1, 0)])]
    ppermute x4 -> x6, starting transfers between devices: 8.8 us -> 7.77 us  [sum_sites(): lax.ppermute(lanes, 'site', [(i, i ^ step) for i in range(NSITE)])]
    ppermute x4 -> x6, waiting for transfers between devices: 4.31 us -> 5.19 us  [sum_sites(): lax.ppermute(lanes, 'site', [(i, i ^ step) for i in range(NSITE)])]
  transfers between devices with their start and end apart: 24 -> 26, of which waited for: 16 -> 18; matrix products, arithmetic and copies ran while one was open for 4% -> 4% of each run, Pallas kernels for 7% -> 7%
where the time goes in v4:
time: 197 us; the launch traced here: 196 us
  starting transfers between devices  54.8 us (28%)
  Pallas kernels  50 us (25%)
  blocking collectives  47.8 us (24%)
  waiting for transfers between devices  29.1 us (15%)
  local copies, waits for them, and re-layouts  7.4 us (4%)
  matrix products  5.85 us (3%)
    all_to_all x2, blocking collectives, spread(): lax.all_to_all(jnp.broadcast_to(value[None], (count,) + value.shape), axe...  30 us
    pallas_call x2, Pallas kernels, build_metric(): pl.pallas_call(functools.partial(metric_kernel, len(blocks), before is no...  28.4 us
    ppermute x9, starting transfers between devices, swap(): return lax.ppermute(value, 'core', [(0, 1), (1, 0)])  23.4 us
    pallas_call x4, Pallas kernels, apply_metric(): pl.pallas_call(functools.partial(apply_kernel, forward, prologue, len(ins...  19.8 us
    all_to_all x1, blocking collectives, body(): lax.all_to_all(mixed, ('x', 'z', 'core'), 0, 0, tiled=True)  17.7 us
    ppermute x8, waiting for transfers between devices, ring(): return lax.ppermute(value, 'z', [(i, (i + step) % NZ) for i in range(NZ)])  12.4 us
    all_to_all x3, starting transfers between devices, spread(): lax.all_to_all(jnp.broadcast_to(value[None], (count,) + value.shape), axe...  11.9 us
    ppermute x8, starting transfers between devices, ring(): return lax.ppermute(value, 'z', [(i, (i + step) % NZ) for i in range(NZ)])  11.7 us
  transfers between devices with their start and end apart: 26, of which 18 were waited for; matrix products, arithmetic and copies ran while one was open for 4% of the time, Pallas kernels for 7%

profile of v4, /device:TPU:1, one launch (start us, length us, event | category | flops | bytes accessed | tf_op | source)
XLA Modules:
  0.0 196.4 jit_solution(4699105028651357593)
XLA Ops:
  2.8 3.3 %collective-permute-start = (bf16[7,4,4,256]{3,2,1,0:T(4,128)(2,1)S(1)}, bf16[7,4,4,256]{3,2,1,0:T(4,128)(2,1)S(1)}, u32[]{:S(2)}, u32[]{:S(2)}) collective-permute-start(bf16[7,4,4,256]{3,2,1,0:T(4,128)(2,1)S(1)} %dynamic-slice_bitcast_fusion), channel_id=1, source_target_pairs={{0,4},{4,0},{1,5},{5,1},{2,6},{6,2},{3,7},{7,3},{8,12},{12,8},{9,1... | collective-permute-start | bytes 172040 | tf_op jit(solution)/shard_map/ppermute | solution.py:364
  8.0 3.5 %all-to-all-start = ((bf16[4,448,128]{2,1,0:T(8,128)(2,1)}), bf16[4,448,128]{2,1,0:T(8,128)(2,1)S(1)}, u32[]{:S(2)}, u32[]{:S(2)}) async-start(bf16[4,448,128]{2,1,0:T(8,128)(2,1)} %broadcast_in_dim.13), calls=%async_computation | async-start | bytes 917504 | tf_op jit(solution)/shard_map/all_to_all | solution.py:360
  11.5 4.0 %fusion.1 = bf16[4,2401,256]{2,1,0:T(8,128)(2,1)S(1)} fusion(bf16[4,256,2401]{1,0,2:T(4,128)(2,1)} %bitcast.60, s32[256]{0:T(256)S(1)} %fusion.18), kind=kOutput, calls=%fused_computation.2 | convolution fusion | flops 1261339648 | bytes 9835520 | tf_op jit(solution)/shard_map/je,iek->ikj/dot_general | solution.py:418
  15.5 2.5 %pad.13.refs_4_.refs_5_ = bf16[4,2432,256]{2,1,0:T(8,128)(2,1)} pad(bf16[4,2401,256]{2,1,0:T(8,128)(2,1)S(1)} %fusion.1, bf16[]{:T(256)} %constant.88.clone.1), padding=0_0x0_31x0_0 | pad | bytes 9897986 | tf_op jit(solution)/shard_map/jit(_pad)/pad | solution.py:419
  18.4 1.6 all-to-all-done
  22.0 3.9 %collective-permute-start.2 = (bf16[28,32,256]{2,1,0:T(8,128)(2,1)S(1)}, bf16[28,32,256]{2,1,0:T(8,128)(2,1)}, u32[]{:S(2)}, u32[]{:S(2)}) collective-permute-start(bf16[28,32,256]{2,1,0:T(8,128)(2,1)S(1)} %copy_bitcast_fusion.refs_0_), channel_id=1, source_target_pairs={{0,56},{8,0},{16,8},{24,16},{32,24},{40,32},{48,40},{56,48},{1,57}... | collective-permute-start | bytes 1376264 | tf_op jit(solution)/shard_map/ppermute | solution.py:397
  26.3 17.7 %all_to_all.30 = bf16[64,2,392]{2,1,0:T(2,128)(2,1)S(1)} all-to-all(bf16[64,2,392]{2,1,0:T(2,128)(2,1)S(1)} %reshape.187), channel_id=1, replica_groups=mesh['x'=4,'z'=8,'core'=2,'site'=4] {'x','z','core'}, dimensions={0} | all-to-all | bytes 200704 | tf_op jit(solution)/shard_map/all_to_all | solution.py:430
  45.4 1.8 collective-permute-start.3
  49.4 7.9 %collective-permute-done.5.refs_3_ = bf16[28,32,256]{2,1,0:T(8,128)(2,1)S(1)} collective-permute-done((bf16[28,32,256]{2,1,0:T(8,128)(2,1)S(1)}, bf16[28,32,256]{2,1,0:T(8,128)(2,1)S(1)}, u32[]{:S(2)}, u32[]{:S(2)}) %collective-permute-start.5) | collective-permute-done | bytes 458784 | tf_op jit(solution)/shard_map/ppermute | solution.py:397
  57.4 2.9 %collective-permute-start.7 = (bf16[28,32,256]{2,1,0:T(8,128)(2,1)S(1)}, bf16[28,32,256]{2,1,0:T(8,128)(2,1)S(1)}, u32[]{:S(2)}, u32[]{:S(2)}) collective-permute-start(bf16[28,32,256]{2,1,0:T(8,128)(2,1)S(1)} %collective-permute-done.3.refs_0_), channel_id=1, source_target_pairs={{0,56},{8,0},{16,8},{24,16},{32,24},{40,32},{48,40},{56,48},{1,57}... | collective-permute-start | bytes 1376264 | tf_op jit(solution)/shard_map/ppermute | solution.py:397
  60.3 13.7 %build_first.1.refs_7_ = bf16[7,224,2432]{2,1,0:T(8,128)(2,1)} custom-call(bf16[448,256]{1,0:T(8,128)(2,1)S(1)} %pad_maximum_fusion.mixed_ref, bf16[28,32,256]{2,1,0:T(8,128)(2,1)} %copy-done.7, bf16[28,32,256]{2,1,0:T(8,128)(2,1)} %copy-done.16, bf16[28,32,256]{2,1,0:T(8,128)(2,1)} %collective-permute-done.2.refs_2_, bf16[28,32,256]{2,1,0:T(8,128)(2,1)} %copy-done.17, ...), custom_call_target="tpu_custom_call" | custom-call | flops 8000000000 | bytes 22000000 | tf_op jit(solution)/shard_map/build_first/pallas_call | solution.py:137
  74.2 1.5 collective-permute-start.9
  76.4 3.2 %collective-permute-done.10.refs_4_ = bf16[14,32,256]{2,1,0:T(8,128)(2,1)} collective-permute-done((bf16[14,32,256]{2,1,0:T(8,128)(2,1)S(1)}, bf16[14,32,256]{2,1,0:T(8,128)(2,1)}, u32[]{:S(2)}, u32[]{:S(2)}) %collective-permute-start.10) | collective-permute-done | bytes 229408 | tf_op jit(solution)/shard_map/ppermute | solution.py:397
  79.6 1.3 collective-permute-done.9.refs_3_
  80.9 14.7 %build_second.1.refs_0_ = bf16[7,224,2432]{2,1,0:T(8,128)(2,1)} custom-call(bf16[448,256]{1,0:T(8,128)(2,1)S(1)} %pad_maximum_fusion.mixed_ref, bf16[28,32,256]{2,1,0:T(8,128)(2,1)} %copy-done.15, bf16[28,32,256]{2,1,0:T(8,128)(2,1)} %copy-done.10, bf16[28,32,256]{2,1,0:T(8,128)(2,1)} %copy-done.11, bf16[14,32,256]{2,1,0:T(8,128)(2,1)} %collective-permute-done.9.refs_3_, ...), custom_call_target="tpu_custom_call" | custom-call | flops 8000000000 | bytes 22000000 | tf_op jit(solution)/shard_map/build_second/pallas_call | solution.py:137
  95.6 4.6 %forward.2 = f32[32,128]{1,0:T(8,128)S(1)} custom-call(s32[1]{0:T(128)} %bitcast.core_ref, bf16[7,224,2432]{2,1,0:T(8,128)(2,1)} %build_second.1.refs_0_, bf16[128,2432]{1,0:T(8,128)(2,1)S(1)} %copy-done.1, bf16[2432,128]{1,0:T(8,128)(2,1)S(1)} %copy-done.5, bf16[112,784]{1,0:T(8,128)(2,1)S(1)} %copy-done.2, ...), custom_call_target="tpu_custom_call" | custom-call | flops 50000000 | bytes 8000000 | tf_op jit(solution)/shard_map/forward/pallas_call | solution.py:249
  100.3 13.1 %all_to_all.31 = bf16[32,32,128]{2,1,0:T(8,128)(2,1)S(1)} all-to-all(bf16[32,32,128]{2,1,0:T(8,128)(2,1)S(1)} %broadcast_in_dim.14), channel_id=1, replica_groups=mesh['x'=4,'z'=8,'core'=2,'site'=4] {'x','z'}, dimensions={0} | all-to-all | bytes 524288 | tf_op jit(solution)/shard_map/all_to_all | solution.py:360
  113.5 5.3 %backward.2 = (f32[2,128]{1,0:T(2,128)S(1)}, f32[32,128]{1,0:T(8,128)S(1)}, f32[32,128]{1,0:T(8,128)S(1)}) custom-call(s32[1]{0:T(128)} %bitcast.core_ref, bf16[7,224,2432]{2,1,0:T(8,128)(2,1)} %build_second.1.refs_0_, bf16[128,2432]{1,0:T(8,128)(2,1)S(1)} %copy-done.3, bf16[2432,128]{1,0:T(8,128)(2,1)S(1)} %copy-done.4, bf16[112,784]{1,0:T(8,128)(2,1)S(1)} %copy-done.2, ...), custom_call_target="tpu_custom_call" | custom-call | flops 50000000 | bytes 8000000 | tf_op jit(solution)/shard_map/backward/pallas_call | solution.py:249
  118.8 4.8 %collective-permute-start.11 = (f32[32,128]{1,0:T(8,128)S(1)}, f32[32,128]{1,0:T(8,128)S(1)}, u32[]{:S(2)}, u32[]{:S(2)}) collective-permute-start(f32[32,128]{1,0:T(8,128)S(1)} %get-tuple-element.27), channel_id=1, source_target_pairs={{0,4},{4,0},{1,5},{5,1},{2,6},{6,2},{3,7},{7,3},{8,12},{12,8},{9,1... | collective-permute-start | bytes 49160 | tf_op jit(solution)/shard_map/ppermute | solution.py:364
  125.1 4.3 %all-to-all-start.3 = ((bf16[32,32,128]{2,1,0:T(8,128)(2,1)}), bf16[32,32,128]{2,1,0:T(8,128)(2,1)S(1)}, u32[]{:S(2)}, u32[]{:S(2)}) async-start(bf16[32,32,128]{2,1,0:T(8,128)(2,1)} %broadcast_in_dim.15), calls=%async_computation.3 | async-start | bytes 524288 | tf_op jit(solution)/shard_map/all_to_all | solution.py:360
  132.5 2.6 %collective-permute-start.14 = (f32[2,128]{1,0:T(2,128)S(1)}, f32[2,128]{1,0:T(2,128)S(1)}, u32[]{:S(2)}, u32[]{:S(2)}) collective-permute-start(f32[2,128]{1,0:T(2,128)S(1)} %add.136), channel_id=1, source_target_pairs={{0,2},{1,3},{2,0},{3,1},{4,6},{5,7},{6,4},{7,5},{8,10},{9,11},{10,... | collective-permute-start | bytes 3080 | tf_op jit(solution)/shard_map/ppermute | solution.py:368
  136.4 2.6 %collective-permute-done.15 = f32[2,128]{1,0:T(2,128)S(1)} collective-permute-done((f32[2,128]{1,0:T(2,128)S(1)}, f32[2,128]{1,0:T(2,128)S(1)}, u32[]{:S(2)}, u32[]{:S(2)}) %collective-permute-start.15) | collective-permute-done | bytes 1056 | tf_op jit(solution)/shard_map/ppermute | solution.py:368
  139.2 3.8 %collective-permute-start.16 = (f32[32,128]{1,0:T(8,128)S(1)}, f32[32,128]{1,0:T(8,128)S(1)}, u32[]{:S(2)}, u32[]{:S(2)}) collective-permute-start(f32[32,128]{1,0:T(8,128)S(1)} %convert_reduce_fusion.2.refs_4_.half_0_ref), channel_id=1, source_target_pairs={{0,4},{4,0},{1,5},{5,1},{2,6},{6,2},{3,7},{7,3},{8,12},{12,8},{9,1... | collective-permute-start | bytes 49160 | tf_op jit(solution)/shard_map/ppermute | solution.py:364
  143.8 4.5 %forward.3 = (f32[2,32,128]{2,1,0:T(8,128)S(1)}, f32[32,128]{1,0:T(8,128)S(1)}) custom-call(s32[1]{0:T(128)} %bitcast.core_ref, bf16[7,224,2432]{2,1,0:T(8,128)(2,1)} %build_second.1.refs_0_, bf16[128,2432]{1,0:T(8,128)(2,1)S(1)} %copy-done.1, bf16[2432,128]{1,0:T(8,128)(2,1)S(1)} %copy-done.5, bf16[112,784]{1,0:T(8,128)(2,1)S(1)} %copy-done.2, ...), custom_call_target="tpu_custom_call" | custom-call | flops 50000000 | bytes 8000000 | tf_op jit(solution)/shard_map/forward/pallas_call | solution.py:249
  148.4 17.0 %all_to_all.32 = bf16[32,32,128]{2,1,0:T(8,128)(2,1)S(1)} all-to-all(bf16[32,32,128]{2,1,0:T(8,128)(2,1)S(1)} %broadcast_in_dim.16), channel_id=1, replica_groups=mesh['x'=4,'z'=8,'core'=2,'site'=4] {'x','z'}, dimensions={0} | all-to-all | bytes 524288 | tf_op jit(solution)/shard_map/all_to_all | solution.py:360
  165.4 5.4 %backward.3 = (f32[3,128]{1,0:T(4,128)S(1)}, f32[32,128]{1,0:T(8,128)S(1)}, f32[32,128]{1,0:T(8,128)S(1)}) custom-call(s32[1]{0:T(128)} %bitcast.core_ref, bf16[7,224,2432]{2,1,0:T(8,128)(2,1)} %build_second.1.refs_0_, bf16[128,2432]{1,0:T(8,128)(2,1)S(1)} %copy-done.3, bf16[2432,128]{1,0:T(8,128)(2,1)S(1)} %copy-done.4, bf16[112,784]{1,0:T(8,128)(2,1)S(1)} %copy-done.2, ...), custom_call_target="tpu_custom_call" | custom-call | flops 50000000 | bytes 8000000 | tf_op jit(solution)/shard_map/backward/pallas_call | solution.py:249
  170.7 3.8 %collective-permute-start.17 = (f32[32,128]{1,0:T(8,128)S(1)}, f32[32,128]{1,0:T(8,128)S(1)}, u32[]{:S(2)}, u32[]{:S(2)}) collective-permute-start(f32[32,128]{1,0:T(8,128)S(1)} %get-tuple-element.34), channel_id=1, source_target_pairs={{0,4},{4,0},{1,5},{5,1},{2,6},{6,2},{3,7},{7,3},{8,12},{12,8},{9,1... | collective-permute-start | bytes 49160 | tf_op jit(solution)/shard_map/ppermute | solution.py:364
  176.1 4.2 %all-to-all-start.5 = ((bf16[32,32,128]{2,1,0:T(8,128)(2,1)}), bf16[32,32,128]{2,1,0:T(8,128)(2,1)S(1)}, u32[]{:S(2)}, u32[]{:S(2)}) async-start(bf16[32,32,128]{2,1,0:T(8,128)(2,1)} %broadcast_in_dim.17), calls=%async_computation.5 | async-start | bytes 524288 | tf_op jit(solution)/shard_map/all_to_all | solution.py:360
  182.9 2.7 %collective-permute-start.21 = (f32[3,128]{1,0:T(4,128)S(1)}, f32[3,128]{1,0:T(4,128)S(1)}, u32[]{:S(2)}, u32[]{:S(2)}) collective-permute-start(f32[3,128]{1,0:T(4,128)S(1)} %add.141), channel_id=1, source_target_pairs={{0,3},{1,2},{2,1},{3,0},{4,7},{5,6},{6,5},{7,4},{8,11},{9,10},{10,... | collective-permute-start | bytes 4616 | tf_op jit(solution)/shard_map/ppermute | solution.py:368
  186.9 3.0 %all-to-all-done.5 = bf16[32,32,128]{2,1,0:T(8,128)(2,1)S(1)} async-done(((bf16[32,32,128]{2,1,0:T(8,128)(2,1)}), bf16[32,32,128]{2,1,0:T(8,128)(2,1)S(1)}, u32[]{:S(2)}, u32[]{:S(2)}) %all-to-all-start.5) | async-done | bytes 262176 | tf_op jit(solution)/shard_map/all_to_all | solution.py:360
  190.0 3.8 %collective-permute-start.22 = (f32[32,128]{1,0:T(8,128)S(1)}, f32[32,128]{1,0:T(8,128)S(1)}, u32[]{:S(2)}, u32[]{:S(2)}) collective-permute-start(f32[32,128]{1,0:T(8,128)S(1)} %convert_reduce_fusion.half_1_ref), channel_id=1, source_target_pairs={{0,4},{4,0},{1,5},{5,1},{2,6},{6,2},{3,7},{7,3},{8,12},{12,8},{9,1... | collective-permute-start | bytes 49160 | tf_op jit(solution)/shard_map/ppermute | solution.py:364
  194.6 1.8 finish.1
  (111 shorter events, 24.7 us)
Async XLA Ops:
  2.8 4.2 %collective-permute-start = (bf16[7,4,4,256]{3,2,1,0:T(4,128)(2,1)S(1)}, bf16[7,4,4,256]{3,2,1,0:T(4,128)(2,1)S(1)}, u32[]{:S(2)}, u32[]{:S(2)}) collective-permute-start(bf16[7,4,4,256]{3,2,1,0:T(4,128)(2,1)S(1)} %dynamic-slice_bitcast_fusion), channel_id=1, source_target_pairs={{0,4},{4,0},{1,5},{5,1},{2,6},{6,2},{3,7},{7,3},{8,12},{12,8},{9,1... | collective-permute-start | bytes 172040 | tf_op jit(solution)/shard_map/ppermute | solution.py:364
  8.0 12.0 %all-to-all-start = ((bf16[4,448,128]{2,1,0:T(8,128)(2,1)}), bf16[4,448,128]{2,1,0:T(8,128)(2,1)S(1)}, u32[]{:S(2)}, u32[]{:S(2)}) async-start(bf16[4,448,128]{2,1,0:T(8,128)(2,1)} %broadcast_in_dim.13), calls=%async_computation | async-start | bytes 917504 | tf_op jit(solution)/shard_map/all_to_all | solution.py:360
  15.5 31.6 %copy-start.14 = (bf16[56,49,1]{1,0,2:T(8,128)(2,1)S(1)}, bf16[56,49,1]{1,0,2:T(8,128)(2,1)}, u32[]{:S(2)}) copy-start(bf16[56,49,1]{1,0,2:T(8,128)(2,1)} %constant.148) | copy-start | bytes 16468
  20.2 40.1 %copy-start.7 = (bf16[28,32,256]{2,1,0:T(8,128)(2,1)}, bf16[28,32,256]{2,1,0:T(8,128)(2,1)S(1)}, u32[]{:S(2)}) copy-start(bf16[28,32,256]{2,1,0:T(8,128)(2,1)S(1)} %copy_bitcast_fusion.refs_0_) | copy-start | bytes 1376260
  20.3 40.0 %collective-permute-start.8 = (bf16[4,2432,256]{2,1,0:T(8,128)(2,1)}, bf16[4,2432,256]{2,1,0:T(8,128)(2,1)}, u32[]{:S(2)}, u32[]{:S(2)}) collective-permute-start(bf16[4,2432,256]{2,1,0:T(8,128)(2,1)} %pad.13.refs_4_.refs_5_), channel_id=1, source_target_pairs={{0,4},{4,0},{1,5},{5,1},{2,6},{6,2},{3,7},{7,3},{8,12},{12,8},{9,1... | collective-permute-start | bytes 14942216 | tf_op jit(solution)/shard_map/ppermute | solution.py:364
  21.5 22.8 %collective-permute-start.4 = (bf16[28,32,256]{2,1,0:T(8,128)(2,1)S(1)}, bf16[28,32,256]{2,1,0:T(8,128)(2,1)S(1)}, u32[]{:S(2)}, u32[]{:S(2)}) collective-permute-start(bf16[28,32,256]{2,1,0:T(8,128)(2,1)S(1)} %copy_bitcast_fusion.refs_0_), channel_id=1, source_target_pairs={{0,8},{8,16},{16,24},{24,32},{32,40},{40,48},{48,56},{56,0},{1,9},... | collective-permute-start | bytes 1376264 | tf_op jit(solution)/shard_map/ppermute | solution.py:397
  22.0 23.3 %collective-permute-start.2 = (bf16[28,32,256]{2,1,0:T(8,128)(2,1)S(1)}, bf16[28,32,256]{2,1,0:T(8,128)(2,1)}, u32[]{:S(2)}, u32[]{:S(2)}) collective-permute-start(bf16[28,32,256]{2,1,0:T(8,128)(2,1)S(1)} %copy_bitcast_fusion.refs_0_), channel_id=1, source_target_pairs={{0,56},{8,0},{16,8},{24,16},{32,24},{40,32},{48,40},{56,48},{1,57}... | collective-permute-start | bytes 1376264 | tf_op jit(solution)/shard_map/ppermute | solution.py:397
  44.4 13.0 %collective-permute-start.5 = (bf16[28,32,256]{2,1,0:T(8,128)(2,1)S(1)}, bf16[28,32,256]{2,1,0:T(8,128)(2,1)S(1)}, u32[]{:S(2)}, u32[]{:S(2)}) collective-permute-start(bf16[28,32,256]{2,1,0:T(8,128)(2,1)S(1)} %collective-permute-done.4.refs_1_), channel_id=1, source_target_pairs={{0,8},{8,16},{16,24},{24,32},{32,40},{40,48},{48,56},{56,0},{1,9},... | collective-permute-start | bytes 1376264 | tf_op jit(solution)/shard_map/ppermute | solution.py:397
  45.4 12.0 %collective-permute-start.3 = (bf16[28,32,256]{2,1,0:T(8,128)(2,1)}, bf16[28,32,256]{2,1,0:T(8,128)(2,1)S(1)}, u32[]{:S(2)}, u32[]{:S(2)}) collective-permute-start(bf16[28,32,256]{2,1,0:T(8,128)(2,1)} %collective-permute-done.2.refs_2_), channel_id=1, source_target_pairs={{0,56},{8,0},{16,8},{24,16},{32,24},{40,32},{48,40},{56,48},{1,57}... | collective-permute-start | bytes 1376264 | tf_op jit(solution)/shard_map/ppermute | solution.py:397
  47.4 2.0 %collective-permute-start.1 = (bf16[224,256]{1,0:T(8,128)(2,1)S(1)}, bf16[224,256]{1,0:T(8,128)(2,1)S(1)}, u32[]{:S(2)}, u32[]{:S(2)}) collective-permute-start(bf16[224,256]{1,0:T(8,128)(2,1)S(1)} %bitcast.65), channel_id=1, source_target_pairs={{0,4},{4,0},{1,5},{5,1},{2,6},{6,2},{3,7},{7,3},{8,12},{12,8},{9,1... | collective-permute-start | bytes 344072 | tf_op jit(solution)/shard_map/ppermute | solution.py:364
  49.4 26.3 %copy-start.13 = (f32[1,2,2401]{2,1,0:T(2,128)S(1)}, f32[1,2,2401]{2,1,0:T(2,128)}, u32[]{:S(2)}) copy-start(f32[1,2,2401]{2,1,0:T(2,128)} %param.18) | copy-start | bytes 57628
  49.4 26.4 %copy-start.12 = (f32[2,32,49,1]{2,1,3,0:T(8,128)S(1)}, f32[2,32,49,1]{2,1,3,0:T(8,128)}, u32[]{:S(2)}) copy-start(f32[2,32,49,1]{2,1,3,0:T(8,128)} %constant.149) | copy-start | bytes 37636
  57.4 16.7 %collective-permute-start.6 = (bf16[28,32,256]{2,1,0:T(8,128)(2,1)S(1)}, bf16[28,32,256]{2,1,0:T(8,128)(2,1)S(1)}, u32[]{:S(2)}, u32[]{:S(2)}) collective-permute-start(bf16[28,32,256]{2,1,0:T(8,128)(2,1)S(1)} %collective-permute-done.5.refs_3_), channel_id=1, source_target_pairs={{0,8},{8,16},{16,24},{24,32},{32,40},{40,48},{48,56},{56,0},{1,9},... | collective-permute-start | bytes 1376264 | tf_op jit(solution)/shard_map/ppermute | solution.py:397
  57.4 16.6 %collective-permute-start.7 = (bf16[28,32,256]{2,1,0:T(8,128)(2,1)S(1)}, bf16[28,32,256]{2,1,0:T(8,128)(2,1)S(1)}, u32[]{:S(2)}, u32[]{:S(2)}) collective-permute-start(bf16[28,32,256]{2,1,0:T(8,128)(2,1)S(1)} %collective-permute-done.3.refs_0_), channel_id=1, source_target_pairs={{0,56},{8,0},{16,8},{24,16},{32,24},{40,32},{48,40},{56,48},{1,57}... | collective-permute-start | bytes 1376264 | tf_op jit(solution)/shard_map/ppermute | solution.py:397
  74.1 5.5 %collective-permute-start.10 = (bf16[14,32,256]{2,1,0:T(8,128)(2,1)S(1)}, bf16[14,32,256]{2,1,0:T(8,128)(2,1)}, u32[]{:S(2)}, u32[]{:S(2)}) collective-permute-start(bf16[14,32,256]{2,1,0:T(8,128)(2,1)S(1)} %slice.7), channel_id=1, source_target_pairs={{0,56},{8,0},{16,8},{24,16},{32,24},{40,32},{48,40},{56,48},{1,57}... | collective-permute-start | bytes 688136 | tf_op jit(solution)/shard_map/ppermute | solution.py:397
  74.2 6.7 %collective-permute-start.9 = (bf16[14,32,256]{2,1,0:T(8,128)(2,1)S(1)}, bf16[14,32,256]{2,1,0:T(8,128)(2,1)}, u32[]{:S(2)}, u32[]{:S(2)}) collective-permute-start(bf16[14,32,256]{2,1,0:T(8,128)(2,1)S(1)} %slice.6), channel_id=1, source_target_pairs={{0,8},{8,16},{16,24},{24,32},{32,40},{40,48},{48,56},{56,0},{1,9},... | collective-permute-start | bytes 688136 | tf_op jit(solution)/shard_map/ppermute | solution.py:397
  76.4 19.2 %copy-start.5 = (bf16[2432,128]{1,0:T(8,128)(2,1)S(1)}, bf16[2432,128]{1,0:T(8,128)(2,1)}, u32[]{:S(2)}) copy-start(bf16[2432,128]{1,0:T(8,128)(2,1)} %constant.121.refs_2_) | copy-start | bytes 1867780
  118.8 5.6 %collective-permute-start.11 = (f32[32,128]{1,0:T(8,128)S(1)}, f32[32,128]{1,0:T(8,128)S(1)}, u32[]{:S(2)}, u32[]{:S(2)}) collective-permute-start(f32[32,128]{1,0:T(8,128)S(1)} %get-tuple-element.27), channel_id=1, source_target_pairs={{0,4},{4,0},{1,5},{5,1},{2,6},{6,2},{3,7},{7,3},{8,12},{12,8},{9,1... | collective-permute-start | bytes 49160 | tf_op jit(solution)/shard_map/ppermute | solution.py:364
  125.1 14.0 %all-to-all-start.3 = ((bf16[32,32,128]{2,1,0:T(8,128)(2,1)}), bf16[32,32,128]{2,1,0:T(8,128)(2,1)S(1)}, u32[]{:S(2)}, u32[]{:S(2)}) async-start(bf16[32,32,128]{2,1,0:T(8,128)(2,1)} %broadcast_in_dim.15), calls=%async_computation.3 | async-start | bytes 524288 | tf_op jit(solution)/shard_map/all_to_all | solution.py:360
  129.4 1.8 collective-permute-start.12
  131.2 3.9 %collective-permute-start.13 = (f32[2,128]{1,0:T(2,128)S(1)}, f32[2,128]{1,0:T(2,128)S(1)}, u32[]{:S(2)}, u32[]{:S(2)}) collective-permute-start(f32[2,128]{1,0:T(2,128)S(1)} %add.136), channel_id=1, source_target_pairs={{0,1},{1,0},{2,3},{3,2},{4,5},{5,4},{6,7},{7,6},{8,9},{9,8},{10,11... | collective-permute-start | bytes 3080 | tf_op jit(solution)/shard_map/ppermute | solution.py:368
  132.5 3.9 %collective-permute-start.14 = (f32[2,128]{1,0:T(2,128)S(1)}, f32[2,128]{1,0:T(2,128)S(1)}, u32[]{:S(2)}, u32[]{:S(2)}) collective-permute-start(f32[2,128]{1,0:T(2,128)S(1)} %add.136), channel_id=1, source_target_pairs={{0,2},{1,3},{2,0},{3,1},{4,6},{5,7},{6,4},{7,5},{8,10},{9,11},{10,... | collective-permute-start | bytes 3080 | tf_op jit(solution)/shard_map/ppermute | solution.py:368
  135.1 3.9 %collective-permute-start.15 = (f32[2,128]{1,0:T(2,128)S(1)}, f32[2,128]{1,0:T(2,128)S(1)}, u32[]{:S(2)}, u32[]{:S(2)}) collective-permute-start(f32[2,128]{1,0:T(2,128)S(1)} %add.136), channel_id=1, source_target_pairs={{0,3},{1,2},{2,1},{3,0},{4,7},{5,6},{6,5},{7,4},{8,11},{9,10},{10,... | collective-permute-start | bytes 3080 | tf_op jit(solution)/shard_map/ppermute | solution.py:368
  139.2 4.6 %collective-permute-start.16 = (f32[32,128]{1,0:T(8,128)S(1)}, f32[32,128]{1,0:T(8,128)S(1)}, u32[]{:S(2)}, u32[]{:S(2)}) collective-permute-start(f32[32,128]{1,0:T(8,128)S(1)} %convert_reduce_fusion.2.refs_4_.half_0_ref), channel_id=1, source_target_pairs={{0,4},{4,0},{1,5},{5,1},{2,6},{6,2},{3,7},{7,3},{8,12},{12,8},{9,1... | collective-permute-start | bytes 49160 | tf_op jit(solution)/shard_map/ppermute | solution.py:364
  165.4 29.2 %copy-start.6 = (bf16[56,2432]{1,0:T(8,128)(2,1)S(1)}, bf16[56,2432]{1,0:T(8,128)(2,1)}, u32[]{:S(2)}) copy-start(bf16[56,2432]{1,0:T(8,128)(2,1)} %constant.107.clone.own_lane_ref) | copy-start | bytes 817156
  170.7 4.6 %collective-permute-start.17 = (f32[32,128]{1,0:T(8,128)S(1)}, f32[32,128]{1,0:T(8,128)S(1)}, u32[]{:S(2)}, u32[]{:S(2)}) collective-permute-start(f32[32,128]{1,0:T(8,128)S(1)} %get-tuple-element.34), channel_id=1, source_target_pairs={{0,4},{4,0},{1,5},{5,1},{2,6},{6,2},{3,7},{7,3},{8,12},{12,8},{9,1... | collective-permute-start | bytes 49160 | tf_op jit(solution)/shard_map/ppermute | solution.py:364
  176.1 13.8 %all-to-all-start.5 = ((bf16[32,32,128]{2,1,0:T(8,128)(2,1)}), bf16[32,32,128]{2,1,0:T(8,128)(2,1)S(1)}, u32[]{:S(2)}, u32[]{:S(2)}) async-start(bf16[32,32,128]{2,1,0:T(8,128)(2,1)} %broadcast_in_dim.17), calls=%async_computation.5 | async-start | bytes 524288 | tf_op jit(solution)/shard_map/all_to_all | solution.py:360
  180.3 1.5 collective-permute-start.18
  181.8 3.9 %collective-permute-start.19 = (f32[3,128]{1,0:T(4,128)S(1)}, f32[3,128]{1,0:T(4,128)S(1)}, u32[]{:S(2)}, u32[]{:S(2)}) collective-permute-start(f32[3,128]{1,0:T(4,128)S(1)} %add.141), channel_id=1, source_target_pairs={{0,1},{1,0},{2,3},{3,2},{4,5},{5,4},{6,7},{7,6},{8,9},{9,8},{10,11... | collective-permute-start | bytes 4616 | tf_op jit(solution)/shard_map/ppermute | solution.py:368
  181.8 4.1 %collective-permute-start.20 = (f32[3,128]{1,0:T(4,128)S(1)}, f32[3,128]{1,0:T(4,128)S(1)}, u32[]{:S(2)}, u32[]{:S(2)}) collective-permute-start(f32[3,128]{1,0:T(4,128)S(1)} %add.141), channel_id=1, source_target_pairs={{0,2},{1,3},{2,0},{3,1},{4,6},{5,7},{6,4},{7,5},{8,10},{9,11},{10,... | collective-permute-start | bytes 4616 | tf_op jit(solution)/shard_map/ppermute | solution.py:368
  182.9 4.0 %collective-permute-start.21 = (f32[3,128]{1,0:T(4,128)S(1)}, f32[3,128]{1,0:T(4,128)S(1)}, u32[]{:S(2)}, u32[]{:S(2)}) collective-permute-start(f32[3,128]{1,0:T(4,128)S(1)} %add.141), channel_id=1, source_target_pairs={{0,3},{1,2},{2,1},{3,0},{4,7},{5,6},{6,5},{7,4},{8,11},{9,10},{10,... | collective-permute-start | bytes 4616 | tf_op jit(solution)/shard_map/ppermute | solution.py:368
  190.0 4.6 %collective-permute-start.22 = (f32[32,128]{1,0:T(8,128)S(1)}, f32[32,128]{1,0:T(8,128)S(1)}, u32[]{:S(2)}, u32[]{:S(2)}) collective-permute-start(f32[32,128]{1,0:T(8,128)S(1)} %convert_reduce_fusion.half_1_ref), channel_id=1, source_target_pairs={{0,4},{4,0},{1,5},{5,1},{2,6},{6,2},{3,7},{7,3},{8,12},{12,8},{9,1... | collective-permute-start | bytes 49160 | tf_op jit(solution)/shard_map/ppermute | solution.py:364
  (12 other events, 126.5 us)

commit v5 on v3

--- a/solution.py
+++ b/solution.py
@@ -223,14 +223,12 @@
     @pl.when(step == D - 1)
     def _():
         if forward:
-            high, low = two_terms(sum_ref[...])
-            rows = dot(high, reduce_ref[...]) + dot(low, reduce_ref[...])
-            refs[-5][...] = pack_image(rows * scale_metric)
+            rows = dot(jnp.concatenate(two_terms(sum_ref[...]), axis=0), reduce_ref[...])
+            refs[-5][...] = pack_image((rows[:IMG] + rows[IMG:]) * scale_metric)
         else:
-            sums = [dot(sum_ref[r].astype(BF), reduce_ref[...]) for r in range(D)]
-            high, low = two_terms(jnp.concatenate(sums, axis=0))
-            rows = dot(fold_ref[...], high) + dot(fold_ref[...], low)
-            parts = pack(rows * scale_metric)
+            sums = dot(sum_ref[...].reshape(D * VEC, WIDE).astype(BF), reduce_ref[...])
+            rows = dot(fold_ref[...], jnp.concatenate(two_terms(sums), axis=1))
+            parts = pack((rows[:, :128] + rows[:, 128:]) * scale_metric)
             first = core_ref[0] == 0
             refs[-6][...] = jnp.where(first, parts[0], parts[1])
             refs[-5][...] = jnp.where(first, parts[1], parts[0])

time: 196 us -> 196 us (level)
  no operation moved by 1% of the time
where the time goes in v5:
time: 196 us; the launch traced here: 195 us
  starting transfers between devices  58.7 us (30%)
  Pallas kernels  49.9 us (25%)
  blocking collectives  46.9 us (24%)
  waiting for transfers between devices  25.1 us (13%)
  local copies, waits for them, and re-layouts  7.41 us (4%)
  matrix products  5.85 us (3%)
    all_to_all x2, blocking collectives, spread(): lax.all_to_all(jnp.broadcast_to(value[None], (count,) + value.shape), axe...  29.2 us
    pallas_call x2, Pallas kernels, build_metric(): pl.pallas_call(functools.partial(metric_kernel, len(blocks), before is no...  28.4 us
    ppermute x9, starting transfers between devices, swap(): return lax.ppermute(value, 'core', [(0, 1), (1, 0)])  26.5 us
    pallas_call x4, Pallas kernels, apply_metric(): pl.pallas_call(functools.partial(apply_kernel, forward, prologue, len(ins...  19.7 us
    all_to_all x1, blocking collectives, body(): lax.all_to_all(mixed, ('x', 'z', 'core'), 0, 0, tiled=True)  17.7 us
    ppermute x8, waiting for transfers between devices, ring(): return lax.ppermute(value, 'z', [(i, (i + step) % NZ) for i in range(NZ)])  12.4 us
    all_to_all x3, starting transfers between devices, spread(): lax.all_to_all(jnp.broadcast_to(value[None], (count,) + value.shape), axe...  11.9 us
    ppermute x8, starting transfers between devices, ring(): return lax.ppermute(value, 'z', [(i, (i + step) % NZ) for i in range(NZ)])  11.7 us
  transfers between devices with their start and end apart: 24, of which 16 were waited for; matrix products, arithmetic and copies ran while one was open for 4% of the time, Pallas kernels for 7%

profile of v5, /device:TPU:1, one launch (start us, length us, event | category | flops | bytes accessed | tf_op | source)
XLA Modules:
  0.0 195.5 jit_solution(10432110728501035733)
XLA Ops:
  2.8 3.3 %collective-permute-start = (bf16[7,4,4,256]{3,2,1,0:T(4,128)(2,1)S(1)}, bf16[7,4,4,256]{3,2,1,0:T(4,128)(2,1)S(1)}, u32[]{:S(2)}, u32[]{:S(2)}) collective-permute-start(bf16[7,4,4,256]{3,2,1,0:T(4,128)(2,1)S(1)} %dynamic-slice_bitcast_fusion), channel_id=1, source_target_pairs={{0,4},{4,0},{1,5},{5,1},{2,6},{6,2},{3,7},{7,3},{8,12},{12,8},{9,1... | collective-permute-start | bytes 172040 | tf_op jit(solution)/shard_map/ppermute | solution.py:362
  8.1 3.5 %all-to-all-start = ((bf16[4,448,128]{2,1,0:T(8,128)(2,1)}), bf16[4,448,128]{2,1,0:T(8,128)(2,1)S(1)}, u32[]{:S(2)}, u32[]{:S(2)}) async-start(bf16[4,448,128]{2,1,0:T(8,128)(2,1)} %broadcast_in_dim.13), calls=%async_computation | async-start | bytes 917504 | tf_op jit(solution)/shard_map/all_to_all | solution.py:358
  11.5 4.0 %fusion.1 = bf16[4,2401,256]{2,1,0:T(8,128)(2,1)S(1)} fusion(bf16[4,256,2401]{1,0,2:T(4,128)(2,1)} %bitcast.60, s32[256]{0:T(256)S(1)} %fusion.18), kind=kOutput, calls=%fused_computation.2 | convolution fusion | flops 1261339648 | bytes 9835520 | tf_op jit(solution)/shard_map/je,iek->ikj/dot_general | solution.py:417
  15.5 2.5 %pad.13.refs_4_.refs_5_ = bf16[4,2432,256]{2,1,0:T(8,128)(2,1)} pad(bf16[4,2401,256]{2,1,0:T(8,128)(2,1)S(1)} %fusion.1, bf16[]{:T(256)} %constant.88.clone.1), padding=0_0x0_31x0_0 | pad | bytes 9897986 | tf_op jit(solution)/shard_map/jit(_pad)/pad | solution.py:418
  18.4 1.6 all-to-all-done
  22.0 3.9 %collective-permute-start.2 = (bf16[28,32,256]{2,1,0:T(8,128)(2,1)S(1)}, bf16[28,32,256]{2,1,0:T(8,128)(2,1)}, u32[]{:S(2)}, u32[]{:S(2)}) collective-permute-start(bf16[28,32,256]{2,1,0:T(8,128)(2,1)S(1)} %copy_bitcast_fusion.refs_0_), channel_id=1, source_target_pairs={{0,56},{8,0},{16,8},{24,16},{32,24},{40,32},{48,40},{56,48},{1,57}... | collective-permute-start | bytes 1376264 | tf_op jit(solution)/shard_map/ppermute | solution.py:396
  26.4 17.7 %all_to_all.30 = bf16[64,2,392]{2,1,0:T(2,128)(2,1)S(1)} all-to-all(bf16[64,2,392]{2,1,0:T(2,128)(2,1)S(1)} %reshape.187), channel_id=1, replica_groups=mesh['x'=4,'z'=8,'core'=2,'site'=4] {'x','z','core'}, dimensions={0} | all-to-all | bytes 200704 | tf_op jit(solution)/shard_map/all_to_all | solution.py:429
  45.4 1.8 collective-permute-start.3
  49.5 7.9 %collective-permute-done.5.refs_3_ = bf16[28,32,256]{2,1,0:T(8,128)(2,1)S(1)} collective-permute-done((bf16[28,32,256]{2,1,0:T(8,128)(2,1)S(1)}, bf16[28,32,256]{2,1,0:T(8,128)(2,1)S(1)}, u32[]{:S(2)}, u32[]{:S(2)}) %collective-permute-start.5) | collective-permute-done | bytes 458784 | tf_op jit(solution)/shard_map/ppermute | solution.py:396
  57.4 2.9 %collective-permute-start.7 = (bf16[28,32,256]{2,1,0:T(8,128)(2,1)S(1)}, bf16[28,32,256]{2,1,0:T(8,128)(2,1)S(1)}, u32[]{:S(2)}, u32[]{:S(2)}) collective-permute-start(bf16[28,32,256]{2,1,0:T(8,128)(2,1)S(1)} %collective-permute-done.3.refs_0_), channel_id=1, source_target_pairs={{0,56},{8,0},{16,8},{24,16},{32,24},{40,32},{48,40},{56,48},{1,57}... | collective-permute-start | bytes 1376264 | tf_op jit(solution)/shard_map/ppermute | solution.py:396
  60.3 13.7 %build_first.1.refs_7_ = bf16[7,224,2432]{2,1,0:T(8,128)(2,1)} custom-call(bf16[448,256]{1,0:T(8,128)(2,1)S(1)} %pad_maximum_fusion.mixed_ref, bf16[28,32,256]{2,1,0:T(8,128)(2,1)} %copy-done.7, bf16[28,32,256]{2,1,0:T(8,128)(2,1)} %copy-done.16, bf16[28,32,256]{2,1,0:T(8,128)(2,1)} %collective-permute-done.2.refs_2_, bf16[28,32,256]{2,1,0:T(8,128)(2,1)} %copy-done.17, ...), custom_call_target="tpu_custom_call" | custom-call | flops 8000000000 | bytes 22000000 | tf_op jit(solution)/shard_map/build_first/pallas_call | solution.py:137
  74.2 1.5 collective-permute-start.9
  76.3 3.2 %collective-permute-done.10.refs_4_ = bf16[14,32,256]{2,1,0:T(8,128)(2,1)} collective-permute-done((bf16[14,32,256]{2,1,0:T(8,128)(2,1)S(1)}, bf16[14,32,256]{2,1,0:T(8,128)(2,1)}, u32[]{:S(2)}, u32[]{:S(2)}) %collective-permute-start.10) | collective-permute-done | bytes 229408 | tf_op jit(solution)/shard_map/ppermute | solution.py:396
  80.9 14.7 %build_second.1.refs_0_ = bf16[7,224,2432]{2,1,0:T(8,128)(2,1)} custom-call(bf16[448,256]{1,0:T(8,128)(2,1)S(1)} %pad_maximum_fusion.mixed_ref, bf16[28,32,256]{2,1,0:T(8,128)(2,1)} %copy-done.15, bf16[28,32,256]{2,1,0:T(8,128)(2,1)} %copy-done.10, bf16[28,32,256]{2,1,0:T(8,128)(2,1)} %copy-done.11, bf16[14,32,256]{2,1,0:T(8,128)(2,1)} %collective-permute-done.9.refs_3_, ...), custom_call_target="tpu_custom_call" | custom-call | flops 8000000000 | bytes 22000000 | tf_op jit(solution)/shard_map/build_second/pallas_call | solution.py:137
  95.6 4.6 %forward.2 = f32[32,128]{1,0:T(8,128)S(1)} custom-call(s32[1]{0:T(128)} %bitcast.core_ref, bf16[7,224,2432]{2,1,0:T(8,128)(2,1)} %build_second.1.refs_0_, bf16[128,2432]{1,0:T(8,128)(2,1)S(1)} %copy-done.1, bf16[2432,128]{1,0:T(8,128)(2,1)S(1)} %copy-done.5, bf16[112,784]{1,0:T(8,128)(2,1)S(1)} %copy-done.2, ...), custom_call_target="tpu_custom_call" | custom-call | flops 50000000 | bytes 8000000 | tf_op jit(solution)/shard_map/forward/pallas_call | solution.py:247
  100.3 13.1 %all_to_all.31 = bf16[32,32,128]{2,1,0:T(8,128)(2,1)S(1)} all-to-all(bf16[32,32,128]{2,1,0:T(8,128)(2,1)S(1)} %broadcast_in_dim.14), channel_id=1, replica_groups=mesh['x'=4,'z'=8,'core'=2,'site'=4] {'x','z'}, dimensions={0} | all-to-all | bytes 524288 | tf_op jit(solution)/shard_map/all_to_all | solution.py:358
  113.4 5.3 %backward.2 = (f32[2,128]{1,0:T(2,128)S(1)}, f32[32,128]{1,0:T(8,128)S(1)}, f32[32,128]{1,0:T(8,128)S(1)}) custom-call(s32[1]{0:T(128)} %bitcast.core_ref, bf16[7,224,2432]{2,1,0:T(8,128)(2,1)} %build_second.1.refs_0_, bf16[128,2432]{1,0:T(8,128)(2,1)S(1)} %copy-done.3, bf16[2432,128]{1,0:T(8,128)(2,1)S(1)} %copy-done.4, bf16[112,784]{1,0:T(8,128)(2,1)S(1)} %copy-done.2, ...), custom_call_target="tpu_custom_call" | custom-call | flops 50000000 | bytes 8000000 | tf_op jit(solution)/shard_map/backward/pallas_call | solution.py:247
  118.7 4.8 %collective-permute-start.11 = (f32[32,128]{1,0:T(8,128)S(1)}, f32[32,128]{1,0:T(8,128)S(1)}, u32[]{:S(2)}, u32[]{:S(2)}) collective-permute-start(f32[32,128]{1,0:T(8,128)S(1)} %get-tuple-element.27), channel_id=1, source_target_pairs={{0,4},{4,0},{1,5},{5,1},{2,6},{6,2},{3,7},{7,3},{8,12},{12,8},{9,1... | collective-permute-start | bytes 49160 | tf_op jit(solution)/shard_map/ppermute | solution.py:362
  125.1 4.3 %all-to-all-start.3 = ((bf16[32,32,128]{2,1,0:T(8,128)(2,1)}), bf16[32,32,128]{2,1,0:T(8,128)(2,1)S(1)}, u32[]{:S(2)}, u32[]{:S(2)}) async-start(bf16[32,32,128]{2,1,0:T(8,128)(2,1)} %broadcast_in_dim.15), calls=%async_computation.3 | async-start | bytes 524288 | tf_op jit(solution)/shard_map/all_to_all | solution.py:358
  129.4 1.4 collective-permute-start.12
  131.9 2.9 %collective-permute-start.13 = (f32[2,128]{1,0:T(2,128)S(1)}, f32[2,128]{1,0:T(2,128)S(1)}, u32[]{:S(2)}, u32[]{:S(2)}) collective-permute-start(f32[2,128]{1,0:T(2,128)S(1)} %add.130), channel_id=1, source_target_pairs={{0,2},{1,3},{2,0},{3,1},{4,6},{5,7},{6,4},{7,5},{8,10},{9,11},{10,... | collective-permute-start | bytes 3080 | tf_op jit(solution)/shard_map/ppermute | solution.py:367
  135.8 2.9 %collective-permute-start.14 = (f32[2,128]{1,0:T(2,128)S(1)}, f32[2,128]{1,0:T(2,128)S(1)}, u32[]{:S(2)}, u32[]{:S(2)}) collective-permute-start(f32[2,128]{1,0:T(2,128)S(1)} %add.131), channel_id=1, source_target_pairs={{0,4},{4,0},{1,5},{5,1},{2,6},{6,2},{3,7},{7,3},{8,12},{12,8},{9,1... | collective-permute-start | bytes 3080 | tf_op jit(solution)/shard_map/ppermute | solution.py:362
  139.6 3.3 %collective-permute-start.15 = (f32[32,128]{1,0:T(8,128)S(1)}, f32[32,128]{1,0:T(8,128)S(1)}, u32[]{:S(2)}, u32[]{:S(2)}) collective-permute-start(f32[32,128]{1,0:T(8,128)S(1)} %convert_reduce_fusion.2.refs_4_.half_0_ref), channel_id=1, source_target_pairs={{0,4},{4,0},{1,5},{5,1},{2,6},{6,2},{3,7},{7,3},{8,12},{12,8},{9,1... | collective-permute-start | bytes 49160 | tf_op jit(solution)/shard_map/ppermute | solution.py:362
  143.7 4.5 %forward.3 = (f32[2,32,128]{2,1,0:T(8,128)S(1)}, f32[32,128]{1,0:T(8,128)S(1)}) custom-call(s32[1]{0:T(128)} %bitcast.core_ref, bf16[7,224,2432]{2,1,0:T(8,128)(2,1)} %build_second.1.refs_0_, bf16[128,2432]{1,0:T(8,128)(2,1)S(1)} %copy-done.1, bf16[2432,128]{1,0:T(8,128)(2,1)S(1)} %copy-done.5, bf16[112,784]{1,0:T(8,128)(2,1)S(1)} %copy-done.2, ...), custom_call_target="tpu_custom_call" | custom-call | flops 50000000 | bytes 8000000 | tf_op jit(solution)/shard_map/forward/pallas_call | solution.py:247
  148.3 16.1 %all_to_all.32 = bf16[32,32,128]{2,1,0:T(8,128)(2,1)S(1)} all-to-all(bf16[32,32,128]{2,1,0:T(8,128)(2,1)S(1)} %broadcast_in_dim.16), channel_id=1, replica_groups=mesh['x'=4,'z'=8,'core'=2,'site'=4] {'x','z'}, dimensions={0} | all-to-all | bytes 524288 | tf_op jit(solution)/shard_map/all_to_all | solution.py:358
  164.5 5.3 %backward.3 = (f32[3,128]{1,0:T(4,128)S(1)}, f32[32,128]{1,0:T(8,128)S(1)}, f32[32,128]{1,0:T(8,128)S(1)}) custom-call(s32[1]{0:T(128)} %bitcast.core_ref, bf16[7,224,2432]{2,1,0:T(8,128)(2,1)} %build_second.1.refs_0_, bf16[128,2432]{1,0:T(8,128)(2,1)S(1)} %copy-done.3, bf16[2432,128]{1,0:T(8,128)(2,1)S(1)} %copy-done.4, bf16[112,784]{1,0:T(8,128)(2,1)S(1)} %copy-done.2, ...), custom_call_target="tpu_custom_call" | custom-call | flops 50000000 | bytes 8000000 | tf_op jit(solution)/shard_map/backward/pallas_call | solution.py:247
  169.8 3.8 %collective-permute-start.16 = (f32[32,128]{1,0:T(8,128)S(1)}, f32[32,128]{1,0:T(8,128)S(1)}, u32[]{:S(2)}, u32[]{:S(2)}) collective-permute-start(f32[32,128]{1,0:T(8,128)S(1)} %get-tuple-element.34), channel_id=1, source_target_pairs={{0,4},{4,0},{1,5},{5,1},{2,6},{6,2},{3,7},{7,3},{8,12},{12,8},{9,1... | collective-permute-start | bytes 49160 | tf_op jit(solution)/shard_map/ppermute | solution.py:362
  175.1 4.2 %all-to-all-start.5 = ((bf16[32,32,128]{2,1,0:T(8,128)(2,1)}), bf16[32,32,128]{2,1,0:T(8,128)(2,1)S(1)}, u32[]{:S(2)}, u32[]{:S(2)}) async-start(bf16[32,32,128]{2,1,0:T(8,128)(2,1)} %broadcast_in_dim.17), calls=%async_computation.5 | async-start | bytes 524288 | tf_op jit(solution)/shard_map/all_to_all | solution.py:358
  181.8 2.9 %collective-permute-start.18 = (f32[3,128]{1,0:T(4,128)S(1)}, f32[3,128]{1,0:T(4,128)S(1)}, u32[]{:S(2)}, u32[]{:S(2)}) collective-permute-start(f32[3,128]{1,0:T(4,128)S(1)} %add.134), channel_id=1, source_target_pairs={{0,2},{1,3},{2,0},{3,1},{4,6},{5,7},{6,4},{7,5},{8,10},{9,11},{10,... | collective-permute-start | bytes 4616 | tf_op jit(solution)/shard_map/ppermute | solution.py:367
  185.8 2.9 %collective-permute-start.19 = (f32[3,128]{1,0:T(4,128)S(1)}, f32[3,128]{1,0:T(4,128)S(1)}, u32[]{:S(2)}, u32[]{:S(2)}) collective-permute-start(f32[3,128]{1,0:T(4,128)S(1)} %add.135), channel_id=1, source_target_pairs={{0,4},{4,0},{1,5},{5,1},{2,6},{6,2},{3,7},{7,3},{8,12},{12,8},{9,1... | collective-permute-start | bytes 4616 | tf_op jit(solution)/shard_map/ppermute | solution.py:362
  189.6 3.2 %collective-permute-start.20 = (f32[32,128]{1,0:T(8,128)S(1)}, f32[32,128]{1,0:T(8,128)S(1)}, u32[]{:S(2)}, u32[]{:S(2)}) collective-permute-start(f32[32,128]{1,0:T(8,128)S(1)} %convert_reduce_fusion.half_1_ref), channel_id=1, source_target_pairs={{0,4},{4,0},{1,5},{5,1},{2,6},{6,2},{3,7},{7,3},{8,12},{12,8},{9,1... | collective-permute-start | bytes 49160 | tf_op jit(solution)/shard_map/ppermute | solution.py:362
  193.7 1.8 finish.1
  (109 shorter events, 25.0 us)
Async XLA Ops:
  2.8 4.2 %collective-permute-start = (bf16[7,4,4,256]{3,2,1,0:T(4,128)(2,1)S(1)}, bf16[7,4,4,256]{3,2,1,0:T(4,128)(2,1)S(1)}, u32[]{:S(2)}, u32[]{:S(2)}) collective-permute-start(bf16[7,4,4,256]{3,2,1,0:T(4,128)(2,1)S(1)} %dynamic-slice_bitcast_fusion), channel_id=1, source_target_pairs={{0,4},{4,0},{1,5},{5,1},{2,6},{6,2},{3,7},{7,3},{8,12},{12,8},{9,1... | collective-permute-start | bytes 172040 | tf_op jit(solution)/shard_map/ppermute | solution.py:362
  8.1 12.0 %all-to-all-start = ((bf16[4,448,128]{2,1,0:T(8,128)(2,1)}), bf16[4,448,128]{2,1,0:T(8,128)(2,1)S(1)}, u32[]{:S(2)}, u32[]{:S(2)}) async-start(bf16[4,448,128]{2,1,0:T(8,128)(2,1)} %broadcast_in_dim.13), calls=%async_computation | async-start | bytes 917504 | tf_op jit(solution)/shard_map/all_to_all | solution.py:358
  15.5 31.6 %copy-start.14 = (bf16[56,49,1]{1,0,2:T(8,128)(2,1)S(1)}, bf16[56,49,1]{1,0,2:T(8,128)(2,1)}, u32[]{:S(2)}) copy-start(bf16[56,49,1]{1,0,2:T(8,128)(2,1)} %constant.148) | copy-start | bytes 16468
  20.3 40.1 %copy-start.7 = (bf16[28,32,256]{2,1,0:T(8,128)(2,1)}, bf16[28,32,256]{2,1,0:T(8,128)(2,1)S(1)}, u32[]{:S(2)}) copy-start(bf16[28,32,256]{2,1,0:T(8,128)(2,1)S(1)} %copy_bitcast_fusion.refs_0_) | copy-start | bytes 1376260
  20.3 40.1 %collective-permute-start.8 = (bf16[4,2432,256]{2,1,0:T(8,128)(2,1)}, bf16[4,2432,256]{2,1,0:T(8,128)(2,1)}, u32[]{:S(2)}, u32[]{:S(2)}) collective-permute-start(bf16[4,2432,256]{2,1,0:T(8,128)(2,1)} %pad.13.refs_4_.refs_5_), channel_id=1, source_target_pairs={{0,4},{4,0},{1,5},{5,1},{2,6},{6,2},{3,7},{7,3},{8,12},{12,8},{9,1... | collective-permute-start | bytes 14942216 | tf_op jit(solution)/shard_map/ppermute | solution.py:362
  21.5 22.8 %collective-permute-start.4 = (bf16[28,32,256]{2,1,0:T(8,128)(2,1)S(1)}, bf16[28,32,256]{2,1,0:T(8,128)(2,1)S(1)}, u32[]{:S(2)}, u32[]{:S(2)}) collective-permute-start(bf16[28,32,256]{2,1,0:T(8,128)(2,1)S(1)} %copy_bitcast_fusion.refs_0_), channel_id=1, source_target_pairs={{0,8},{8,16},{16,24},{24,32},{32,40},{40,48},{48,56},{56,0},{1,9},... | collective-permute-start | bytes 1376264 | tf_op jit(solution)/shard_map/ppermute | solution.py:396
  22.0 23.4 %collective-permute-start.2 = (bf16[28,32,256]{2,1,0:T(8,128)(2,1)S(1)}, bf16[28,32,256]{2,1,0:T(8,128)(2,1)}, u32[]{:S(2)}, u32[]{:S(2)}) collective-permute-start(bf16[28,32,256]{2,1,0:T(8,128)(2,1)S(1)} %copy_bitcast_fusion.refs_0_), channel_id=1, source_target_pairs={{0,56},{8,0},{16,8},{24,16},{32,24},{40,32},{48,40},{56,48},{1,57}... | collective-permute-start | bytes 1376264 | tf_op jit(solution)/shard_map/ppermute | solution.py:396
  44.4 13.0 %collective-permute-start.5 = (bf16[28,32,256]{2,1,0:T(8,128)(2,1)S(1)}, bf16[28,32,256]{2,1,0:T(8,128)(2,1)S(1)}, u32[]{:S(2)}, u32[]{:S(2)}) collective-permute-start(bf16[28,32,256]{2,1,0:T(8,128)(2,1)S(1)} %collective-permute-done.4.refs_1_), channel_id=1, source_target_pairs={{0,8},{8,16},{16,24},{24,32},{32,40},{40,48},{48,56},{56,0},{1,9},... | collective-permute-start | bytes 1376264 | tf_op jit(solution)/shard_map/ppermute | solution.py:396
  45.4 12.0 %collective-permute-start.3 = (bf16[28,32,256]{2,1,0:T(8,128)(2,1)}, bf16[28,32,256]{2,1,0:T(8,128)(2,1)S(1)}, u32[]{:S(2)}, u32[]{:S(2)}) collective-permute-start(bf16[28,32,256]{2,1,0:T(8,128)(2,1)} %collective-permute-done.2.refs_2_), channel_id=1, source_target_pairs={{0,56},{8,0},{16,8},{24,16},{32,24},{40,32},{48,40},{56,48},{1,57}... | collective-permute-start | bytes 1376264 | tf_op jit(solution)/shard_map/ppermute | solution.py:396
  47.4 2.0 %collective-permute-start.1 = (bf16[224,256]{1,0:T(8,128)(2,1)S(1)}, bf16[224,256]{1,0:T(8,128)(2,1)S(1)}, u32[]{:S(2)}, u32[]{:S(2)}) collective-permute-start(bf16[224,256]{1,0:T(8,128)(2,1)S(1)} %bitcast.65), channel_id=1, source_target_pairs={{0,4},{4,0},{1,5},{5,1},{2,6},{6,2},{3,7},{7,3},{8,12},{12,8},{9,1... | collective-permute-start | bytes 344072 | tf_op jit(solution)/shard_map/ppermute | solution.py:362
  49.4 26.2 %copy-start.13 = (f32[1,2,2401]{2,1,0:T(2,128)S(1)}, f32[1,2,2401]{2,1,0:T(2,128)}, u32[]{:S(2)}) copy-start(f32[1,2,2401]{2,1,0:T(2,128)} %param.18) | copy-start | bytes 57628
  49.5 26.4 %copy-start.12 = (f32[2,32,49,1]{2,1,3,0:T(8,128)S(1)}, f32[2,32,49,1]{2,1,3,0:T(8,128)}, u32[]{:S(2)}) copy-start(f32[2,32,49,1]{2,1,3,0:T(8,128)} %constant.149) | copy-start | bytes 37636
  57.4 16.6 %collective-permute-start.6 = (bf16[28,32,256]{2,1,0:T(8,128)(2,1)S(1)}, bf16[28,32,256]{2,1,0:T(8,128)(2,1)S(1)}, u32[]{:S(2)}, u32[]{:S(2)}) collective-permute-start(bf16[28,32,256]{2,1,0:T(8,128)(2,1)S(1)} %collective-permute-done.5.refs_3_), channel_id=1, source_target_pairs={{0,8},{8,16},{16,24},{24,32},{32,40},{40,48},{48,56},{56,0},{1,9},... | collective-permute-start | bytes 1376264 | tf_op jit(solution)/shard_map/ppermute | solution.py:396
  57.4 16.6 %collective-permute-start.7 = (bf16[28,32,256]{2,1,0:T(8,128)(2,1)S(1)}, bf16[28,32,256]{2,1,0:T(8,128)(2,1)S(1)}, u32[]{:S(2)}, u32[]{:S(2)}) collective-permute-start(bf16[28,32,256]{2,1,0:T(8,128)(2,1)S(1)} %collective-permute-done.3.refs_0_), channel_id=1, source_target_pairs={{0,56},{8,0},{16,8},{24,16},{32,24},{40,32},{48,40},{56,48},{1,57}... | collective-permute-start | bytes 1376264 | tf_op jit(solution)/shard_map/ppermute | solution.py:396
  74.0 5.5 %collective-permute-start.10 = (bf16[14,32,256]{2,1,0:T(8,128)(2,1)S(1)}, bf16[14,32,256]{2,1,0:T(8,128)(2,1)}, u32[]{:S(2)}, u32[]{:S(2)}) collective-permute-start(bf16[14,32,256]{2,1,0:T(8,128)(2,1)S(1)} %slice.7), channel_id=1, source_target_pairs={{0,56},{8,0},{16,8},{24,16},{32,24},{40,32},{48,40},{56,48},{1,57}... | collective-permute-start | bytes 688136 | tf_op jit(solution)/shard_map/ppermute | solution.py:396
  74.2 6.7 %collective-permute-start.9 = (bf16[14,32,256]{2,1,0:T(8,128)(2,1)S(1)}, bf16[14,32,256]{2,1,0:T(8,128)(2,1)}, u32[]{:S(2)}, u32[]{:S(2)}) collective-permute-start(bf16[14,32,256]{2,1,0:T(8,128)(2,1)S(1)} %slice.6), channel_id=1, source_target_pairs={{0,8},{8,16},{16,24},{24,32},{32,40},{40,48},{48,56},{56,0},{1,9},... | collective-permute-start | bytes 688136 | tf_op jit(solution)/shard_map/ppermute | solution.py:396
  76.3 19.3 %copy-start.1 = (bf16[128,2432]{1,0:T(8,128)(2,1)S(1)}, bf16[128,2432]{1,0:T(8,128)(2,1)}, u32[]{:S(2)}) copy-start(bf16[128,2432]{1,0:T(8,128)(2,1)} %constant.104.clone.refs_1_.expand_ref) | copy-start | bytes 1867780
  76.3 19.3 %copy-start.2 = (bf16[112,784]{1,0:T(8,128)(2,1)S(1)}, bf16[112,784]{1,0:T(8,128)(2,1)}, u32[]{:S(2)}) copy-start(bf16[112,784]{1,0:T(8,128)(2,1)} %constant.106.clone.refs_3_) | copy-start | bytes 526852
  76.3 19.3 %copy-start.5 = (bf16[2432,128]{1,0:T(8,128)(2,1)S(1)}, bf16[2432,128]{1,0:T(8,128)(2,1)}, u32[]{:S(2)}) copy-start(bf16[2432,128]{1,0:T(8,128)(2,1)} %constant.121.refs_2_) | copy-start | bytes 1867780
  118.7 5.6 %collective-permute-start.11 = (f32[32,128]{1,0:T(8,128)S(1)}, f32[32,128]{1,0:T(8,128)S(1)}, u32[]{:S(2)}, u32[]{:S(2)}) collective-permute-start(f32[32,128]{1,0:T(8,128)S(1)} %get-tuple-element.27), channel_id=1, source_target_pairs={{0,4},{4,0},{1,5},{5,1},{2,6},{6,2},{3,7},{7,3},{8,12},{12,8},{9,1... | collective-permute-start | bytes 49160 | tf_op jit(solution)/shard_map/ppermute | solution.py:362
  125.1 14.5 %all-to-all-start.3 = ((bf16[32,32,128]{2,1,0:T(8,128)(2,1)}), bf16[32,32,128]{2,1,0:T(8,128)(2,1)S(1)}, u32[]{:S(2)}, u32[]{:S(2)}) async-start(bf16[32,32,128]{2,1,0:T(8,128)(2,1)} %broadcast_in_dim.15), calls=%async_computation.3 | async-start | bytes 524288 | tf_op jit(solution)/shard_map/all_to_all | solution.py:358
  129.4 2.5 %collective-permute-start.12 = (f32[2,128]{1,0:T(2,128)S(1)}, f32[2,128]{1,0:T(2,128)S(1)}, u32[]{:S(2)}, u32[]{:S(2)}) collective-permute-start(f32[2,128]{1,0:T(2,128)S(1)} %get-tuple-element.28), channel_id=1, source_target_pairs={{0,1},{1,0},{2,3},{3,2},{4,5},{5,4},{6,7},{7,6},{8,9},{9,8},{10,11... | collective-permute-start | bytes 3080 | tf_op jit(solution)/shard_map/ppermute | solution.py:367
  131.9 3.9 %collective-permute-start.13 = (f32[2,128]{1,0:T(2,128)S(1)}, f32[2,128]{1,0:T(2,128)S(1)}, u32[]{:S(2)}, u32[]{:S(2)}) collective-permute-start(f32[2,128]{1,0:T(2,128)S(1)} %add.130), channel_id=1, source_target_pairs={{0,2},{1,3},{2,0},{3,1},{4,6},{5,7},{6,4},{7,5},{8,10},{9,11},{10,... | collective-permute-start | bytes 3080 | tf_op jit(solution)/shard_map/ppermute | solution.py:367
  135.8 3.7 %collective-permute-start.14 = (f32[2,128]{1,0:T(2,128)S(1)}, f32[2,128]{1,0:T(2,128)S(1)}, u32[]{:S(2)}, u32[]{:S(2)}) collective-permute-start(f32[2,128]{1,0:T(2,128)S(1)} %add.131), channel_id=1, source_target_pairs={{0,4},{4,0},{1,5},{5,1},{2,6},{6,2},{3,7},{7,3},{8,12},{12,8},{9,1... | collective-permute-start | bytes 3080 | tf_op jit(solution)/shard_map/ppermute | solution.py:362
  139.6 4.1 %collective-permute-start.15 = (f32[32,128]{1,0:T(8,128)S(1)}, f32[32,128]{1,0:T(8,128)S(1)}, u32[]{:S(2)}, u32[]{:S(2)}) collective-permute-start(f32[32,128]{1,0:T(8,128)S(1)} %convert_reduce_fusion.2.refs_4_.half_0_ref), channel_id=1, source_target_pairs={{0,4},{4,0},{1,5},{5,1},{2,6},{6,2},{3,7},{7,3},{8,12},{12,8},{9,1... | collective-permute-start | bytes 49160 | tf_op jit(solution)/shard_map/ppermute | solution.py:362
  164.5 29.2 %copy-start.6 = (bf16[56,2432]{1,0:T(8,128)(2,1)S(1)}, bf16[56,2432]{1,0:T(8,128)(2,1)}, u32[]{:S(2)}) copy-start(bf16[56,2432]{1,0:T(8,128)(2,1)} %constant.107.clone.own_lane_ref) | copy-start | bytes 817156
  169.8 4.6 %collective-permute-start.16 = (f32[32,128]{1,0:T(8,128)S(1)}, f32[32,128]{1,0:T(8,128)S(1)}, u32[]{:S(2)}, u32[]{:S(2)}) collective-permute-start(f32[32,128]{1,0:T(8,128)S(1)} %get-tuple-element.34), channel_id=1, source_target_pairs={{0,4},{4,0},{1,5},{5,1},{2,6},{6,2},{3,7},{7,3},{8,12},{12,8},{9,1... | collective-permute-start | bytes 49160 | tf_op jit(solution)/shard_map/ppermute | solution.py:362
  175.1 14.4 %all-to-all-start.5 = ((bf16[32,32,128]{2,1,0:T(8,128)(2,1)}), bf16[32,32,128]{2,1,0:T(8,128)(2,1)S(1)}, u32[]{:S(2)}, u32[]{:S(2)}) async-start(bf16[32,32,128]{2,1,0:T(8,128)(2,1)} %broadcast_in_dim.17), calls=%async_computation.5 | async-start | bytes 524288 | tf_op jit(solution)/shard_map/all_to_all | solution.py:358
  179.3 2.5 %collective-permute-start.17 = (f32[3,128]{1,0:T(4,128)S(1)}, f32[3,128]{1,0:T(4,128)S(1)}, u32[]{:S(2)}, u32[]{:S(2)}) collective-permute-start(f32[3,128]{1,0:T(4,128)S(1)} %get-tuple-element.35), channel_id=1, source_target_pairs={{0,1},{1,0},{2,3},{3,2},{4,5},{5,4},{6,7},{7,6},{8,9},{9,8},{10,11... | collective-permute-start | bytes 4616 | tf_op jit(solution)/shard_map/ppermute | solution.py:367
  181.8 3.9 %collective-permute-start.18 = (f32[3,128]{1,0:T(4,128)S(1)}, f32[3,128]{1,0:T(4,128)S(1)}, u32[]{:S(2)}, u32[]{:S(2)}) collective-permute-start(f32[3,128]{1,0:T(4,128)S(1)} %add.134), channel_id=1, source_target_pairs={{0,2},{1,3},{2,0},{3,1},{4,6},{5,7},{6,4},{7,5},{8,10},{9,11},{10,... | collective-permute-start | bytes 4616 | tf_op jit(solution)/shard_map/ppermute | solution.py:367
  185.8 3.7 %collective-permute-start.19 = (f32[3,128]{1,0:T(4,128)S(1)}, f32[3,128]{1,0:T(4,128)S(1)}, u32[]{:S(2)}, u32[]{:S(2)}) collective-permute-start(f32[3,128]{1,0:T(4,128)S(1)} %add.135), channel_id=1, source_target_pairs={{0,4},{4,0},{1,5},{5,1},{2,6},{6,2},{3,7},{7,3},{8,12},{12,8},{9,1... | collective-permute-start | bytes 4616 | tf_op jit(solution)/shard_map/ppermute | solution.py:362
  189.6 4.1 %collective-permute-start.20 = (f32[32,128]{1,0:T(8,128)S(1)}, f32[32,128]{1,0:T(8,128)S(1)}, u32[]{:S(2)}, u32[]{:S(2)}) collective-permute-start(f32[32,128]{1,0:T(8,128)S(1)} %convert_reduce_fusion.half_1_ref), channel_id=1, source_target_pairs={{0,4},{4,0},{1,5},{5,1},{2,6},{6,2},{3,7},{7,3},{8,12},{12,8},{9,1... | collective-permute-start | bytes 49160 | tf_op jit(solution)/shard_map/ppermute | solution.py:362
  (10 other events, 87.9 us)
